TPU v7x, 256 devices: a whole 4x4x8 slice. The times are simulated.
256 devices in a mesh: rep: 32 (over z_lo, x, core), fsdp: 8 (over z_hi, y).
Axes of the slice: x: 4, y: 4, z: 8 (z_hi: 2, z_lo: 4; z = z_hi * 4 + z_lo), core: 2. Of those that a mesh axis runs over, the one named last changes fastest.
Arguments:
- activations: bfloat16 [32768, 3072], P(('rep', 'fsdp')), may hold values from -6 to 6
- targets: bfloat16 [32768, 6144], P('rep', 'fsdp'), may hold values from -16 to 16
- replica_weight: bfloat16 [32, 3072, 6144], P('rep', None, 'fsdp'), may hold values from -6 to 6
- row_state: float32 [32, 3072], P('rep'), may hold values from 3.1789146e-08 to 9.536743e-06
- col_state: float32 [32, 6144], P('rep', 'fsdp'), may hold values from 3.1789146e-08 to 9.536743e-06
- anchor: float32 [3072, 6144], P('rep', 'fsdp'), may hold values from -6 to 6
- momentum: float32 [3072, 6144], P('rep', 'fsdp'), may hold values from -4 to 4
Outputs:
- merged_weight: bfloat16 [32, 3072, 6144], P('rep', None, 'fsdp')
- row_next: float32 [32, 3072], P('rep')
- col_next: float32 [32, 6144], P('rep', 'fsdp')
- anchor_next: float32 [3072, 6144], P('rep', 'fsdp')
- momentum_next: float32 [3072, 6144], P('rep', 'fsdp')
All inputs are finite; a program needn't handle non-finite values.
Results may differ from a plain program's by a relative error of at most 0.015.
Values may be sent and summed in bfloat16 or wider, within the bound.
No kernel may reach another device: no remote copies, remote signals or barrier semaphores. Data moves between devices by JAX's collectives and lax.ppermute only.
A program may use at most 128 MiB of HBM per device.

v0:
```python
import functools

import jax
import jax.numpy as jnp
from jax import lax
from jax.experimental import pallas as pl
from jax.experimental.pallas import tpu as pltpu
from jax.sharding import Mesh, PartitionSpec as P

D = 6144
decay_second = 0.95
inner_rate = 0.25
weight_decay = 0.1
outer_rate = 0.7
outer_momentum = 0.9

NZ, NX, NC, NH, NY = 4, 4, 2, 2, 4
VMEM_LIMIT = 60 * 1024 * 1024
SMALL_LIMIT = 12 * 1024 * 1024
SHADE = 16


def after(value, *others):
    return lax.optimization_barrier((value, *others))[0]


def ring(n, k):
    return [(i, (i + k) % n) for i in range(n)]


def pieces_kernel(n, index_ref, *refs):
    mine, pair, outs = refs[:n], refs[n : 2 * n], refs[2 * n :]
    for a, b, out in zip(mine, pair, outs):
        total = a[0, 0, 0].astype(jnp.float32) + b[0, 0].astype(jnp.float32)
        out[0] = total.astype(out.dtype)


def pieces_call(grid, pair, c, columns):
    nz, nx, _, rows, width = grid.shape
    n = len(columns)
    index = jnp.stack([c, *columns]).astype(jnp.int32)

    def mine_spec(i):
        return pl.BlockSpec((1, 1, 1, rows, width), lambda j, s: (j, s[i + 1], s[0], 0, 0))

    def pair_spec(i):
        return pl.BlockSpec((1, 1, rows, width), lambda j, s: (j, s[i + 1], 0, 0))

    return pl.pallas_call(
        functools.partial(pieces_kernel, n),
        grid_spec=pltpu.PrefetchScalarGridSpec(
            num_scalar_prefetch=1,
            grid=(nz,),
            in_specs=[mine_spec(i) for i in range(n)] + [pair_spec(i) for i in range(n)],
            out_specs=[pl.BlockSpec((1, rows, width), lambda j, s: (j, 0, 0))] * n,
        ),
        out_shape=[jax.ShapeDtypeStruct((nz, rows, width), jnp.bfloat16)] * n,
        compiler_params=pltpu.CompilerParams(vmem_limit_bytes=SMALL_LIMIT),
        cost_estimate=pl.CostEstimate(
            flops=0, bytes_accessed=400 * 1000 * 1000, transcendentals=0
        ),
        name="pieces",
    )(index, *([grid] * n), *([pair] * n))


def corner_kernel(in_ref, out_ref):
    out_ref[...] = in_ref[...]


def corner(array):
    block = pl.BlockSpec((16, 128), lambda i: (0, 0))
    return pl.pallas_call(
        corner_kernel,
        grid=(1,),
        in_specs=[block],
        out_specs=block,
        out_shape=jax.ShapeDtypeStruct((16, 128), array.dtype),
        compiler_params=pltpu.CompilerParams(vmem_limit_bytes=SMALL_LIMIT),
        name="corner",
    )(array)


def total_kernel(index_ref, here, near, back, far, corner_ref, a_ref, b_ref, c_ref, own_ref):
    step = pl.program_id(0)
    total = here[0].astype(jnp.float32)
    for array in (near, back, far):
        total = total + array[0].astype(jnp.float32)

    for i, out in enumerate((a_ref, b_ref, c_ref, own_ref)):

        @pl.when(step == i)
        def _(out=out):
            out[...] = total.astype(out.dtype)


def total_call(arrays, waited, order):
    nz, rows, width = arrays[0].shape
    block = pl.BlockSpec((1, rows, width), lambda j, s: (s[j], 0, 0))
    out = pl.BlockSpec((rows, width), lambda j, s: (0, 0))
    half = jax.ShapeDtypeStruct((rows, width), jnp.bfloat16)
    return pl.pallas_call(
        total_kernel,
        grid_spec=pltpu.PrefetchScalarGridSpec(
            num_scalar_prefetch=1,
            grid=(nz,),
            in_specs=[block] * 4 + [pl.BlockSpec(memory_space=pl.ANY)],
            out_specs=[out] * 4,
        ),
        out_shape=[half] * 3 + [jax.ShapeDtypeStruct((rows, width), jnp.float32)],
        compiler_params=pltpu.CompilerParams(vmem_limit_bytes=SMALL_LIMIT),
        name="total",
    )(order, *arrays, waited)


def resid_kernel(scale, heights, index_ref, w_ref, *refs):
    n = len(heights)
    blocks, goals, out_ref = refs[:n], refs[n:-1], refs[-1]
    acts = jnp.concatenate([b[...] for b in blocks], axis=0)
    output = jnp.dot(acts, w_ref[...], preferred_element_type=jnp.float32) * scale
    goal = jnp.concatenate([g[...] for g in goals], axis=0).astype(jnp.float32)
    out_ref[...] = (output - goal).astype(jnp.bfloat16)


def resid_call(blocks, weight, targets, index, scale):
    heights = tuple(b.shape[0] for b in blocks)
    rows, hf = sum(heights), weight.shape[0]
    width, step = weight.shape[1], 256
    goals = rows // 128

    def goal_spec(i):
        return pl.BlockSpec((128, step), lambda j, s: (s[i], j))

    return pl.pallas_call(
        functools.partial(resid_kernel, scale, heights),
        grid_spec=pltpu.PrefetchScalarGridSpec(
            num_scalar_prefetch=1,
            grid=(width // step,),
            in_specs=[pl.BlockSpec((hf, step), lambda j, s: (0, j))]
            + [pl.BlockSpec(b.shape, lambda j, s: (0, 0)) for b in blocks]
            + [goal_spec(i) for i in range(goals)],
            out_specs=pl.BlockSpec((rows, step), lambda j, s: (0, j)),
        ),
        out_shape=jax.ShapeDtypeStruct((rows, width), jnp.bfloat16),
        compiler_params=pltpu.CompilerParams(vmem_limit_bytes=VMEM_LIMIT),
        cost_estimate=pl.CostEstimate(
            flops=2 * rows * hf * width // SHADE,
            bytes_accessed=2 * (rows * hf + hf * width + 2 * rows * width) // SHADE,
            transcendentals=0,
        ),
        name="resid",
    )(index, weight, *blocks, *([targets] * goals))


def grad_kernel(scale, n, m, more, *refs):
    blocks, resids = refs[:n], refs[n : n + m]
    grad_ref, row_ref, col_ref = refs[-3:]
    acts = jnp.concatenate([b[...] for b in blocks], axis=0)
    resid = jnp.concatenate([r[...] for r in resids], axis=0)
    grad = lax.dot_general(
        acts, resid, (((0,), (0,)), ((), ())), preferred_element_type=jnp.float32
    ) * scale
    grad_ref[...] = grad.astype(grad_ref.dtype)
    squares = grad * grad + 1e-30
    width = squares.shape[1]
    part = squares[:, :128]
    for k in range(1, width // 128):
        part = part + squares[:, k * 128 : (k + 1) * 128]
    row_ref[...] = jnp.sum(part.T, axis=0, keepdims=True)

    @pl.when(pl.program_id(0) == 0)
    def _():
        col_ref[...] = refs[n + m][...] if more else jnp.zeros_like(col_ref)

    col_ref[...] += jnp.sum(squares, axis=0, keepdims=True)


def grad_call(blocks, resids, scale, part, parts, partial=None):
    rows = sum(b.shape[0] for b in blocks)
    hf, width, step = blocks[0].shape[1], resids[0].shape[1], 512
    steps = hf // step // parts
    base = part * steps
    given, given_specs, aliases = [], [], {}
    if partial is not None:
        grad, row, col = partial
        given = [col, grad, row]
        given_specs = [pl.BlockSpec((1, width), lambda j: (0, 0))]
        given_specs += [pl.BlockSpec(memory_space=pl.ANY)] * 2
        first = len(blocks) + len(resids)
        aliases = {first + 1: 0, first + 2: 1}
    return pl.pallas_call(
        functools.partial(grad_kernel, scale, len(blocks), len(resids), bool(given)),
        grid=(steps,),
        in_specs=[pl.BlockSpec((b.shape[0], step), lambda j: (0, j + base)) for b in blocks]
        + [pl.BlockSpec(r.shape, lambda j: (0, 0)) for r in resids]
        + given_specs,
        out_specs=[
            pl.BlockSpec((step, width), lambda j: (j + base, 0)),
            pl.BlockSpec((1, step), lambda j: (0, j + base)),
            pl.BlockSpec((1, width), lambda j: (0, 0)),
        ],
        out_shape=[
            jax.ShapeDtypeStruct((hf, width), jnp.bfloat16),
            jax.ShapeDtypeStruct((1, hf), jnp.float32),
            jax.ShapeDtypeStruct((1, width), jnp.float32),
        ],
        input_output_aliases=aliases,
        compiler_params=pltpu.CompilerParams(vmem_limit_bytes=VMEM_LIMIT),
        cost_estimate=pl.CostEstimate(
            flops=2 * rows * hf * width // parts,
            bytes_accessed=(2 * rows * (hf + width) + 2 * hf * width) // parts,
            transcendentals=0,
        ),
        name="grad",
    )(*blocks, *resids, *given)


SLOTS = 8


def merge_kernel(
    pieces, index_ref, row_state, row_a, row_b, col_state, col_sum, grad_ref, w_ref, *refs
):
    n = len(pieces)
    sources, refs = refs[:-12], refs[-12:]
    out_ref, row_next, col_next, g_buf, w_buf, a_buf, o_buf, column = refs[:8]
    g_sem, w_sem, a_sem, o_sem = refs[8:]
    rows = w_buf.shape[1]

    def at(i):
        return pl.ds(pl.multiple_of(index_ref[i] * rows, rows), rows)

    def loads(i):
        s = i % SLOTS
        array, part = pieces[i]
        return (
            pltpu.make_async_copy(grad_ref.at[at(i)], g_buf.at[s], g_sem.at[s]),
            pltpu.make_async_copy(w_ref.at[at(i)], w_buf.at[s], w_sem.at[s]),
            pltpu.make_async_copy(sources[array].at[part], a_buf.at[s], a_sem.at[s]),
        )

    def store(i):
        s = i % SLOTS
        return pltpu.make_async_copy(o_buf.at[s], out_ref.at[at(i)], o_sem.at[s])

    for i in range(SLOTS - 1):
        for copy in loads(i):
            copy.start()

    hf = w_ref.shape[0]
    row_new = decay_second * row_state[...] + (1.0 - decay_second) * (
        (row_a[...] + row_b[...]) / D
    )
    row_next[...] = row_new
    col_new = decay_second * col_state[...] + (1.0 - decay_second) * (col_sum[...] / hf)
    col_next[...] = col_new
    turned = lax.rsqrt(row_new).T
    for i in range(turned.shape[1]):
        column[i * 128 : (i + 1) * 128, :] = turned[:, i : i + 1]
    colfac = (0.5 * inner_rate) * lax.rsqrt(col_new) * jnp.sqrt(jnp.mean(row_new))

    for i in range(n):
        if i + SLOTS - 1 < n:
            for copy in loads(i + SLOTS - 1):
                copy.start()
        for copy in loads(i):
            copy.wait()
        s = i % SLOTS
        if i >= SLOTS:
            store(i - SLOTS).wait()
        w = w_buf[s].astype(jnp.float32)
        a = a_buf[s].astype(jnp.float32)
        keep = 0.5 * (1.0 - inner_rate * weight_decay)
        step = g_buf[s].astype(jnp.float32) * column[at(i), :] * colfac
        o_buf[s] = (keep * w - step + 0.5 * a).astype(jnp.bfloat16)
        store(i).start()
    for i in range(n - SLOTS, n):
        store(i).wait()


def merge_call(sources, pieces, index, row_state, row_a, row_b, col_state, col_sum, grad, weight):
    rows, width = 96, weight.shape[1]
    vmem = pl.BlockSpec(memory_space=pltpu.VMEM)
    anywhere = pl.BlockSpec(memory_space=pl.ANY)
    return pl.pallas_call(
        functools.partial(merge_kernel, pieces),
        in_specs=[pl.BlockSpec(memory_space=pltpu.SMEM)]
        + [vmem] * 5
        + [anywhere] * (2 + len(sources)),
        out_specs=[anywhere, vmem, vmem],
        out_shape=[
            jax.ShapeDtypeStruct(weight.shape, jnp.bfloat16),
            jax.ShapeDtypeStruct(row_state.shape, jnp.float32),
            jax.ShapeDtypeStruct(col_state.shape, jnp.float32),
        ],
        scratch_shapes=[pltpu.VMEM((SLOTS, rows, width), jnp.bfloat16)] * 4
        + [pltpu.VMEM((weight.shape[0], 1), jnp.float32)]
        + [pltpu.SemaphoreType.DMA((SLOTS,))] * 4,
        compiler_params=pltpu.CompilerParams(vmem_limit_bytes=VMEM_LIMIT),
        cost_estimate=pl.CostEstimate(
            flops=8 * weight.size, bytes_accessed=8 * weight.size, transcendentals=0
        ),
        name="merge",
    )(index, row_state, row_a, row_b, col_state, col_sum, grad, weight, *sources)


def body(activations, targets, replica_weight, row_state, col_state, anchor, momentum):
    weight = replica_weight[0]
    hf, width = weight.shape
    island = targets.shape[0]
    inv_root = 1.0 / float(hf) ** 0.5
    mesh_size = {"zl": NZ, "x": NX, "c": NC, "zh": NH, "y": NY}
    zl, x, c = lax.axis_index("zl"), lax.axis_index("x"), lax.axis_index("c")
    zh, y = lax.axis_index("zh"), lax.axis_index("y")
    rows = hf // (NZ * NX * NC)

    def send(block, axis, k, what):
        with jax.named_scope(what):
            return lax.ppermute(block, axis, ring(mesh_size[axis], k))

    side = 1 - 2 * c

    def turn(block, axis, k, what):
        n = mesh_size[axis]
        axes = ("x", "c") if axis == "x" else ("c", axis)

        def place(i, j):
            return i * NC + j if axis == "x" else j * n + i

        pairs = [
            (place(i, j), place((i + (k if j == 0 else -k)) % n, j))
            for i in range(n)
            for j in range(NC)
        ]
        with jax.named_scope(what):
            return lax.ppermute(block, axes, pairs)

    grid = weight.reshape(NZ, NX, NC, rows, width)
    theirs = lax.dynamic_index_in_dim(grid, 1 - c, 2, keepdims=False)
    pair = send(theirs, "c", 1, "sum_core")
    near = turn(activations, "y", 1, "acts_near")
    zown = send(activations, "zh", 1, "acts_zown")

    half_type = jnp.bfloat16
    here, ahead, behind, across = pieces_call(
        grid, pair, c, [(x + dx + NX) % NX for dx in (0, side, -side, 2)]
    )
    far = turn(after(near, ahead), "y", 1, "acts_far")
    got_near = turn(ahead, "x", 1, "sum_near")
    got_back = turn(behind, "x", -1, "sum_back")
    got_far = send(across, "x", 2, "sum_far")
    back = turn(after(activations, got_far), "y", -1, "acts_back")
    z_order = (2, 1, 3, 0)
    *z_sent, share = total_call(
        (here, got_near, got_back, got_far),
        corner(zown),
        jnp.stack([(zl + k) % NZ for k in z_order]).astype(jnp.int32),
    )
    z_sent = [after(p, far, back) for p in z_sent]
    z_got = [send(p, "zl", k, "sum_z%d" % k) for p, k in zip(z_sent, z_order)]
    znear = turn(after(zown, *z_sent), "y", 1, "acts_znear")
    zback = turn(after(zown, *z_sent), "y", -1, "acts_zback")
    def goal(dz, dy):
        return (zh + dz) % NH * NY + (y + dy + NY) % NY

    parts = [
        (
            [activations, near, back, far],
            [goal(0, 0), goal(0, -side), goal(0, side), goal(0, 2)],
        ),
        (
            [zown, znear, zback],
            [goal(1, 0), goal(1, -side), goal(1, side), goal(1, 2)],
        ),
    ]
    def resid_of(g, *wait):
        held, goals = parts[g]
        index = after(jnp.stack(goals).astype(jnp.int32), *wait)
        return resid_call(held, weight, targets, index, inv_root)

    resids = [resid_of(0, *z_sent)]
    zfar = turn(after(znear, resids[0], *z_got), "y", 1, "acts_zfar")
    parts[1][0].append(zfar)
    for got in z_got:
        share = share + got.astype(jnp.float32)
    share = after(share, znear, zback, resids[0])

    outer_grad = anchor - share / (NZ * NX * NC)
    momentum_next = outer_momentum * momentum + outer_grad
    anchor_next = anchor - outer_rate * (outer_grad + outer_momentum * momentum_next)
    half = anchor_next.astype(jnp.bfloat16)[None]

    over_z = [send(half, "zl", k, "new_z%d" % k) for k in (1, 2, 3)]
    resids.append(resid_of(1, half))
    over_z = [after(o, *resids) for o in over_z]
    held = jnp.concatenate([half] + over_z)
    new_near = turn(held, "x", 1, "new_near")
    new_back = turn(held, "x", -1, "new_back")
    blocks = [b for blocks, _ in parts for b in blocks]
    scale = inv_root / island
    grad, row_sum, col_sum = grad_call(blocks, resids, scale, 0, 1)
    row_sum = row_sum.reshape(hf // 128, 128)
    row_a = row_sum
    for k in (1, 2, 3):
        row_a = row_a + send(row_sum, "y", k, "row_y")
    row_b = send(row_a, "zh", 1, "row_z")

    new_far = turn(after(new_near, new_back, row_a), "x", 1, "new_far")
    sources, pieces, places = [], [], []
    late = ((held, 0), (new_near, -side), (new_back, side), (new_far, 2))
    for i, (block, origin) in enumerate(late):
        for swap in (0, 1):
            from_c = 1 - c if swap else c
            from_x = (x + (-origin if swap else origin) + NX) % NX
            for k in range(NZ):
                pieces.append((len(sources), k))
                places.append(((zl + NZ - k) % NZ * NX + from_x) * NC + from_c)
            sources.append(send(after(block, row_b if i == 3 else row_a), "c", 1, "new_core") if swap else block)
    places = jnp.stack(places).astype(jnp.int32)

    merged, row_new, col_new = merge_call(
        sources,
        tuple(pieces),
        places,
        row_state.reshape(row_sum.shape),
        row_a,
        row_b,
        col_state,
        col_sum,
        grad,
        weight,
    )
    return (merged[None], row_new.reshape(row_state.shape), col_new, anchor_next, momentum_next)


def solution(mesh):
    fine = Mesh(
        mesh.devices.reshape(NZ, NX, NC, NH, NY), ("zl", "x", "c", "zh", "y")
    )
    rep, fsdp = ("zl", "x", "c"), ("zh", "y")
    placed = (
        P(rep + fsdp, None),
        P(rep, fsdp),
        P(rep, None, fsdp),
        P(rep, None),
        P(rep, fsdp),
        P(rep, fsdp),
        P(rep, fsdp),
    )
    return jax.shard_map(
        body,
        mesh=fine,
        in_specs=placed,
        out_specs=(
            P(rep, None, fsdp),
            P(rep, None),
            P(rep, fsdp),
            P(rep, fsdp),
            P(rep, fsdp),
        ),
        check_vma=False,
    )
```

profile of v0, /device:TPU:1, one launch (start us, length us, event | category | flops | bytes accessed | tf_op | source)
XLA Modules:
  0.0 143.6 jit_solution(3595346585476332434)
XLA Ops:
  0.6 3.2 %dynamic-slice_bitcast_fusion = bf16[4,4,96,768]{3,2,1,0:T(8,128)(2,1)} fusion(bf16[4,4,2,96,768]{4,3,2,1,0:T(8,128)(2,1)} %bitcast.59, s32[]{:T(128)S(6)} %select_n.176), kind=kLoop, calls=%fused_computation | loop fusion | bytes 4718596 | tf_op jit(solution)/shard_map/jit(dynamic_index_in_dim)/squeeze | solution.py:338
  3.9 3.2 %collective-permute-start.1 = (bf16[4,4,96,768]{3,2,1,0:T(8,128)(2,1)}, bf16[4,4,96,768]{3,2,1,0:T(8,128)(2,1)S(1)}, u32[]{:S(2)}, u32[]{:S(2)}) collective-permute-start(bf16[4,4,96,768]{3,2,1,0:T(8,128)(2,1)} %dynamic-slice_bitcast_fusion), channel_id=1, source_target_pairs={{0,8},{8,0},{1,9},{9,1},{2,10},{10,2},{3,11},{11,3},{4,12},{12,4},... | collective-permute-start | bytes 7077896 | tf_op jit(solution)/shard_map/sum_core/ppermute | solution.py:318
  7.1 1.0 collective-permute-start
  8.1 0.1 stack.200.index_ref
  8.2 3.3 %collective-permute-done.1.refs_4_.refs_5_.refs_6_.refs_7_ = bf16[4,4,96,768]{3,2,1,0:T(8,128)(2,1)S(1)} collective-permute-done((bf16[4,4,96,768]{3,2,1,0:T(8,128)(2,1)}, bf16[4,4,96,768]{3,2,1,0:T(8,128)(2,1)S(1)}, u32[]{:S(2)}, u32[]{:S(2)}) %collective-permute-start.1) | collective-permute-done | bytes 2359328 | tf_op jit(solution)/shard_map/sum_core/ppermute | solution.py:318
  11.5 2.3 %copy-done = bf16[1,3072,768]{2,1,0:T(8,128)(2,1)S(1)} copy-done((bf16[1,3072,768]{2,1,0:T(8,128)(2,1)S(1)}, bf16[1,3072,768]{2,1,0:T(8,128)(2,1)}, u32[]{:S(2)}) %copy-start) | copy-done | bytes 4718616
  13.8 2.3 %pieces.1 = (bf16[4,96,768]{2,1,0:T(8,128)(2,1)S(1)}, bf16[4,96,768]{2,1,0:T(8,128)(2,1)}, bf16[4,96,768]{2,1,0:T(8,128)(2,1)}, bf16[4,96,768]{2,1,0:T(8,128)(2,1)S(1)}) custom-call(s32[5]{0:T(128)S(1)} %stack.200.index_ref, bf16[4,4,2,96,768]{4,3,2,1,0:T(8,128)(2,1)S(1)} %bitcast.63, bf16[4,4,2,96,768]{4,3,2,1,0:T(8,128)(2,1)S(1)} %bitcast.64, ...), custom_call_target="tpu_custom_call" | custom-call | bytes 400000000 | tf_op jit(solution)/shard_map/pieces/pallas_call | solution.py:49
  16.2 1.0 collective-permute-start.2
  17.2 6.9 %collective-permute-start.5 = (bf16[128,3072]{1,0:T(8,128)(2,1)}, bf16[128,3072]{1,0:T(8,128)(2,1)S(1)}, u32[]{:S(2)}, u32[]{:S(2)}) collective-permute-start(bf16[128,3072]{1,0:T(8,128)(2,1)} %refs_0_.3), channel_id=1, source_target_pairs={{0,4},{4,0},{1,5},{5,1},{2,6},{6,2},{3,7},{7,3},{8,12},{12,8},{9,1... | collective-permute-start | bytes 2359304 | tf_op jit(solution)/shard_map/acts_zown/ppermute | solution.py:318
  24.1 2.7 %collective-permute-start.4 = (bf16[128,3072]{1,0:T(8,128)(2,1)}, bf16[128,3072]{1,0:T(8,128)(2,1)}, u32[]{:S(2)}, u32[]{:S(2)}) collective-permute-start(bf16[128,3072]{1,0:T(8,128)(2,1)} %collective-permute-done.refs_1_), channel_id=1, source_target_pairs={{0,1},{8,11},{1,2},{9,8},{2,3},{10,9},{3,0},{11,10},{4,5},{12,15},... | collective-permute-start | bytes 2359304 | tf_op jit(solution)/shard_map/acts_far/ppermute | solution.py:335
  26.8 5.4 %collective-permute-done.2.far = bf16[4,96,768]{2,1,0:T(8,128)(2,1)S(1)} collective-permute-done((bf16[4,96,768]{2,1,0:T(8,128)(2,1)S(1)}, bf16[4,96,768]{2,1,0:T(8,128)(2,1)S(1)}, u32[]{:S(2)}, u32[]{:S(2)}) %collective-permute-start.2) | collective-permute-done | bytes 589856 | tf_op jit(solution)/shard_map/sum_far/ppermute | solution.py:318
  32.2 0.8 collective-permute-start.7
  33.0 1.9 %collective-permute-start.6 = (bf16[4,96,768]{2,1,0:T(8,128)(2,1)}, bf16[4,96,768]{2,1,0:T(8,128)(2,1)S(1)}, u32[]{:S(2)}, u32[]{:S(2)}) collective-permute-start(bf16[4,96,768]{2,1,0:T(8,128)(2,1)} %get-tuple-element.39), channel_id=1, source_target_pairs={{0,16},{8,56},{16,32},{24,8},{32,48},{40,24},{48,0},{56,40},{1,17}... | collective-permute-start | bytes 1769480 | tf_op jit(solution)/shard_map/sum_near/ppermute | solution.py:335
  35.0 10.0 %collective-permute-done.5.in_ref.refs_0_.refs_4_ = bf16[128,3072]{1,0:T(8,128)(2,1)S(1)} collective-permute-done((bf16[128,3072]{1,0:T(8,128)(2,1)}, bf16[128,3072]{1,0:T(8,128)(2,1)S(1)}, u32[]{:S(2)}, u32[]{:S(2)}) %collective-permute-start.5) | collective-permute-done | bytes 786464 | tf_op jit(solution)/shard_map/acts_zown/ppermute | solution.py:318
  44.9 1.4 collective-permute-done.6.near
  46.3 1.8 %total.1 = (bf16[96,768]{1,0:T(8,128)(2,1)}, bf16[96,768]{1,0:T(8,128)(2,1)}, bf16[96,768]{1,0:T(8,128)(2,1)}, f32[96,768]{1,0:T(8,128)S(1)}) custom-call(s32[4]{0:T(128)S(1)} %pad_add_fusion.index_ref, bf16[4,96,768]{2,1,0:T(8,128)(2,1)S(1)} %get-tuple-element.41.here, bf16[4,96,768]{2,1,0:T(8,128)(2,1)S(1)} %collective-permute-done.6.near, ...), custom_call_target="tpu_custom_call" | custom-call | tf_op jit(solution)/shard_map/total/pallas_call | solution.py:101
  48.1 4.3 %collective-permute-start.8 = (bf16[128,3072]{1,0:T(8,128)(2,1)S(1)}, bf16[128,3072]{1,0:T(8,128)(2,1)S(1)}, u32[]{:S(2)}, u32[]{:S(2)}) collective-permute-start(bf16[128,3072]{1,0:T(8,128)(2,1)S(1)} %collective-permute-done.5.in_ref.refs_0_.refs_4_), channel_id=1, source_target_pairs={{0,1},{8,11},{1,2},{9,8},{2,3},{10,9},{3,0},{11,10},{4,5},{12,15},... | collective-permute-start | bytes 2359304 | tf_op jit(solution)/shard_map/acts_znear/ppermute | solution.py:335
  52.4 12.2 %collective-permute-start.10 = (bf16[96,768]{1,0:T(8,128)(2,1)}, bf16[96,768]{1,0:T(8,128)(2,1)S(1)}, u32[]{:S(2)}, u32[]{:S(2)}) collective-permute-start(bf16[96,768]{1,0:T(8,128)(2,1)} %get-tuple-element.44), channel_id=1, source_target_pairs={{0,128},{64,192},{128,0},{192,64},{1,129},{65,193},{129,1},{193,65... | collective-permute-start | bytes 442376 | tf_op jit(solution)/shard_map/sum_z2/ppermute | solution.py:318
  64.6 3.3 %collective-permute-start.12 = (bf16[96,768]{1,0:T(8,128)(2,1)}, bf16[96,768]{1,0:T(8,128)(2,1)}, u32[]{:S(2)}, u32[]{:S(2)}) collective-permute-start(bf16[96,768]{1,0:T(8,128)(2,1)} %get-tuple-element.48), channel_id=1, source_target_pairs={{0,192},{64,0},{128,64},{192,128},{1,193},{65,1},{129,65},{193,129... | collective-permute-start | bytes 442376 | tf_op jit(solution)/shard_map/sum_z3/ppermute | solution.py:318
  67.9 0.6 pad_add_fusion.1.index_ref
  68.5 7.6 %resid.2.refs_8_ = bf16[512,768]{1,0:T(8,128)(2,1)} custom-call(s32[4]{0:T(128)} %pad_add_fusion.1.index_ref, bf16[3072,768]{1,0:T(8,128)(2,1)} %bitcast.60, bf16[128,3072]{1,0:T(8,128)(2,1)} %refs_0_.3, bf16[128,3072]{1,0:T(8,128)(2,1)} %collective-permute-done.refs_1_, bf16[128,3072]{1,0:T(8,128)(2,1)} %collective-permute-done.3.refs_2_, ...), custom_call_target="tpu_custom_call" | custom-call | flops 150994944 | bytes 589824 | tf_op jit(solution)/shard_map/resid/pallas_call | solution.py:133
  76.1 2.7 %collective-permute-start.13 = (bf16[128,3072]{1,0:T(8,128)(2,1)S(1)}, bf16[128,3072]{1,0:T(8,128)(2,1)}, u32[]{:S(2)}, u32[]{:S(2)}) collective-permute-start(bf16[128,3072]{1,0:T(8,128)(2,1)S(1)} %collective-permute-done.8.refs_1_.refs_5_), channel_id=1, source_target_pairs={{0,1},{8,11},{1,2},{9,8},{2,3},{10,9},{3,0},{11,10},{4,5},{12,15},... | collective-permute-start | bytes 2359304 | tf_op jit(solution)/shard_map/acts_zfar/ppermute | solution.py:335
  78.9 1.0 convert_add_fusion
  79.9 1.0 convert_bitcast_fusion
  81.0 1.9 %collective-permute-start.20 = (bf16[1,96,768]{2,1,0:T(8,128)(2,1)S(1)}, bf16[1,96,768]{2,1,0:T(8,128)(2,1)S(1)}, u32[]{:S(2)}, u32[]{:S(2)}) collective-permute-start(bf16[1,96,768]{2,1,0:T(8,128)(2,1)S(1)} %get-tuple-element.69), channel_id=1, source_target_pairs={{0,192},{64,0},{128,64},{192,128},{1,193},{65,1},{129,65},{193,129... | collective-permute-start | bytes 442376 | tf_op jit(solution)/shard_map/new_z3/ppermute | solution.py:318
  82.8 3.0 %collective-permute-start.19 = (bf16[1,96,768]{2,1,0:T(8,128)(2,1)S(1)}, bf16[1,96,768]{2,1,0:T(8,128)(2,1)S(1)}, u32[]{:S(2)}, u32[]{:S(2)}) collective-permute-start(bf16[1,96,768]{2,1,0:T(8,128)(2,1)S(1)} %get-tuple-element.69), channel_id=1, source_target_pairs={{0,128},{64,192},{128,0},{192,64},{1,129},{65,193},{129,1},{193,65... | collective-permute-start | bytes 442376 | tf_op jit(solution)/shard_map/new_z2/ppermute | solution.py:318
  85.8 1.2 collective-permute-start.18
  87.0 0.7 pad_add_fusion.2.index_ref
  87.7 0.1 collective-permute-done.13.refs_3_.refs_7_
  87.8 7.5 %resid.3.refs_9_ = bf16[512,768]{1,0:T(8,128)(2,1)} custom-call(s32[4]{0:T(128)} %pad_add_fusion.2.index_ref, bf16[3072,768]{1,0:T(8,128)(2,1)} %bitcast.61, bf16[128,3072]{1,0:T(8,128)(2,1)} %copy-done.1, bf16[128,3072]{1,0:T(8,128)(2,1)} %copy-done.3, bf16[128,3072]{1,0:T(8,128)(2,1)} %copy-done.4, ...), custom_call_target="tpu_custom_call" | custom-call | flops 150994944 | bytes 589824 | tf_op jit(solution)/shard_map/resid/pallas_call | solution.py:133
  95.3 2.2 %collective-permute-done.19 = bf16[1,96,768]{2,1,0:T(8,128)(2,1)S(1)} collective-permute-done((bf16[1,96,768]{2,1,0:T(8,128)(2,1)S(1)}, bf16[1,96,768]{2,1,0:T(8,128)(2,1)S(1)}, u32[]{:S(2)}, u32[]{:S(2)}) %collective-permute-start.19) | collective-permute-done | bytes 147488 | tf_op jit(solution)/shard_map/new_z2/ppermute | solution.py:318
  97.5 0.4 collective-permute-start.24
  97.9 2.4 %collective-permute-start.22 = (bf16[4,96,768]{2,1,0:T(8,128)(2,1)S(1)}, bf16[4,96,768]{2,1,0:T(8,128)(2,1)S(1)}, u32[]{:S(2)}, u32[]{:S(2)}) collective-permute-start(bf16[4,96,768]{2,1,0:T(8,128)(2,1)S(1)} %pad_maximum_fusion.refs_0_), channel_id=1, source_target_pairs={{0,16},{8,56},{16,32},{24,8},{32,48},{40,24},{48,0},{56,40},{1,17}... | collective-permute-start | bytes 1769480 | tf_op jit(solution)/shard_map/new_near/ppermute | solution.py:335
  100.3 10.7 %grad.1 = (bf16[3072,768]{1,0:T(8,128)(2,1)}, f32[1,3072]{1,0:T(1,128)}, f32[1,768]{1,0:T(1,128)}) custom-call(bf16[128,3072]{1,0:T(8,128)(2,1)} %refs_0_.3, bf16[128,3072]{1,0:T(8,128)(2,1)} %collective-permute-done.refs_1_, bf16[128,3072]{1,0:T(8,128)(2,1)} %collective-permute-done.3.refs_2_, bf16[128,3072]{1,0:T(8,128)(2,1)} %collective-permute-done.4.refs_3_, ...), custom_call_target="tpu_custom_call" | custom-call | flops 4831838208 | bytes 12582912 | tf_op jit(solution)/shard_map/grad/pallas_call | solution.py:190
  111.0 1.2 collective-permute-start.16
  112.2 0.7 collective-permute-start.14
  112.8 1.3 collective-permute-done.16
  114.1 2.3 %collective-permute-done.15 = f32[24,128]{1,0:T(8,128)S(1)} collective-permute-done((f32[24,128]{1,0:T(8,128)}, f32[24,128]{1,0:T(8,128)S(1)}, u32[]{:S(2)}, u32[]{:S(2)}) %collective-permute-start.15) | collective-permute-done | bytes 12320 | tf_op jit(solution)/shard_map/row_y/ppermute | solution.py:318
  116.4 0.7 add_add_fusion.row_a
  117.2 0.2 collective-permute-start.26
  117.4 4.9 %collective-permute-start.17 = (f32[24,128]{1,0:T(8,128)S(1)}, f32[24,128]{1,0:T(8,128)S(1)}, u32[]{:S(2)}, u32[]{:S(2)}) collective-permute-start(f32[24,128]{1,0:T(8,128)S(1)} %add_add_fusion.row_a), channel_id=1, source_target_pairs={{0,4},{4,0},{1,5},{5,1},{2,6},{6,2},{3,7},{7,3},{8,12},{12,8},{9,1... | collective-permute-start | bytes 36872 | tf_op jit(solution)/shard_map/row_z/ppermute | solution.py:318
  122.3 4.3 %collective-permute-start.21 = (bf16[4,96,768]{2,1,0:T(8,128)(2,1)S(1)}, bf16[4,96,768]{2,1,0:T(8,128)(2,1)S(1)}, u32[]{:S(2)}, u32[]{:S(2)}) collective-permute-start(bf16[4,96,768]{2,1,0:T(8,128)(2,1)S(1)} %pad_maximum_fusion.refs_0_), channel_id=1, source_target_pairs={{0,8},{8,0},{1,9},{9,1},{2,10},{10,2},{3,11},{11,3},{4,12},{12,4},... | collective-permute-start | bytes 1769480 | tf_op jit(solution)/shard_map/new_core/ppermute | solution.py:318
  126.6 0.5 collective-permute-start.23
  127.1 0.6 copy-done.13
  127.7 4.2 %collective-permute-start.27 = (bf16[4,96,768]{2,1,0:T(8,128)(2,1)S(1)}, bf16[4,96,768]{2,1,0:T(8,128)(2,1)}, u32[]{:S(2)}, u32[]{:S(2)}) collective-permute-start(bf16[4,96,768]{2,1,0:T(8,128)(2,1)S(1)} %collective-permute-done.26.refs_6_), channel_id=1, source_target_pairs={{0,8},{8,0},{1,9},{9,1},{2,10},{10,2},{3,11},{11,3},{4,12},{12,4},... | collective-permute-start | bytes 1769480 | tf_op jit(solution)/shard_map/new_core/ppermute | solution.py:318
  132.0 0.7 stack.194.index_ref
  132.6 1.1 collective-permute-done.27.refs_7_
  133.8 9.6 %merge.1 = (bf16[3072,768]{1,0:T(8,128)(2,1)}, f32[24,128]{1,0:T(8,128)}, f32[1,768]{1,0:T(1,128)}) custom-call(s32[32]{0:T(128)} %stack.194.index_ref, f32[24,128]{1,0:T(8,128)} %bitcast.67, f32[24,128]{1,0:T(8,128)} %copy-done.12, f32[24,128]{1,0:T(8,128)} %copy-done.13, f32[1,768]{1,0:T(1,128)} %col_state.1, f32[1,768]{1,0:T(1,128)} %get-tuple-element.56.col_sum, ...), custom_call_target="tpu_custom_call" | custom-call | flops 18874368 | bytes 18874368 | tf_op jit(solution)/shard_map/merge/pallas_call | solution.py:284
  (53 shorter events, 0.3 us)
Async XLA Ops:
  3.9 7.6 %collective-permute-start.1 = (bf16[4,4,96,768]{3,2,1,0:T(8,128)(2,1)}, bf16[4,4,96,768]{3,2,1,0:T(8,128)(2,1)S(1)}, u32[]{:S(2)}, u32[]{:S(2)}) collective-permute-start(bf16[4,4,96,768]{3,2,1,0:T(8,128)(2,1)} %dynamic-slice_bitcast_fusion), channel_id=1, source_target_pairs={{0,8},{8,0},{1,9},{9,1},{2,10},{10,2},{3,11},{11,3},{4,12},{12,4},... | collective-permute-start | bytes 7077896 | tf_op jit(solution)/shard_map/sum_core/ppermute | solution.py:318
  7.1 17.0 %collective-permute-start = (bf16[128,3072]{1,0:T(8,128)(2,1)}, bf16[128,3072]{1,0:T(8,128)(2,1)}, u32[]{:S(2)}, u32[]{:S(2)}) collective-permute-start(bf16[128,3072]{1,0:T(8,128)(2,1)} %refs_0_.3), channel_id=1, source_target_pairs={{0,1},{8,11},{1,2},{9,8},{2,3},{10,9},{3,0},{11,10},{4,5},{12,15},... | collective-permute-start | bytes 2359304 | tf_op jit(solution)/shard_map/acts_near/ppermute | solution.py:335
  11.5 2.3 %copy-start = (bf16[1,3072,768]{2,1,0:T(8,128)(2,1)S(1)}, bf16[1,3072,768]{2,1,0:T(8,128)(2,1)}, u32[]{:S(2)}) copy-start(bf16[1,3072,768]{2,1,0:T(8,128)(2,1)} %param.9) | copy-start | bytes 14155780
  16.2 16.0 %collective-permute-start.2 = (bf16[4,96,768]{2,1,0:T(8,128)(2,1)S(1)}, bf16[4,96,768]{2,1,0:T(8,128)(2,1)S(1)}, u32[]{:S(2)}, u32[]{:S(2)}) collective-permute-start(bf16[4,96,768]{2,1,0:T(8,128)(2,1)S(1)} %get-tuple-element.37), channel_id=1, source_target_pairs={{0,32},{16,48},{32,0},{48,16},{1,33},{17,49},{33,1},{49,17},{2,34}... | collective-permute-start | bytes 1769480 | tf_op jit(solution)/shard_map/sum_far/ppermute | solution.py:318
  17.2 27.8 %collective-permute-start.5 = (bf16[128,3072]{1,0:T(8,128)(2,1)}, bf16[128,3072]{1,0:T(8,128)(2,1)S(1)}, u32[]{:S(2)}, u32[]{:S(2)}) collective-permute-start(bf16[128,3072]{1,0:T(8,128)(2,1)} %refs_0_.3), channel_id=1, source_target_pairs={{0,4},{4,0},{1,5},{5,1},{2,6},{6,2},{3,7},{7,3},{8,12},{12,8},{9,1... | collective-permute-start | bytes 2359304 | tf_op jit(solution)/shard_map/acts_zown/ppermute | solution.py:318
  24.1 24.0 %collective-permute-start.4 = (bf16[128,3072]{1,0:T(8,128)(2,1)}, bf16[128,3072]{1,0:T(8,128)(2,1)}, u32[]{:S(2)}, u32[]{:S(2)}) collective-permute-start(bf16[128,3072]{1,0:T(8,128)(2,1)} %collective-permute-done.refs_1_), channel_id=1, source_target_pairs={{0,1},{8,11},{1,2},{9,8},{2,3},{10,9},{3,0},{11,10},{4,5},{12,15},... | collective-permute-start | bytes 2359304 | tf_op jit(solution)/shard_map/acts_far/ppermute | solution.py:335
  32.2 15.9 %collective-permute-start.3 = (bf16[128,3072]{1,0:T(8,128)(2,1)}, bf16[128,3072]{1,0:T(8,128)(2,1)}, u32[]{:S(2)}, u32[]{:S(2)}) collective-permute-start(bf16[128,3072]{1,0:T(8,128)(2,1)} %refs_0_.3), channel_id=1, source_target_pairs={{0,3},{8,9},{1,0},{9,10},{2,1},{10,11},{3,2},{11,8},{4,7},{12,13},... | collective-permute-start | bytes 2359304 | tf_op jit(solution)/shard_map/acts_back/ppermute | solution.py:335
  32.2 12.7 %collective-permute-start.7 = (bf16[4,96,768]{2,1,0:T(8,128)(2,1)}, bf16[4,96,768]{2,1,0:T(8,128)(2,1)S(1)}, u32[]{:S(2)}, u32[]{:S(2)}) collective-permute-start(bf16[4,96,768]{2,1,0:T(8,128)(2,1)} %get-tuple-element.42), channel_id=1, source_target_pairs={{0,48},{8,24},{16,0},{24,40},{32,16},{40,56},{48,32},{56,8},{1,49}... | collective-permute-start | bytes 1769480 | tf_op jit(solution)/shard_map/sum_back/ppermute | solution.py:335
  33.0 13.3 %collective-permute-start.6 = (bf16[4,96,768]{2,1,0:T(8,128)(2,1)}, bf16[4,96,768]{2,1,0:T(8,128)(2,1)S(1)}, u32[]{:S(2)}, u32[]{:S(2)}) collective-permute-start(bf16[4,96,768]{2,1,0:T(8,128)(2,1)} %get-tuple-element.39), channel_id=1, source_target_pairs={{0,16},{8,56},{16,32},{24,8},{32,48},{40,24},{48,0},{56,40},{1,17}... | collective-permute-start | bytes 1769480 | tf_op jit(solution)/shard_map/sum_near/ppermute | solution.py:335
  44.9 31.1 %copy-start.1 = (bf16[128,3072]{1,0:T(8,128)(2,1)}, bf16[128,3072]{1,0:T(8,128)(2,1)S(1)}, u32[]{:S(2)}) copy-start(bf16[128,3072]{1,0:T(8,128)(2,1)S(1)} %collective-permute-done.5.in_ref.refs_0_.refs_4_) | copy-start | bytes 2359300
  48.1 28.0 %collective-permute-start.8 = (bf16[128,3072]{1,0:T(8,128)(2,1)S(1)}, bf16[128,3072]{1,0:T(8,128)(2,1)S(1)}, u32[]{:S(2)}, u32[]{:S(2)}) collective-permute-start(bf16[128,3072]{1,0:T(8,128)(2,1)S(1)} %collective-permute-done.5.in_ref.refs_0_.refs_4_), channel_id=1, source_target_pairs={{0,1},{8,11},{1,2},{9,8},{2,3},{10,9},{3,0},{11,10},{4,5},{12,15},... | collective-permute-start | bytes 2359304 | tf_op jit(solution)/shard_map/acts_znear/ppermute | solution.py:335
  52.4 27.5 %collective-permute-start.9 = (bf16[128,3072]{1,0:T(8,128)(2,1)S(1)}, bf16[128,3072]{1,0:T(8,128)(2,1)S(1)}, u32[]{:S(2)}, u32[]{:S(2)}) collective-permute-start(bf16[128,3072]{1,0:T(8,128)(2,1)S(1)} %collective-permute-done.5.in_ref.refs_0_.refs_4_), channel_id=1, source_target_pairs={{0,3},{8,9},{1,0},{9,10},{2,1},{10,11},{3,2},{11,8},{4,7},{12,13},... | collective-permute-start | bytes 2359304 | tf_op jit(solution)/shard_map/acts_zback/ppermute | solution.py:335
  52.4 23.6 %collective-permute-start.10 = (bf16[96,768]{1,0:T(8,128)(2,1)}, bf16[96,768]{1,0:T(8,128)(2,1)S(1)}, u32[]{:S(2)}, u32[]{:S(2)}) collective-permute-start(bf16[96,768]{1,0:T(8,128)(2,1)} %get-tuple-element.44), channel_id=1, source_target_pairs={{0,128},{64,192},{128,0},{192,64},{1,129},{65,193},{129,1},{193,65... | collective-permute-start | bytes 442376 | tf_op jit(solution)/shard_map/sum_z2/ppermute | solution.py:318
  64.6 11.5 %collective-permute-start.11 = (bf16[96,768]{1,0:T(8,128)(2,1)}, bf16[96,768]{1,0:T(8,128)(2,1)}, u32[]{:S(2)}, u32[]{:S(2)}) collective-permute-start(bf16[96,768]{1,0:T(8,128)(2,1)} %get-tuple-element.46), channel_id=1, source_target_pairs={{0,64},{64,128},{128,192},{192,0},{1,65},{65,129},{129,193},{193,1... | collective-permute-start | bytes 442376 | tf_op jit(solution)/shard_map/sum_z1/ppermute | solution.py:318
  64.6 11.5 %collective-permute-start.12 = (bf16[96,768]{1,0:T(8,128)(2,1)}, bf16[96,768]{1,0:T(8,128)(2,1)}, u32[]{:S(2)}, u32[]{:S(2)}) collective-permute-start(bf16[96,768]{1,0:T(8,128)(2,1)} %get-tuple-element.48), channel_id=1, source_target_pairs={{0,192},{64,0},{128,64},{192,128},{1,193},{65,1},{129,65},{193,129... | collective-permute-start | bytes 442376 | tf_op jit(solution)/shard_map/sum_z3/ppermute | solution.py:318
  68.4 11.5 %copy-start.10 = (f32[96,768]{1,0:T(8,128)S(1)}, f32[96,768]{1,0:T(8,128)}, u32[]{:S(2)}) copy-start(f32[96,768]{1,0:T(8,128)} %param.12) | copy-start | bytes 884740
  68.4 11.5 %copy-start.11 = (f32[96,768]{1,0:T(8,128)S(1)}, f32[96,768]{1,0:T(8,128)}, u32[]{:S(2)}) copy-start(f32[96,768]{1,0:T(8,128)} %param.13) | copy-start | bytes 884740
  76.1 11.7 %copy-start.3 = (bf16[128,3072]{1,0:T(8,128)(2,1)}, bf16[128,3072]{1,0:T(8,128)(2,1)S(1)}, u32[]{:S(2)}) copy-start(bf16[128,3072]{1,0:T(8,128)(2,1)S(1)} %collective-permute-done.8.refs_1_.refs_5_) | copy-start | bytes 2359300
  76.1 11.7 %collective-permute-start.13 = (bf16[128,3072]{1,0:T(8,128)(2,1)S(1)}, bf16[128,3072]{1,0:T(8,128)(2,1)}, u32[]{:S(2)}, u32[]{:S(2)}) collective-permute-start(bf16[128,3072]{1,0:T(8,128)(2,1)S(1)} %collective-permute-done.8.refs_1_.refs_5_), channel_id=1, source_target_pairs={{0,1},{8,11},{1,2},{9,8},{2,3},{10,9},{3,0},{11,10},{4,5},{12,15},... | collective-permute-start | bytes 2359304 | tf_op jit(solution)/shard_map/acts_zfar/ppermute | solution.py:335
  79.9 7.9 %copy-start.4 = (bf16[128,3072]{1,0:T(8,128)(2,1)}, bf16[128,3072]{1,0:T(8,128)(2,1)S(1)}, u32[]{:S(2)}) copy-start(bf16[128,3072]{1,0:T(8,128)(2,1)S(1)} %collective-permute-done.9.refs_2_.refs_6_) | copy-start | bytes 2359300
  81.0 14.3 %collective-permute-start.20 = (bf16[1,96,768]{2,1,0:T(8,128)(2,1)S(1)}, bf16[1,96,768]{2,1,0:T(8,128)(2,1)S(1)}, u32[]{:S(2)}, u32[]{:S(2)}) collective-permute-start(bf16[1,96,768]{2,1,0:T(8,128)(2,1)S(1)} %get-tuple-element.69), channel_id=1, source_target_pairs={{0,192},{64,0},{128,64},{192,128},{1,193},{65,1},{129,65},{193,129... | collective-permute-start | bytes 442376 | tf_op jit(solution)/shard_map/new_z3/ppermute | solution.py:318
  82.8 14.6 %collective-permute-start.19 = (bf16[1,96,768]{2,1,0:T(8,128)(2,1)S(1)}, bf16[1,96,768]{2,1,0:T(8,128)(2,1)S(1)}, u32[]{:S(2)}, u32[]{:S(2)}) collective-permute-start(bf16[1,96,768]{2,1,0:T(8,128)(2,1)S(1)} %get-tuple-element.69), channel_id=1, source_target_pairs={{0,128},{64,192},{128,0},{192,64},{1,129},{65,193},{129,1},{193,65... | collective-permute-start | bytes 442376 | tf_op jit(solution)/shard_map/new_z2/ppermute | solution.py:318
  85.8 11.7 %collective-permute-start.18 = (bf16[1,96,768]{2,1,0:T(8,128)(2,1)S(1)}, bf16[1,96,768]{2,1,0:T(8,128)(2,1)S(1)}, u32[]{:S(2)}, u32[]{:S(2)}) collective-permute-start(bf16[1,96,768]{2,1,0:T(8,128)(2,1)S(1)} %get-tuple-element.69), channel_id=1, source_target_pairs={{0,64},{64,128},{128,192},{192,0},{1,65},{65,129},{129,193},{193,1... | collective-permute-start | bytes 442376 | tf_op jit(solution)/shard_map/new_z1/ppermute | solution.py:318
  97.5 24.8 %copy-start.2 = (bf16[4,96,768]{2,1,0:T(8,128)(2,1)}, bf16[4,96,768]{2,1,0:T(8,128)(2,1)S(1)}, u32[]{:S(2)}) copy-start(bf16[4,96,768]{2,1,0:T(8,128)(2,1)S(1)} %pad_maximum_fusion.refs_0_) | copy-start | bytes 1769476
  97.5 19.6 %collective-permute-start.24 = (bf16[4,96,768]{2,1,0:T(8,128)(2,1)S(1)}, bf16[4,96,768]{2,1,0:T(8,128)(2,1)S(1)}, u32[]{:S(2)}, u32[]{:S(2)}) collective-permute-start(bf16[4,96,768]{2,1,0:T(8,128)(2,1)S(1)} %pad_maximum_fusion.refs_0_), channel_id=1, source_target_pairs={{0,48},{8,24},{16,0},{24,40},{32,16},{40,56},{48,32},{56,8},{1,49}... | collective-permute-start | bytes 1769480 | tf_op jit(solution)/shard_map/new_back/ppermute | solution.py:335
  97.9 19.2 %collective-permute-start.22 = (bf16[4,96,768]{2,1,0:T(8,128)(2,1)S(1)}, bf16[4,96,768]{2,1,0:T(8,128)(2,1)S(1)}, u32[]{:S(2)}, u32[]{:S(2)}) collective-permute-start(bf16[4,96,768]{2,1,0:T(8,128)(2,1)S(1)} %pad_maximum_fusion.refs_0_), channel_id=1, source_target_pairs={{0,16},{8,56},{16,32},{24,8},{32,48},{40,24},{48,0},{56,40},{1,17}... | collective-permute-start | bytes 1769480 | tf_op jit(solution)/shard_map/new_near/ppermute | solution.py:335
  111.0 3.1 %collective-permute-start.16 = (f32[24,128]{1,0:T(8,128)}, f32[24,128]{1,0:T(8,128)S(1)}, u32[]{:S(2)}, u32[]{:S(2)}) collective-permute-start(f32[24,128]{1,0:T(8,128)} %bitcast.68), channel_id=1, source_target_pairs={{0,3},{1,0},{2,1},{3,2},{4,7},{5,4},{6,5},{7,6},{8,11},{9,8},{10,9... | collective-permute-start | bytes 36872 | tf_op jit(solution)/shard_map/row_y/ppermute | solution.py:318
  112.2 4.3 %collective-permute-start.15 = (f32[24,128]{1,0:T(8,128)}, f32[24,128]{1,0:T(8,128)S(1)}, u32[]{:S(2)}, u32[]{:S(2)}) collective-permute-start(f32[24,128]{1,0:T(8,128)} %bitcast.69), channel_id=1, source_target_pairs={{0,2},{1,3},{2,0},{3,1},{4,6},{5,7},{6,4},{7,5},{8,10},{9,11},{10,... | collective-permute-start | bytes 36872 | tf_op jit(solution)/shard_map/row_y/ppermute | solution.py:318
  112.2 4.3 %collective-permute-start.14 = (f32[24,128]{1,0:T(8,128)}, f32[24,128]{1,0:T(8,128)S(1)}, u32[]{:S(2)}, u32[]{:S(2)}) collective-permute-start(f32[24,128]{1,0:T(8,128)} %bitcast.70), channel_id=1, source_target_pairs={{0,1},{1,2},{2,3},{3,0},{4,5},{5,6},{6,7},{7,4},{8,9},{9,10},{10,1... | collective-permute-start | bytes 36872 | tf_op jit(solution)/shard_map/row_y/ppermute | solution.py:318
  117.1 16.6 %copy-start.12 = (f32[24,128]{1,0:T(8,128)}, f32[24,128]{1,0:T(8,128)S(1)}, u32[]{:S(2)}) copy-start(f32[24,128]{1,0:T(8,128)S(1)} %add_add_fusion.row_a) | copy-start | bytes 36868
  117.2 16.6 %copy-start.5 = (bf16[4,96,768]{2,1,0:T(8,128)(2,1)}, bf16[4,96,768]{2,1,0:T(8,128)(2,1)S(1)}, u32[]{:S(2)}) copy-start(bf16[4,96,768]{2,1,0:T(8,128)(2,1)S(1)} %collective-permute-done.24.refs_4_) | copy-start | bytes 1769476
  117.2 16.6 %copy-start.6 = (bf16[4,96,768]{2,1,0:T(8,128)(2,1)}, bf16[4,96,768]{2,1,0:T(8,128)(2,1)S(1)}, u32[]{:S(2)}) copy-start(bf16[4,96,768]{2,1,0:T(8,128)(2,1)S(1)} %collective-permute-done.22.refs_2_) | copy-start | bytes 1769476
  117.2 9.9 %collective-permute-start.26 = (bf16[4,96,768]{2,1,0:T(8,128)(2,1)S(1)}, bf16[4,96,768]{2,1,0:T(8,128)(2,1)S(1)}, u32[]{:S(2)}, u32[]{:S(2)}) collective-permute-start(bf16[4,96,768]{2,1,0:T(8,128)(2,1)S(1)} %collective-permute-done.22.refs_2_), channel_id=1, source_target_pairs={{0,16},{8,56},{16,32},{24,8},{32,48},{40,24},{48,0},{56,40},{1,17}... | collective-permute-start | bytes 1769480 | tf_op jit(solution)/shard_map/new_far/ppermute | solution.py:335
  117.4 9.7 %collective-permute-start.17 = (f32[24,128]{1,0:T(8,128)S(1)}, f32[24,128]{1,0:T(8,128)S(1)}, u32[]{:S(2)}, u32[]{:S(2)}) collective-permute-start(f32[24,128]{1,0:T(8,128)S(1)} %add_add_fusion.row_a), channel_id=1, source_target_pairs={{0,4},{4,0},{1,5},{5,1},{2,6},{6,2},{3,7},{7,3},{8,12},{12,8},{9,1... | collective-permute-start | bytes 36872 | tf_op jit(solution)/shard_map/row_z/ppermute | solution.py:318
  122.3 10.3 %collective-permute-start.21 = (bf16[4,96,768]{2,1,0:T(8,128)(2,1)S(1)}, bf16[4,96,768]{2,1,0:T(8,128)(2,1)S(1)}, u32[]{:S(2)}, u32[]{:S(2)}) collective-permute-start(bf16[4,96,768]{2,1,0:T(8,128)(2,1)S(1)} %pad_maximum_fusion.refs_0_), channel_id=1, source_target_pairs={{0,8},{8,0},{1,9},{9,1},{2,10},{10,2},{3,11},{11,3},{4,12},{12,4},... | collective-permute-start | bytes 1769480 | tf_op jit(solution)/shard_map/new_core/ppermute | solution.py:318
  126.6 6.0 %collective-permute-start.25 = (bf16[4,96,768]{2,1,0:T(8,128)(2,1)S(1)}, bf16[4,96,768]{2,1,0:T(8,128)(2,1)S(1)}, u32[]{:S(2)}, u32[]{:S(2)}) collective-permute-start(bf16[4,96,768]{2,1,0:T(8,128)(2,1)S(1)} %collective-permute-done.24.refs_4_), channel_id=1, source_target_pairs={{0,8},{8,0},{1,9},{9,1},{2,10},{10,2},{3,11},{11,3},{4,12},{12,4},... | collective-permute-start | bytes 1769480 | tf_op jit(solution)/shard_map/new_core/ppermute | solution.py:318
  126.6 6.0 %collective-permute-start.23 = (bf16[4,96,768]{2,1,0:T(8,128)(2,1)S(1)}, bf16[4,96,768]{2,1,0:T(8,128)(2,1)}, u32[]{:S(2)}, u32[]{:S(2)}) collective-permute-start(bf16[4,96,768]{2,1,0:T(8,128)(2,1)S(1)} %collective-permute-done.22.refs_2_), channel_id=1, source_target_pairs={{0,8},{8,0},{1,9},{9,1},{2,10},{10,2},{3,11},{11,3},{4,12},{12,4},... | collective-permute-start | bytes 1769480 | tf_op jit(solution)/shard_map/new_core/ppermute | solution.py:318
  127.1 0.6 copy-start.13
  127.7 6.0 %copy-start.7 = (bf16[4,96,768]{2,1,0:T(8,128)(2,1)}, bf16[4,96,768]{2,1,0:T(8,128)(2,1)S(1)}, u32[]{:S(2)}) copy-start(bf16[4,96,768]{2,1,0:T(8,128)(2,1)S(1)} %collective-permute-done.26.refs_6_) | copy-start | bytes 1769476
  127.7 6.0 %collective-permute-start.27 = (bf16[4,96,768]{2,1,0:T(8,128)(2,1)S(1)}, bf16[4,96,768]{2,1,0:T(8,128)(2,1)}, u32[]{:S(2)}, u32[]{:S(2)}) collective-permute-start(bf16[4,96,768]{2,1,0:T(8,128)(2,1)S(1)} %collective-permute-done.26.refs_6_), channel_id=1, source_target_pairs={{0,8},{8,0},{1,9},{9,1},{2,10},{10,2},{3,11},{11,3},{4,12},{12,4},... | collective-permute-start | bytes 1769480 | tf_op jit(solution)/shard_map/new_core/ppermute | solution.py:318
  132.6 1.1 copy-start.8
  132.6 1.1 copy-start.9
where the time goes:
time: 145 us; the launch traced here: 144 us
  starting transfers between devices  64.9 us (45%)
  Pallas kernels  39.6 us (27%)
  waiting for transfers between devices  27 us (19%)
  local copies, waits for them, and re-layouts  6.94 us (5%)
  other arithmetic  4.17 us (3%)
    ppermute x17, starting transfers between devices, send(): return lax.ppermute(block, axis, ring(mesh_size[axis], k))  48.4 us
    ppermute x17, waiting for transfers between devices, send(): return lax.ppermute(block, axis, ring(mesh_size[axis], k))  25.5 us
    ppermute x11, starting transfers between devices, turn(): return lax.ppermute(block, axes, pairs)  16.4 us
    pallas_call x2, Pallas kernels, resid_call(): pl.pallas_call(functools.partial(resid_kernel, scale, heights), grid_spec...  15.1 us
    pallas_call x1, Pallas kernels, grad_call(): pl.pallas_call(functools.partial(grad_kernel, scale, len(blocks), len(res...  10.7 us
    pallas_call x1, Pallas kernels, merge_call(): pl.pallas_call(functools.partial(merge_kernel, pieces), in_specs=[pl.Bloc...  9.62 us
    squeeze x1, local copies, waits for them, and re-layouts, body(): theirs = lax.dynamic_index_in_dim(grid, 1 - c, 2, keepdims=False)  3.23 us
    unnamed x28, local copies, waits for them, and re-layouts  2.98 us
  transfers between devices with their start and end apart: 28, of which 9 were waited for; matrix products, arithmetic and copies ran while one was open for 3% of the time, Pallas kernels for 21%

commit v1 on v0

--- a/solution.py
+++ b/solution.py
@@ -63,24 +63,25 @@
     )(index, *([grid] * n), *([pair] * n))
 
 
-def corner_kernel(in_ref, out_ref):
+def corner_kernel(in_ref, waited_ref, out_ref):
     out_ref[...] = in_ref[...]
 
 
-def corner(array):
+def corner(array, waited):
     block = pl.BlockSpec((16, 128), lambda i: (0, 0))
     return pl.pallas_call(
         corner_kernel,
         grid=(1,),
-        in_specs=[block],
+        in_specs=[block, pl.BlockSpec(memory_space=pl.ANY)],
         out_specs=block,
         out_shape=jax.ShapeDtypeStruct((16, 128), array.dtype),
         compiler_params=pltpu.CompilerParams(vmem_limit_bytes=SMALL_LIMIT),
         name="corner",
-    )(array)
-
-
-def total_kernel(index_ref, here, near, back, far, corner_ref, a_ref, b_ref, c_ref, own_ref):
+    )(array, waited)
+
+
+def total_kernel(index_ref, here, near, back, far, *refs):
+    a_ref, b_ref, c_ref, own_ref = refs[-4:]
     step = pl.program_id(0)
     total = here[0].astype(jnp.float32)
     for array in (near, back, far):
@@ -103,13 +104,13 @@
         grid_spec=pltpu.PrefetchScalarGridSpec(
             num_scalar_prefetch=1,
             grid=(nz,),
-            in_specs=[block] * 4 + [pl.BlockSpec(memory_space=pl.ANY)],
+            in_specs=[block] * 4 + [pl.BlockSpec(memory_space=pl.ANY)] * len(waited),
             out_specs=[out] * 4,
         ),
         out_shape=[half] * 3 + [jax.ShapeDtypeStruct((rows, width), jnp.float32)],
         compiler_params=pltpu.CompilerParams(vmem_limit_bytes=SMALL_LIMIT),
         name="total",
-    )(order, *arrays, waited)
+    )(order, *arrays, *waited)
 
 
 def resid_kernel(scale, heights, index_ref, w_ref, *refs):
@@ -176,7 +177,7 @@
 
 def grad_call(blocks, resids, scale, part, parts, partial=None):
     rows = sum(b.shape[0] for b in blocks)
-    hf, width, step = blocks[0].shape[1], resids[0].shape[1], 512
+    hf, width, step = blocks[0].shape[1], resids[0].shape[1], 1024
     steps = hf // step // parts
     base = part * steps
     given, given_specs, aliases = [], [], {}
@@ -348,28 +349,22 @@
     got_near = turn(ahead, "x", 1, "sum_near")
     got_back = turn(behind, "x", -1, "sum_back")
     got_far = send(across, "x", 2, "sum_far")
-    back = turn(after(activations, got_far), "y", -1, "acts_back")
-    z_order = (2, 1, 3, 0)
-    *z_sent, share = total_call(
-        (here, got_near, got_back, got_far),
-        corner(zown),
-        jnp.stack([(zl + k) % NZ for k in z_order]).astype(jnp.int32),
-    )
-    z_sent = [after(p, far, back) for p in z_sent]
-    z_got = [send(p, "zl", k, "sum_z%d" % k) for p, k in zip(z_sent, z_order)]
-    znear = turn(after(zown, *z_sent), "y", 1, "acts_znear")
-    zback = turn(after(zown, *z_sent), "y", -1, "acts_zback")
+    back = turn(after(activations, far), "y", -1, "acts_back")
     def goal(dz, dy):
         return (zh + dz) % NH * NY + (y + dy + NY) % NY
 
     parts = [
         (
-            [activations, near, back, far],
-            [goal(0, 0), goal(0, -side), goal(0, side), goal(0, 2)],
+            [activations, near],
+            [goal(0, 0), goal(0, -side)],
         ),
         (
-            [zown, znear, zback],
-            [goal(1, 0), goal(1, -side), goal(1, side), goal(1, 2)],
+            [far],
+            [goal(0, 2), goal(1, 0), goal(1, -side), goal(1, side)],
+        ),
+        (
+            [back],
+            [goal(0, side), goal(1, 2)],
         ),
     ]
     def resid_of(g, *wait):
@@ -377,12 +372,23 @@
         index = after(jnp.stack(goals).astype(jnp.int32), *wait)
         return resid_call(held, weight, targets, index, inv_root)
 
-    resids = [resid_of(0, *z_sent)]
-    zfar = turn(after(znear, resids[0], *z_got), "y", 1, "acts_zfar")
-    parts[1][0].append(zfar)
+    resids = [resid_of(0)]
+    z_order = (2, 1, 3, 0)
+    *z_sent, share = total_call(
+        (here, got_near, got_back, got_far),
+        (corner(zown, resids[0]),),
+        jnp.stack([(zl + k) % NZ for k in z_order]).astype(jnp.int32),
+    )
+    z_sent = [after(p, far) for p in z_sent]
+    z_got = [send(p, "zl", k, "sum_z%d" % k) for p, k in zip(z_sent, z_order)]
+    znear = turn(after(zown, *z_sent), "y", 1, "acts_znear")
+    zback = turn(after(zown, *z_sent), "y", -1, "acts_zback")
+    zfar = turn(after(znear, *z_got), "y", 1, "acts_zfar")
     for got in z_got:
         share = share + got.astype(jnp.float32)
-    share = after(share, znear, zback, resids[0])
+    parts[1][0].extend((zown, znear, zback))
+    parts[2][0].append(zfar)
+    share = after(share, znear)
 
     outer_grad = anchor - share / (NZ * NX * NC)
     momentum_next = outer_momentum * momentum + outer_grad
@@ -390,8 +396,8 @@
     half = anchor_next.astype(jnp.bfloat16)[None]
 
     over_z = [send(half, "zl", k, "new_z%d" % k) for k in (1, 2, 3)]
-    resids.append(resid_of(1, half))
-    over_z = [after(o, *resids) for o in over_z]
+    resids += [resid_of(1, half), resid_of(2, half)]
+    over_z = [after(o, *resids[:2]) for o in over_z]
     held = jnp.concatenate([half] + over_z)
     new_near = turn(held, "x", 1, "new_near")
     new_back = turn(held, "x", -1, "new_back")
@@ -404,7 +410,7 @@
         row_a = row_a + send(row_sum, "y", k, "row_y")
     row_b = send(row_a, "zh", 1, "row_z")
 
-    new_far = turn(after(new_near, new_back, row_a), "x", 1, "new_far")
+    new_far = turn(after(new_near, new_back, row_sum), "x", 1, "new_far")
     sources, pieces, places = [], [], []
     late = ((held, 0), (new_near, -side), (new_back, side), (new_far, 2))
     for i, (block, origin) in enumerate(late):

time: 145 us -> 138 us (0.952)
  starting transfers between devices: 64.9 us -> 51.1 us
  Pallas kernels: 39.6 us -> 42.8 us
  waiting for transfers between devices: 27 us -> 29.7 us
  local copies, waits for them, and re-layouts: 6.94 us -> 9.09 us
    ppermute x17, starting transfers between devices: 48.4 us -> 35.5 us  [send(): return lax.ppermute(block, axis, ring(mesh_size[axis], k))]
    pallas_call x2 -> x3, Pallas kernels: 15.1 us -> 19.5 us  [resid_call(): pl.pallas_call(functools.partial(resid_kernel, scale, heights), grid_spec...]
    unnamed x28 -> x32, local copies, waits for them, and re-layouts: 2.98 us -> 5.17 us
  transfers between devices with their start and end apart: 28 -> 28, of which waited for: 9 -> 9; matrix products, arithmetic and copies ran while one was open for 3% -> 3% of each run, Pallas kernels for 21% -> 24%
where the time goes in v1:
time: 138 us; the launch traced here: 137 us
  starting transfers between devices  51.1 us (37%)
  Pallas kernels  42.8 us (31%)
  waiting for transfers between devices  29.7 us (22%)
  local copies, waits for them, and re-layouts  9.09 us (7%)
  other arithmetic  3.66 us (3%)
    ppermute x17, starting transfers between devices, send(): return lax.ppermute(block, axis, ring(mesh_size[axis], k))  35.5 us
    ppermute x17, waiting for transfers between devices, send(): return lax.ppermute(block, axis, ring(mesh_size[axis], k))  26.8 us
    pallas_call x3, Pallas kernels, resid_call(): pl.pallas_call(functools.partial(resid_kernel, scale, heights), grid_spec...  19.5 us
    ppermute x11, starting transfers between devices, turn(): return lax.ppermute(block, axes, pairs)  15.5 us
    pallas_call x1, Pallas kernels, grad_call(): pl.pallas_call(functools.partial(grad_kernel, scale, len(blocks), len(res...  10.2 us
    pallas_call x1, Pallas kernels, merge_call(): pl.pallas_call(functools.partial(merge_kernel, pieces), in_specs=[pl.Bloc...  9.62 us
    unnamed x32, local copies, waits for them, and re-layouts  5.17 us
    squeeze x1, local copies, waits for them, and re-layouts, body(): theirs = lax.dynamic_index_in_dim(grid, 1 - c, 2, keepdims=False)  3.23 us
  transfers between devices with their start and end apart: 28, of which 9 were waited for; matrix products, arithmetic and copies ran while one was open for 3% of the time, Pallas kernels for 24%

profile of v1, /device:TPU:1, one launch (start us, length us, event | category | flops | bytes accessed | tf_op | source)
XLA Modules:
  0.0 137.3 jit_solution(17206923388543622687)
XLA Ops:
  0.6 3.2 %dynamic-slice_bitcast_fusion = bf16[4,4,96,768]{3,2,1,0:T(8,128)(2,1)} fusion(bf16[4,4,2,96,768]{4,3,2,1,0:T(8,128)(2,1)} %bitcast.59, s32[]{:T(128)S(6)} %select_n.176), kind=kLoop, calls=%fused_computation | loop fusion | bytes 4718596 | tf_op jit(solution)/shard_map/jit(dynamic_index_in_dim)/squeeze | solution.py:339
  3.9 3.2 %collective-permute-start.1 = (bf16[4,4,96,768]{3,2,1,0:T(8,128)(2,1)}, bf16[4,4,96,768]{3,2,1,0:T(8,128)(2,1)S(1)}, u32[]{:S(2)}, u32[]{:S(2)}) collective-permute-start(bf16[4,4,96,768]{3,2,1,0:T(8,128)(2,1)} %dynamic-slice_bitcast_fusion), channel_id=1, source_target_pairs={{0,8},{8,0},{1,9},{9,1},{2,10},{10,2},{3,11},{11,3},{4,12},{12,4},... | collective-permute-start | bytes 7077896 | tf_op jit(solution)/shard_map/sum_core/ppermute | solution.py:319
  7.1 1.0 collective-permute-start
  8.1 6.9 %collective-permute-start.3 = (bf16[128,3072]{1,0:T(8,128)(2,1)}, bf16[128,3072]{1,0:T(8,128)(2,1)S(1)}, u32[]{:S(2)}, u32[]{:S(2)}) collective-permute-start(bf16[128,3072]{1,0:T(8,128)(2,1)} %refs_0_.3), channel_id=1, source_target_pairs={{0,4},{4,0},{1,5},{5,1},{2,6},{6,2},{3,7},{7,3},{8,12},{12,8},{9,1... | collective-permute-start | bytes 2359304 | tf_op jit(solution)/shard_map/acts_zown/ppermute | solution.py:319
  15.1 2.3 %copy-done = bf16[1,3072,768]{2,1,0:T(8,128)(2,1)S(1)} copy-done((bf16[1,3072,768]{2,1,0:T(8,128)(2,1)S(1)}, bf16[1,3072,768]{2,1,0:T(8,128)(2,1)}, u32[]{:S(2)}) %copy-start) | copy-done | bytes 4718616
  17.4 2.4 %pieces.1 = (bf16[4,96,768]{2,1,0:T(8,128)(2,1)S(1)}, bf16[4,96,768]{2,1,0:T(8,128)(2,1)}, bf16[4,96,768]{2,1,0:T(8,128)(2,1)}, bf16[4,96,768]{2,1,0:T(8,128)(2,1)}) custom-call(s32[5]{0:T(128)S(1)} %stack.203.index_ref, bf16[4,4,2,96,768]{4,3,2,1,0:T(8,128)(2,1)S(1)} %bitcast.64, bf16[4,4,2,96,768]{4,3,2,1,0:T(8,128)(2,1)S(1)} %bitcast.65, ...), custom_call_target="tpu_custom_call" | custom-call | bytes 400000000 | tf_op jit(solution)/shard_map/pieces/pallas_call | solution.py:49
  19.8 0.8 copy-done.3
  21.1 1.2 collective-permute-start.5
  22.3 2.5 %collective-permute-start.6 = (bf16[4,96,768]{2,1,0:T(8,128)(2,1)}, bf16[4,96,768]{2,1,0:T(8,128)(2,1)S(1)}, u32[]{:S(2)}, u32[]{:S(2)}) collective-permute-start(bf16[4,96,768]{2,1,0:T(8,128)(2,1)} %get-tuple-element.41), channel_id=1, source_target_pairs={{0,32},{16,48},{32,0},{48,16},{1,33},{17,49},{33,1},{49,17},{2,34}... | collective-permute-start | bytes 1769480 | tf_op jit(solution)/shard_map/sum_far/ppermute | solution.py:319
  24.8 1.2 collective-permute-start.4
  25.9 0.6 pad_add_fusion.1.index_ref
  26.6 6.1 %resid.3.waited_ref.refs_8_ = bf16[256,768]{1,0:T(8,128)(2,1)} custom-call(s32[2]{0:T(128)} %pad_add_fusion.1.index_ref, bf16[3072,768]{1,0:T(8,128)(2,1)} %bitcast.60, bf16[128,3072]{1,0:T(8,128)(2,1)} %refs_0_.3, bf16[128,3072]{1,0:T(8,128)(2,1)} %collective-permute-done.refs_1_, bf16[1024,768]{1,0:T(8,128)(2,1)} %refs_3_.3, bf16[1024,768]{1,0:T(8,128)(2,1)} %refs_3_.3), custom_call_target="tpu_custom_call" | custom-call | flops 75497472 | bytes 442368 | tf_op jit(solution)/shard_map/resid/pallas_call | solution.py:134
  32.7 15.8 %collective-permute-done.3.in_ref.refs_1_.refs_3_ = bf16[128,3072]{1,0:T(8,128)(2,1)S(1)} collective-permute-done((bf16[128,3072]{1,0:T(8,128)(2,1)}, bf16[128,3072]{1,0:T(8,128)(2,1)S(1)}, u32[]{:S(2)}, u32[]{:S(2)}) %collective-permute-start.3) | collective-permute-done | bytes 786464 | tf_op jit(solution)/shard_map/acts_zown/ppermute | solution.py:319
  48.5 1.0 copy-done.2
  49.6 0.7 collective-permute-done.4.near
  50.3 1.1 total.1
  51.5 1.5 %collective-permute-start.8 = (bf16[128,3072]{1,0:T(8,128)(2,1)S(1)}, bf16[128,3072]{1,0:T(8,128)(2,1)S(1)}, u32[]{:S(2)}, u32[]{:S(2)}) collective-permute-start(bf16[128,3072]{1,0:T(8,128)(2,1)S(1)} %collective-permute-done.3.in_ref.refs_1_.refs_3_), channel_id=1, source_target_pairs={{0,3},{8,9},{1,0},{9,10},{2,1},{10,11},{3,2},{11,8},{4,7},{12,13},... | collective-permute-start | bytes 2359304 | tf_op jit(solution)/shard_map/acts_zback/ppermute | solution.py:336
  52.9 2.0 %collective-permute-start.10 = (bf16[96,768]{1,0:T(8,128)(2,1)S(1)}, bf16[96,768]{1,0:T(8,128)(2,1)S(1)}, u32[]{:S(2)}, u32[]{:S(2)}) collective-permute-start(bf16[96,768]{1,0:T(8,128)(2,1)S(1)} %get-tuple-element.43), channel_id=1, source_target_pairs={{0,128},{64,192},{128,0},{192,64},{1,129},{65,193},{129,1},{193,65... | collective-permute-start | bytes 442376 | tf_op jit(solution)/shard_map/sum_z2/ppermute | solution.py:319
  55.0 2.0 %collective-permute-start.11 = (bf16[96,768]{1,0:T(8,128)(2,1)S(1)}, bf16[96,768]{1,0:T(8,128)(2,1)S(1)}, u32[]{:S(2)}, u32[]{:S(2)}) collective-permute-start(bf16[96,768]{1,0:T(8,128)(2,1)S(1)} %get-tuple-element.45), channel_id=1, source_target_pairs={{0,64},{64,128},{128,192},{192,0},{1,65},{65,129},{129,193},{193,1... | collective-permute-start | bytes 442376 | tf_op jit(solution)/shard_map/sum_z1/ppermute | solution.py:319
  56.9 1.3 collective-permute-start.12
  58.2 3.7 %collective-permute-done.10 = bf16[96,768]{1,0:T(8,128)(2,1)S(1)} collective-permute-done((bf16[96,768]{1,0:T(8,128)(2,1)S(1)}, bf16[96,768]{1,0:T(8,128)(2,1)S(1)}, u32[]{:S(2)}, u32[]{:S(2)}) %collective-permute-start.10) | collective-permute-done | bytes 147488 | tf_op jit(solution)/shard_map/sum_z2/ppermute | solution.py:319
  61.9 4.5 %collective-permute-start.9 = (bf16[128,3072]{1,0:T(8,128)(2,1)}, bf16[128,3072]{1,0:T(8,128)(2,1)}, u32[]{:S(2)}, u32[]{:S(2)}) collective-permute-start(bf16[128,3072]{1,0:T(8,128)(2,1)} %refs_0_.3), channel_id=1, source_target_pairs={{0,3},{8,9},{1,0},{9,10},{2,1},{10,11},{3,2},{11,8},{4,7},{12,13},... | collective-permute-start | bytes 2359304 | tf_op jit(solution)/shard_map/acts_back/ppermute | solution.py:336
  66.5 2.1 %collective-permute-done.7.refs_2_.refs_4_ = bf16[128,3072]{1,0:T(8,128)(2,1)S(1)} collective-permute-done((bf16[128,3072]{1,0:T(8,128)(2,1)S(1)}, bf16[128,3072]{1,0:T(8,128)(2,1)S(1)}, u32[]{:S(2)}, u32[]{:S(2)}) %collective-permute-start.7) | collective-permute-done | bytes 786464 | tf_op jit(solution)/shard_map/acts_znear/ppermute | solution.py:336
  68.7 1.0 convert_bitcast_fusion
  69.7 4.7 %collective-permute-start.20 = (bf16[1,96,768]{2,1,0:T(8,128)(2,1)S(1)}, bf16[1,96,768]{2,1,0:T(8,128)(2,1)S(1)}, u32[]{:S(2)}, u32[]{:S(2)}) collective-permute-start(bf16[1,96,768]{2,1,0:T(8,128)(2,1)S(1)} %get-tuple-element.69), channel_id=1, source_target_pairs={{0,192},{64,0},{128,64},{192,128},{1,193},{65,1},{129,65},{193,129... | collective-permute-start | bytes 442376 | tf_op jit(solution)/shard_map/new_z3/ppermute | solution.py:319
  74.4 1.0 copy-done.7
  75.4 1.5 %collective-permute-start.18 = (bf16[1,96,768]{2,1,0:T(8,128)(2,1)S(1)}, bf16[1,96,768]{2,1,0:T(8,128)(2,1)S(1)}, u32[]{:S(2)}, u32[]{:S(2)}) collective-permute-start(bf16[1,96,768]{2,1,0:T(8,128)(2,1)S(1)} %get-tuple-element.69), channel_id=1, source_target_pairs={{0,64},{64,128},{128,192},{192,0},{1,65},{65,129},{129,193},{193,1... | collective-permute-start | bytes 442376 | tf_op jit(solution)/shard_map/new_z1/ppermute | solution.py:319
  76.9 0.6 pad_add_fusion.2.index_ref
  77.5 7.5 %resid.4.refs_9_ = bf16[512,768]{1,0:T(8,128)(2,1)} custom-call(s32[4]{0:T(128)} %pad_add_fusion.2.index_ref, bf16[3072,768]{1,0:T(8,128)(2,1)} %bitcast.61, bf16[128,3072]{1,0:T(8,128)(2,1)} %collective-permute-done.2.refs_0_.refs_2_, bf16[128,3072]{1,0:T(8,128)(2,1)} %copy-done.1, bf16[128,3072]{1,0:T(8,128)(2,1)} %copy-done.6, ...), custom_call_target="tpu_custom_call" | custom-call | flops 150994944 | bytes 589824 | tf_op jit(solution)/shard_map/resid/pallas_call | solution.py:134
  85.0 2.1 %collective-permute-done.19 = bf16[1,96,768]{2,1,0:T(8,128)(2,1)S(1)} collective-permute-done((bf16[1,96,768]{2,1,0:T(8,128)(2,1)S(1)}, bf16[1,96,768]{2,1,0:T(8,128)(2,1)S(1)}, u32[]{:S(2)}, u32[]{:S(2)}) %collective-permute-start.19) | collective-permute-done | bytes 147488 | tf_op jit(solution)/shard_map/new_z2/ppermute | solution.py:319
  87.2 1.1 collective-permute-start.24
  88.3 3.1 %collective-permute-start.22 = (bf16[4,96,768]{2,1,0:T(8,128)(2,1)S(1)}, bf16[4,96,768]{2,1,0:T(8,128)(2,1)S(1)}, u32[]{:S(2)}, u32[]{:S(2)}) collective-permute-start(bf16[4,96,768]{2,1,0:T(8,128)(2,1)S(1)} %pad_maximum_fusion.refs_0_), channel_id=1, source_target_pairs={{0,16},{8,56},{16,32},{24,8},{32,48},{40,24},{48,0},{56,40},{1,17}... | collective-permute-start | bytes 1769480 | tf_op jit(solution)/shard_map/new_near/ppermute | solution.py:336
  91.4 0.6 pad_add_fusion.3.index_ref
  91.9 6.0 %resid.5.refs_10_ = bf16[256,768]{1,0:T(8,128)(2,1)} custom-call(s32[2]{0:T(128)} %pad_add_fusion.3.index_ref, bf16[3072,768]{1,0:T(8,128)(2,1)} %bitcast.62, bf16[128,3072]{1,0:T(8,128)(2,1)} %collective-permute-done.9.refs_0_.refs_6_, bf16[128,3072]{1,0:T(8,128)(2,1)} %collective-permute-done.13.refs_1_.refs_7_, bf16[1024,768]{1,0:T(8,128)(2,1)} %refs_3_.3, ...), custom_call_target="tpu_custom_call" | custom-call | flops 75497472 | bytes 442368 | tf_op jit(solution)/shard_map/resid/pallas_call | solution.py:134
  97.9 10.2 %grad.1 = (bf16[3072,768]{1,0:T(8,128)(2,1)}, f32[1,3072]{1,0:T(1,128)}, f32[1,768]{1,0:T(1,128)}) custom-call(bf16[128,3072]{1,0:T(8,128)(2,1)} %refs_0_.3, bf16[128,3072]{1,0:T(8,128)(2,1)} %collective-permute-done.refs_1_, bf16[128,3072]{1,0:T(8,128)(2,1)} %collective-permute-done.2.refs_0_.refs_2_, bf16[128,3072]{1,0:T(8,128)(2,1)} %copy-done.1, ...), custom_call_target="tpu_custom_call" | custom-call | flops 4831838208 | bytes 12582912 | tf_op jit(solution)/shard_map/grad/pallas_call | solution.py:191
  108.1 1.5 %collective-permute-start.26 = (bf16[4,96,768]{2,1,0:T(8,128)(2,1)S(1)}, bf16[4,96,768]{2,1,0:T(8,128)(2,1)S(1)}, u32[]{:S(2)}, u32[]{:S(2)}) collective-permute-start(bf16[4,96,768]{2,1,0:T(8,128)(2,1)S(1)} %collective-permute-done.22.refs_2_), channel_id=1, source_target_pairs={{0,16},{8,56},{16,32},{24,8},{32,48},{40,24},{48,0},{56,40},{1,17}... | collective-permute-start | bytes 1769480 | tf_op jit(solution)/shard_map/new_far/ppermute | solution.py:336
  109.6 0.6 collective-permute-start.15
  110.2 0.9 collective-permute-start.14
  111.0 1.3 collective-permute-done.16
  112.3 1.5 %collective-permute-done.15 = f32[24,128]{1,0:T(8,128)S(1)} collective-permute-done((f32[24,128]{1,0:T(8,128)}, f32[24,128]{1,0:T(8,128)S(1)}, u32[]{:S(2)}, u32[]{:S(2)}) %collective-permute-start.15) | collective-permute-done | bytes 12320 | tf_op jit(solution)/shard_map/row_y/ppermute | solution.py:319
  113.9 1.2 collective-permute-done.14
  115.0 0.7 add_add_fusion.row_a
  115.8 5.4 %collective-permute-start.17 = (f32[24,128]{1,0:T(8,128)S(1)}, f32[24,128]{1,0:T(8,128)S(1)}, u32[]{:S(2)}, u32[]{:S(2)}) collective-permute-start(f32[24,128]{1,0:T(8,128)S(1)} %add_add_fusion.row_a), channel_id=1, source_target_pairs={{0,4},{4,0},{1,5},{5,1},{2,6},{6,2},{3,7},{7,3},{8,12},{12,8},{9,1... | collective-permute-start | bytes 36872 | tf_op jit(solution)/shard_map/row_z/ppermute | solution.py:319
  121.1 1.6 %collective-permute-start.21 = (bf16[4,96,768]{2,1,0:T(8,128)(2,1)S(1)}, bf16[4,96,768]{2,1,0:T(8,128)(2,1)S(1)}, u32[]{:S(2)}, u32[]{:S(2)}) collective-permute-start(bf16[4,96,768]{2,1,0:T(8,128)(2,1)S(1)} %pad_maximum_fusion.refs_0_), channel_id=1, source_target_pairs={{0,8},{8,0},{1,9},{9,1},{2,10},{10,2},{3,11},{11,3},{4,12},{12,4},... | collective-permute-start | bytes 1769480 | tf_op jit(solution)/shard_map/new_core/ppermute | solution.py:319
  123.3 2.4 %collective-permute-start.27 = (bf16[4,96,768]{2,1,0:T(8,128)(2,1)S(1)}, bf16[4,96,768]{2,1,0:T(8,128)(2,1)}, u32[]{:S(2)}, u32[]{:S(2)}) collective-permute-start(bf16[4,96,768]{2,1,0:T(8,128)(2,1)S(1)} %collective-permute-done.26.refs_6_), channel_id=1, source_target_pairs={{0,8},{8,0},{1,9},{9,1},{2,10},{10,2},{3,11},{11,3},{4,12},{12,4},... | collective-permute-start | bytes 1769480 | tf_op jit(solution)/shard_map/new_core/ppermute | solution.py:319
  125.7 0.6 stack.197.index_ref
  126.3 1.1 collective-permute-done.27.refs_7_
  127.5 9.6 %merge.1 = (bf16[3072,768]{1,0:T(8,128)(2,1)}, f32[24,128]{1,0:T(8,128)}, f32[1,768]{1,0:T(1,128)}) custom-call(s32[32]{0:T(128)} %stack.197.index_ref, f32[24,128]{1,0:T(8,128)} %bitcast.68, f32[24,128]{1,0:T(8,128)} %copy-done.14, f32[24,128]{1,0:T(8,128)} %copy-done.15, f32[1,768]{1,0:T(1,128)} %col_state.1, f32[1,768]{1,0:T(1,128)} %get-tuple-element.56.col_sum, ...), custom_call_target="tpu_custom_call" | custom-call | flops 18874368 | bytes 18874368 | tf_op jit(solution)/shard_map/merge/pallas_call | solution.py:285
  (59 shorter events, 1.5 us)
Async XLA Ops:
  3.9 11.2 %collective-permute-start.1 = (bf16[4,4,96,768]{3,2,1,0:T(8,128)(2,1)}, bf16[4,4,96,768]{3,2,1,0:T(8,128)(2,1)S(1)}, u32[]{:S(2)}, u32[]{:S(2)}) collective-permute-start(bf16[4,4,96,768]{3,2,1,0:T(8,128)(2,1)} %dynamic-slice_bitcast_fusion), channel_id=1, source_target_pairs={{0,8},{8,0},{1,9},{9,1},{2,10},{10,2},{3,11},{11,3},{4,12},{12,4},... | collective-permute-start | bytes 7077896 | tf_op jit(solution)/shard_map/sum_core/ppermute | solution.py:319
  7.1 13.5 %collective-permute-start = (bf16[128,3072]{1,0:T(8,128)(2,1)}, bf16[128,3072]{1,0:T(8,128)(2,1)}, u32[]{:S(2)}, u32[]{:S(2)}) collective-permute-start(bf16[128,3072]{1,0:T(8,128)(2,1)} %refs_0_.3), channel_id=1, source_target_pairs={{0,1},{8,11},{1,2},{9,8},{2,3},{10,9},{3,0},{11,10},{4,5},{12,15},... | collective-permute-start | bytes 2359304 | tf_op jit(solution)/shard_map/acts_near/ppermute | solution.py:336
  8.1 40.4 %collective-permute-start.3 = (bf16[128,3072]{1,0:T(8,128)(2,1)}, bf16[128,3072]{1,0:T(8,128)(2,1)S(1)}, u32[]{:S(2)}, u32[]{:S(2)}) collective-permute-start(bf16[128,3072]{1,0:T(8,128)(2,1)} %refs_0_.3), channel_id=1, source_target_pairs={{0,4},{4,0},{1,5},{5,1},{2,6},{6,2},{3,7},{7,3},{8,12},{12,8},{9,1... | collective-permute-start | bytes 2359304 | tf_op jit(solution)/shard_map/acts_zown/ppermute | solution.py:319
  15.1 2.3 %copy-start = (bf16[1,3072,768]{2,1,0:T(8,128)(2,1)S(1)}, bf16[1,3072,768]{2,1,0:T(8,128)(2,1)}, u32[]{:S(2)}) copy-start(bf16[1,3072,768]{2,1,0:T(8,128)(2,1)} %param.9) | copy-start | bytes 14155780
  19.8 0.8 copy-start.3
  20.7 30.7 %collective-permute-start.2 = (bf16[128,3072]{1,0:T(8,128)(2,1)}, bf16[128,3072]{1,0:T(8,128)(2,1)}, u32[]{:S(2)}, u32[]{:S(2)}) collective-permute-start(bf16[128,3072]{1,0:T(8,128)(2,1)} %collective-permute-done.refs_1_), channel_id=1, source_target_pairs={{0,1},{8,11},{1,2},{9,8},{2,3},{10,9},{3,0},{11,10},{4,5},{12,15},... | collective-permute-start | bytes 2359304 | tf_op jit(solution)/shard_map/acts_far/ppermute | solution.py:336
  21.1 28.4 %collective-permute-start.5 = (bf16[4,96,768]{2,1,0:T(8,128)(2,1)}, bf16[4,96,768]{2,1,0:T(8,128)(2,1)S(1)}, u32[]{:S(2)}, u32[]{:S(2)}) collective-permute-start(bf16[4,96,768]{2,1,0:T(8,128)(2,1)} %get-tuple-element.40), channel_id=1, source_target_pairs={{0,48},{8,24},{16,0},{24,40},{32,16},{40,56},{48,32},{56,8},{1,49}... | collective-permute-start | bytes 1769480 | tf_op jit(solution)/shard_map/sum_back/ppermute | solution.py:336
  22.3 27.2 %collective-permute-start.6 = (bf16[4,96,768]{2,1,0:T(8,128)(2,1)}, bf16[4,96,768]{2,1,0:T(8,128)(2,1)S(1)}, u32[]{:S(2)}, u32[]{:S(2)}) collective-permute-start(bf16[4,96,768]{2,1,0:T(8,128)(2,1)} %get-tuple-element.41), channel_id=1, source_target_pairs={{0,32},{16,48},{32,0},{48,16},{1,33},{17,49},{33,1},{49,17},{2,34}... | collective-permute-start | bytes 1769480 | tf_op jit(solution)/shard_map/sum_far/ppermute | solution.py:319
  24.8 25.5 %collective-permute-start.4 = (bf16[4,96,768]{2,1,0:T(8,128)(2,1)}, bf16[4,96,768]{2,1,0:T(8,128)(2,1)S(1)}, u32[]{:S(2)}, u32[]{:S(2)}) collective-permute-start(bf16[4,96,768]{2,1,0:T(8,128)(2,1)} %get-tuple-element.37), channel_id=1, source_target_pairs={{0,16},{8,56},{16,32},{24,8},{32,48},{40,24},{48,0},{56,40},{1,17}... | collective-permute-start | bytes 1769480 | tf_op jit(solution)/shard_map/sum_near/ppermute | solution.py:336
  26.6 23.7 %copy-start.4 = (bf16[4,96,768]{2,1,0:T(8,128)(2,1)S(1)}, bf16[4,96,768]{2,1,0:T(8,128)(2,1)}, u32[]{:S(2)}) copy-start(bf16[4,96,768]{2,1,0:T(8,128)(2,1)} %copy-done.3) | copy-start | bytes 1769476
  48.5 1.0 copy-start.2
  49.5 28.0 %copy-start.1 = (bf16[128,3072]{1,0:T(8,128)(2,1)}, bf16[128,3072]{1,0:T(8,128)(2,1)S(1)}, u32[]{:S(2)}) copy-start(bf16[128,3072]{1,0:T(8,128)(2,1)S(1)} %collective-permute-done.3.in_ref.refs_1_.refs_3_) | copy-start | bytes 2359300
  49.5 19.1 %copy-start.12 = (f32[96,768]{1,0:T(8,128)S(1)}, f32[96,768]{1,0:T(8,128)}, u32[]{:S(2)}) copy-start(f32[96,768]{1,0:T(8,128)} %param.12) | copy-start | bytes 884740
  49.5 19.2 %copy-start.13 = (f32[96,768]{1,0:T(8,128)S(1)}, f32[96,768]{1,0:T(8,128)}, u32[]{:S(2)}) copy-start(f32[96,768]{1,0:T(8,128)} %param.13) | copy-start | bytes 884740
  51.4 17.2 %collective-permute-start.7 = (bf16[128,3072]{1,0:T(8,128)(2,1)S(1)}, bf16[128,3072]{1,0:T(8,128)(2,1)S(1)}, u32[]{:S(2)}, u32[]{:S(2)}) collective-permute-start(bf16[128,3072]{1,0:T(8,128)(2,1)S(1)} %collective-permute-done.3.in_ref.refs_1_.refs_3_), channel_id=1, source_target_pairs={{0,1},{8,11},{1,2},{9,8},{2,3},{10,9},{3,0},{11,10},{4,5},{12,15},... | collective-permute-start | bytes 2359304 | tf_op jit(solution)/shard_map/acts_znear/ppermute | solution.py:336
  51.5 23.0 %collective-permute-start.8 = (bf16[128,3072]{1,0:T(8,128)(2,1)S(1)}, bf16[128,3072]{1,0:T(8,128)(2,1)S(1)}, u32[]{:S(2)}, u32[]{:S(2)}) collective-permute-start(bf16[128,3072]{1,0:T(8,128)(2,1)S(1)} %collective-permute-done.3.in_ref.refs_1_.refs_3_), channel_id=1, source_target_pairs={{0,3},{8,9},{1,0},{9,10},{2,1},{10,11},{3,2},{11,8},{4,7},{12,13},... | collective-permute-start | bytes 2359304 | tf_op jit(solution)/shard_map/acts_zback/ppermute | solution.py:336
  52.9 9.0 %collective-permute-start.10 = (bf16[96,768]{1,0:T(8,128)(2,1)S(1)}, bf16[96,768]{1,0:T(8,128)(2,1)S(1)}, u32[]{:S(2)}, u32[]{:S(2)}) collective-permute-start(bf16[96,768]{1,0:T(8,128)(2,1)S(1)} %get-tuple-element.43), channel_id=1, source_target_pairs={{0,128},{64,192},{128,0},{192,64},{1,129},{65,193},{129,1},{193,65... | collective-permute-start | bytes 442376 | tf_op jit(solution)/shard_map/sum_z2/ppermute | solution.py:319
  55.0 11.5 %collective-permute-start.11 = (bf16[96,768]{1,0:T(8,128)(2,1)S(1)}, bf16[96,768]{1,0:T(8,128)(2,1)S(1)}, u32[]{:S(2)}, u32[]{:S(2)}) collective-permute-start(bf16[96,768]{1,0:T(8,128)(2,1)S(1)} %get-tuple-element.45), channel_id=1, source_target_pairs={{0,64},{64,128},{128,192},{192,0},{1,65},{65,129},{129,193},{193,1... | collective-permute-start | bytes 442376 | tf_op jit(solution)/shard_map/sum_z1/ppermute | solution.py:319
  56.9 9.5 %collective-permute-start.12 = (bf16[96,768]{1,0:T(8,128)(2,1)S(1)}, bf16[96,768]{1,0:T(8,128)(2,1)S(1)}, u32[]{:S(2)}, u32[]{:S(2)}) collective-permute-start(bf16[96,768]{1,0:T(8,128)(2,1)S(1)} %get-tuple-element.47), channel_id=1, source_target_pairs={{0,192},{64,0},{128,64},{192,128},{1,193},{65,1},{129,65},{193,129... | collective-permute-start | bytes 442376 | tf_op jit(solution)/shard_map/sum_z3/ppermute | solution.py:319
  61.9 30.0 %collective-permute-start.9 = (bf16[128,3072]{1,0:T(8,128)(2,1)}, bf16[128,3072]{1,0:T(8,128)(2,1)}, u32[]{:S(2)}, u32[]{:S(2)}) collective-permute-start(bf16[128,3072]{1,0:T(8,128)(2,1)} %refs_0_.3), channel_id=1, source_target_pairs={{0,3},{8,9},{1,0},{9,10},{2,1},{10,11},{3,2},{11,8},{4,7},{12,13},... | collective-permute-start | bytes 2359304 | tf_op jit(solution)/shard_map/acts_back/ppermute | solution.py:336
  68.6 8.9 %copy-start.6 = (bf16[128,3072]{1,0:T(8,128)(2,1)}, bf16[128,3072]{1,0:T(8,128)(2,1)S(1)}, u32[]{:S(2)}) copy-start(bf16[128,3072]{1,0:T(8,128)(2,1)S(1)} %collective-permute-done.7.refs_2_.refs_4_) | copy-start | bytes 2359300
  68.6 23.3 %collective-permute-start.13 = (bf16[128,3072]{1,0:T(8,128)(2,1)S(1)}, bf16[128,3072]{1,0:T(8,128)(2,1)}, u32[]{:S(2)}, u32[]{:S(2)}) collective-permute-start(bf16[128,3072]{1,0:T(8,128)(2,1)S(1)} %collective-permute-done.7.refs_2_.refs_4_), channel_id=1, source_target_pairs={{0,1},{8,11},{1,2},{9,8},{2,3},{10,9},{3,0},{11,10},{4,5},{12,15},... | collective-permute-start | bytes 2359304 | tf_op jit(solution)/shard_map/acts_zfar/ppermute | solution.py:336
  69.7 15.3 %collective-permute-start.20 = (bf16[1,96,768]{2,1,0:T(8,128)(2,1)S(1)}, bf16[1,96,768]{2,1,0:T(8,128)(2,1)S(1)}, u32[]{:S(2)}, u32[]{:S(2)}) collective-permute-start(bf16[1,96,768]{2,1,0:T(8,128)(2,1)S(1)} %get-tuple-element.69), channel_id=1, source_target_pairs={{0,192},{64,0},{128,64},{192,128},{1,193},{65,1},{129,65},{193,129... | collective-permute-start | bytes 442376 | tf_op jit(solution)/shard_map/new_z3/ppermute | solution.py:319
  74.4 12.7 %collective-permute-start.19 = (bf16[1,96,768]{2,1,0:T(8,128)(2,1)S(1)}, bf16[1,96,768]{2,1,0:T(8,128)(2,1)S(1)}, u32[]{:S(2)}, u32[]{:S(2)}) collective-permute-start(bf16[1,96,768]{2,1,0:T(8,128)(2,1)S(1)} %get-tuple-element.69), channel_id=1, source_target_pairs={{0,128},{64,192},{128,0},{192,64},{1,129},{65,193},{129,1},{193,65... | collective-permute-start | bytes 442376 | tf_op jit(solution)/shard_map/new_z2/ppermute | solution.py:319
  74.4 1.0 copy-start.7
  75.4 11.7 %collective-permute-start.18 = (bf16[1,96,768]{2,1,0:T(8,128)(2,1)S(1)}, bf16[1,96,768]{2,1,0:T(8,128)(2,1)S(1)}, u32[]{:S(2)}, u32[]{:S(2)}) collective-permute-start(bf16[1,96,768]{2,1,0:T(8,128)(2,1)S(1)} %get-tuple-element.69), channel_id=1, source_target_pairs={{0,64},{64,128},{128,192},{192,0},{1,65},{65,129},{129,193},{193,1... | collective-permute-start | bytes 442376 | tf_op jit(solution)/shard_map/new_z1/ppermute | solution.py:319
  87.2 34.0 %copy-start.5 = (bf16[4,96,768]{2,1,0:T(8,128)(2,1)}, bf16[4,96,768]{2,1,0:T(8,128)(2,1)S(1)}, u32[]{:S(2)}) copy-start(bf16[4,96,768]{2,1,0:T(8,128)(2,1)S(1)} %pad_maximum_fusion.refs_0_) | copy-start | bytes 1769476
  87.2 20.9 %collective-permute-start.24 = (bf16[4,96,768]{2,1,0:T(8,128)(2,1)S(1)}, bf16[4,96,768]{2,1,0:T(8,128)(2,1)S(1)}, u32[]{:S(2)}, u32[]{:S(2)}) collective-permute-start(bf16[4,96,768]{2,1,0:T(8,128)(2,1)S(1)} %pad_maximum_fusion.refs_0_), channel_id=1, source_target_pairs={{0,48},{8,24},{16,0},{24,40},{32,16},{40,56},{48,32},{56,8},{1,49}... | collective-permute-start | bytes 1769480 | tf_op jit(solution)/shard_map/new_back/ppermute | solution.py:336
  88.3 19.8 %collective-permute-start.22 = (bf16[4,96,768]{2,1,0:T(8,128)(2,1)S(1)}, bf16[4,96,768]{2,1,0:T(8,128)(2,1)S(1)}, u32[]{:S(2)}, u32[]{:S(2)}) collective-permute-start(bf16[4,96,768]{2,1,0:T(8,128)(2,1)S(1)} %pad_maximum_fusion.refs_0_), channel_id=1, source_target_pairs={{0,16},{8,56},{16,32},{24,8},{32,48},{40,24},{48,0},{56,40},{1,17}... | collective-permute-start | bytes 1769480 | tf_op jit(solution)/shard_map/new_near/ppermute | solution.py:336
  108.1 19.4 %copy-start.8 = (bf16[4,96,768]{2,1,0:T(8,128)(2,1)}, bf16[4,96,768]{2,1,0:T(8,128)(2,1)S(1)}, u32[]{:S(2)}) copy-start(bf16[4,96,768]{2,1,0:T(8,128)(2,1)S(1)} %collective-permute-done.24.refs_4_) | copy-start | bytes 1769476
  108.1 19.4 %copy-start.9 = (bf16[4,96,768]{2,1,0:T(8,128)(2,1)}, bf16[4,96,768]{2,1,0:T(8,128)(2,1)S(1)}, u32[]{:S(2)}) copy-start(bf16[4,96,768]{2,1,0:T(8,128)(2,1)S(1)} %collective-permute-done.22.refs_2_) | copy-start | bytes 1769476
  108.1 15.2 %collective-permute-start.26 = (bf16[4,96,768]{2,1,0:T(8,128)(2,1)S(1)}, bf16[4,96,768]{2,1,0:T(8,128)(2,1)S(1)}, u32[]{:S(2)}, u32[]{:S(2)}) collective-permute-start(bf16[4,96,768]{2,1,0:T(8,128)(2,1)S(1)} %collective-permute-done.22.refs_2_), channel_id=1, source_target_pairs={{0,16},{8,56},{16,32},{24,8},{32,48},{40,24},{48,0},{56,40},{1,17}... | collective-permute-start | bytes 1769480 | tf_op jit(solution)/shard_map/new_far/ppermute | solution.py:336
  109.6 2.8 %collective-permute-start.16 = (f32[24,128]{1,0:T(8,128)}, f32[24,128]{1,0:T(8,128)S(1)}, u32[]{:S(2)}, u32[]{:S(2)}) collective-permute-start(f32[24,128]{1,0:T(8,128)} %bitcast.69), channel_id=1, source_target_pairs={{0,3},{1,0},{2,1},{3,2},{4,7},{5,4},{6,5},{7,6},{8,11},{9,8},{10,9... | collective-permute-start | bytes 36872 | tf_op jit(solution)/shard_map/row_y/ppermute | solution.py:319
  109.6 4.3 %collective-permute-start.15 = (f32[24,128]{1,0:T(8,128)}, f32[24,128]{1,0:T(8,128)S(1)}, u32[]{:S(2)}, u32[]{:S(2)}) collective-permute-start(f32[24,128]{1,0:T(8,128)} %bitcast.70), channel_id=1, source_target_pairs={{0,2},{1,3},{2,0},{3,1},{4,6},{5,7},{6,4},{7,5},{8,10},{9,11},{10,... | collective-permute-start | bytes 36872 | tf_op jit(solution)/shard_map/row_y/ppermute | solution.py:319
  110.2 4.9 %collective-permute-start.14 = (f32[24,128]{1,0:T(8,128)}, f32[24,128]{1,0:T(8,128)S(1)}, u32[]{:S(2)}, u32[]{:S(2)}) collective-permute-start(f32[24,128]{1,0:T(8,128)} %bitcast.71), channel_id=1, source_target_pairs={{0,1},{1,2},{2,3},{3,0},{4,5},{5,6},{6,7},{7,4},{8,9},{9,10},{10,1... | collective-permute-start | bytes 36872 | tf_op jit(solution)/shard_map/row_y/ppermute | solution.py:319
  115.8 11.7 %copy-start.14 = (f32[24,128]{1,0:T(8,128)}, f32[24,128]{1,0:T(8,128)S(1)}, u32[]{:S(2)}) copy-start(f32[24,128]{1,0:T(8,128)S(1)} %add_add_fusion.row_a) | copy-start | bytes 36868
  115.8 7.5 %collective-permute-start.17 = (f32[24,128]{1,0:T(8,128)S(1)}, f32[24,128]{1,0:T(8,128)S(1)}, u32[]{:S(2)}, u32[]{:S(2)}) collective-permute-start(f32[24,128]{1,0:T(8,128)S(1)} %add_add_fusion.row_a), channel_id=1, source_target_pairs={{0,4},{4,0},{1,5},{5,1},{2,6},{6,2},{3,7},{7,3},{8,12},{12,8},{9,1... | collective-permute-start | bytes 36872 | tf_op jit(solution)/shard_map/row_z/ppermute | solution.py:319
  121.1 5.2 %collective-permute-start.21 = (bf16[4,96,768]{2,1,0:T(8,128)(2,1)S(1)}, bf16[4,96,768]{2,1,0:T(8,128)(2,1)S(1)}, u32[]{:S(2)}, u32[]{:S(2)}) collective-permute-start(bf16[4,96,768]{2,1,0:T(8,128)(2,1)S(1)} %pad_maximum_fusion.refs_0_), channel_id=1, source_target_pairs={{0,8},{8,0},{1,9},{9,1},{2,10},{10,2},{3,11},{11,3},{4,12},{12,4},... | collective-permute-start | bytes 1769480 | tf_op jit(solution)/shard_map/new_core/ppermute | solution.py:319
  122.8 3.6 %collective-permute-start.23 = (bf16[4,96,768]{2,1,0:T(8,128)(2,1)S(1)}, bf16[4,96,768]{2,1,0:T(8,128)(2,1)}, u32[]{:S(2)}, u32[]{:S(2)}) collective-permute-start(bf16[4,96,768]{2,1,0:T(8,128)(2,1)S(1)} %collective-permute-done.22.refs_2_), channel_id=1, source_target_pairs={{0,8},{8,0},{1,9},{9,1},{2,10},{10,2},{3,11},{11,3},{4,12},{12,4},... | collective-permute-start | bytes 1769480 | tf_op jit(solution)/shard_map/new_core/ppermute | solution.py:319
  122.8 3.6 %collective-permute-start.25 = (bf16[4,96,768]{2,1,0:T(8,128)(2,1)S(1)}, bf16[4,96,768]{2,1,0:T(8,128)(2,1)}, u32[]{:S(2)}, u32[]{:S(2)}) collective-permute-start(bf16[4,96,768]{2,1,0:T(8,128)(2,1)S(1)} %collective-permute-done.24.refs_4_), channel_id=1, source_target_pairs={{0,8},{8,0},{1,9},{9,1},{2,10},{10,2},{3,11},{11,3},{4,12},{12,4},... | collective-permute-start | bytes 1769480 | tf_op jit(solution)/shard_map/new_core/ppermute | solution.py:319
  123.3 4.2 %copy-start.15 = (f32[24,128]{1,0:T(8,128)}, f32[24,128]{1,0:T(8,128)S(1)}, u32[]{:S(2)}) copy-start(f32[24,128]{1,0:T(8,128)S(1)} %collective-permute-done.17.row_b) | copy-start | bytes 36868
  123.3 4.2 %copy-start.10 = (bf16[4,96,768]{2,1,0:T(8,128)(2,1)}, bf16[4,96,768]{2,1,0:T(8,128)(2,1)S(1)}, u32[]{:S(2)}) copy-start(bf16[4,96,768]{2,1,0:T(8,128)(2,1)S(1)} %collective-permute-done.26.refs_6_) | copy-start | bytes 1769476
  123.3 4.2 %collective-permute-start.27 = (bf16[4,96,768]{2,1,0:T(8,128)(2,1)S(1)}, bf16[4,96,768]{2,1,0:T(8,128)(2,1)}, u32[]{:S(2)}, u32[]{:S(2)}) collective-permute-start(bf16[4,96,768]{2,1,0:T(8,128)(2,1)S(1)} %collective-permute-done.26.refs_6_), channel_id=1, source_target_pairs={{0,8},{8,0},{1,9},{9,1},{2,10},{10,2},{3,11},{11,3},{4,12},{12,4},... | collective-permute-start | bytes 1769480 | tf_op jit(solution)/shard_map/new_core/ppermute | solution.py:319
  126.3 1.2 copy-start.11

commit v2 on v1

--- a/solution.py
+++ b/solution.py
@@ -345,26 +345,28 @@
     here, ahead, behind, across = pieces_call(
         grid, pair, c, [(x + dx + NX) % NX for dx in (0, side, -side, 2)]
     )
-    far = turn(after(near, ahead), "y", 1, "acts_far")
+    back = turn(activations, "y", -1, "acts_back")
+    cut = 80
+    far0 = turn(after(near, back)[:cut], "y", 1, "acts_far0")
+    far1 = turn(after(near, far0)[cut:], "y", 1, "acts_far1")
     got_near = turn(ahead, "x", 1, "sum_near")
     got_back = turn(behind, "x", -1, "sum_back")
     got_far = send(across, "x", 2, "sum_far")
-    back = turn(after(activations, far), "y", -1, "acts_back")
     def goal(dz, dy):
         return (zh + dz) % NH * NY + (y + dy + NY) % NY
 
     parts = [
         (
-            [activations, near],
-            [goal(0, 0), goal(0, -side)],
+            [activations, near, back],
+            [goal(0, 0), goal(0, -side), goal(0, side)],
         ),
         (
-            [far],
+            [far0, far1],
             [goal(0, 2), goal(1, 0), goal(1, -side), goal(1, side)],
         ),
         (
-            [back],
-            [goal(0, side), goal(1, 2)],
+            [],
+            [goal(1, 2)],
         ),
     ]
     def resid_of(g, *wait):
@@ -379,7 +381,7 @@
         (corner(zown, resids[0]),),
         jnp.stack([(zl + k) % NZ for k in z_order]).astype(jnp.int32),
     )
-    z_sent = [after(p, far) for p in z_sent]
+    z_sent = [after(p, far0) for p in z_sent]
     z_got = [send(p, "zl", k, "sum_z%d" % k) for p, k in zip(z_sent, z_order)]
     znear = turn(after(zown, *z_sent), "y", 1, "acts_znear")
     zback = turn(after(zown, *z_sent), "y", -1, "acts_zback")

time: 138 us -> 136 us (0.986)
  starting transfers between devices: 51.1 us -> 46.4 us
  local copies, waits for them, and re-layouts: 9.09 us -> 11.2 us
  waiting for transfers between devices: 29.7 us -> 31.7 us
    ppermute x17, starting transfers between devices: 35.5 us -> 25.1 us  [send(): return lax.ppermute(block, axis, ring(mesh_size[axis], k))]
    ppermute x11 -> x12, starting transfers between devices: 15.5 us -> 21.3 us  [turn(): return lax.ppermute(block, axes, pairs)]
    slice x0 -> x2, local copies, waits for them, and re-layouts: none -> 2.83 us  [the longest x1 1.84 us: body(): far0 = turn(after(near, back)[:cut], 'y', 1, 'acts_far0')]
    ppermute x11 -> x12, waiting for transfers between devices: 2.9 us -> 4.64 us  [turn(): return lax.ppermute(block, axes, pairs)]
  transfers between devices with their start and end apart: 28 -> 29, of which waited for: 9 -> 12; matrix products, arithmetic and copies ran while one was open for 3% -> 5% of each run, Pallas kernels for 24% -> 24%
where the time goes in v2:
time: 136 us
  starting transfers between devices  46.4 us (34%)
  Pallas kernels  42.2 us (31%)
  waiting for transfers between devices  31.7 us (23%)
  local copies, waits for them, and re-layouts  11.2 us (8%)
  other arithmetic  3.07 us (2%)
    ppermute x17, waiting for transfers between devices, send(): return lax.ppermute(block, axis, ring(mesh_size[axis], k))  27 us
    ppermute x17, starting transfers between devices, send(): return lax.ppermute(block, axis, ring(mesh_size[axis], k))  25.1 us
    ppermute x12, starting transfers between devices, turn(): return lax.ppermute(block, axes, pairs)  21.3 us
    pallas_call x3, Pallas kernels, resid_call(): pl.pallas_call(functools.partial(resid_kernel, scale, heights), grid_spec...  18.8 us
    pallas_call x1, Pallas kernels, grad_call(): pl.pallas_call(functools.partial(grad_kernel, scale, len(blocks), len(res...  10.2 us
    pallas_call x1, Pallas kernels, merge_call(): pl.pallas_call(functools.partial(merge_kernel, pieces), in_specs=[pl.Bloc...  9.62 us
    ppermute x12, waiting for transfers between devices, turn(): return lax.ppermute(block, axes, pairs)  4.64 us
    unnamed x32, local copies, waits for them, and re-layouts  4.33 us
  transfers between devices with their start and end apart: 29, of which 12 were waited for; matrix products, arithmetic and copies ran while one was open for 5% of the time, Pallas kernels for 24%

profile of v2, /device:TPU:1, one launch (start us, length us, event | category | flops | bytes accessed | tf_op | source)
XLA Modules:
  0.0 135.5 jit_solution(3586871645436741825)
XLA Ops:
  0.6 3.2 %dynamic-slice_bitcast_fusion = bf16[4,4,96,768]{3,2,1,0:T(8,128)(2,1)} fusion(bf16[4,4,2,96,768]{4,3,2,1,0:T(8,128)(2,1)} %bitcast.59, s32[]{:T(128)S(6)} %select_n.177), kind=kLoop, calls=%fused_computation | loop fusion | bytes 4718596 | tf_op jit(solution)/shard_map/jit(dynamic_index_in_dim)/squeeze | solution.py:339
  3.9 3.2 %collective-permute-start.5 = (bf16[4,4,96,768]{3,2,1,0:T(8,128)(2,1)}, bf16[4,4,96,768]{3,2,1,0:T(8,128)(2,1)S(1)}, u32[]{:S(2)}, u32[]{:S(2)}) collective-permute-start(bf16[4,4,96,768]{3,2,1,0:T(8,128)(2,1)} %dynamic-slice_bitcast_fusion), channel_id=1, source_target_pairs={{0,8},{8,0},{1,9},{9,1},{2,10},{10,2},{3,11},{11,3},{4,12},{12,4},... | collective-permute-start | bytes 7077896 | tf_op jit(solution)/shard_map/sum_core/ppermute | solution.py:319
  7.1 2.7 %collective-permute-start = (bf16[128,3072]{1,0:T(8,128)(2,1)}, bf16[128,3072]{1,0:T(8,128)(2,1)}, u32[]{:S(2)}, u32[]{:S(2)}) collective-permute-start(bf16[128,3072]{1,0:T(8,128)(2,1)} %refs_0_.3), channel_id=1, source_target_pairs={{0,1},{8,11},{1,2},{9,8},{2,3},{10,9},{3,0},{11,10},{4,5},{12,15},... | collective-permute-start | bytes 2359304 | tf_op jit(solution)/shard_map/acts_near/ppermute | solution.py:336
  9.8 5.2 %collective-permute-start.4 = (bf16[128,3072]{1,0:T(8,128)(2,1)}, bf16[128,3072]{1,0:T(8,128)(2,1)S(1)}, u32[]{:S(2)}, u32[]{:S(2)}) collective-permute-start(bf16[128,3072]{1,0:T(8,128)(2,1)} %refs_0_.3), channel_id=1, source_target_pairs={{0,4},{4,0},{1,5},{5,1},{2,6},{6,2},{3,7},{7,3},{8,12},{12,8},{9,1... | collective-permute-start | bytes 2359304 | tf_op jit(solution)/shard_map/acts_zown/ppermute | solution.py:319
  15.1 2.3 %copy-done = bf16[1,3072,768]{2,1,0:T(8,128)(2,1)S(1)} copy-done((bf16[1,3072,768]{2,1,0:T(8,128)(2,1)S(1)}, bf16[1,3072,768]{2,1,0:T(8,128)(2,1)}, u32[]{:S(2)}) %copy-start) | copy-done | bytes 4718616
  17.4 2.4 %pieces.1 = (bf16[4,96,768]{2,1,0:T(8,128)(2,1)S(1)}, bf16[4,96,768]{2,1,0:T(8,128)(2,1)}, bf16[4,96,768]{2,1,0:T(8,128)(2,1)}, bf16[4,96,768]{2,1,0:T(8,128)(2,1)}) custom-call(s32[5]{0:T(128)S(1)} %stack.205.index_ref, bf16[4,4,2,96,768]{4,3,2,1,0:T(8,128)(2,1)S(1)} %bitcast.64, bf16[4,4,2,96,768]{4,3,2,1,0:T(8,128)(2,1)S(1)} %bitcast.65, ...), custom_call_target="tpu_custom_call" | custom-call | bytes 400000000 | tf_op jit(solution)/shard_map/pieces/pallas_call | solution.py:49
  19.8 0.9 copy-done.3
  20.7 2.5 %collective-permute-start.6 = (bf16[4,96,768]{2,1,0:T(8,128)(2,1)}, bf16[4,96,768]{2,1,0:T(8,128)(2,1)S(1)}, u32[]{:S(2)}, u32[]{:S(2)}) collective-permute-start(bf16[4,96,768]{2,1,0:T(8,128)(2,1)} %get-tuple-element.40), channel_id=1, source_target_pairs={{0,16},{8,56},{16,32},{24,8},{32,48},{40,24},{48,0},{56,40},{1,17}... | collective-permute-start | bytes 1769480 | tf_op jit(solution)/shard_map/sum_near/ppermute | solution.py:336
  23.2 3.2 %collective-permute-done.1.refs_2_ = bf16[128,3072]{1,0:T(8,128)(2,1)} collective-permute-done((bf16[128,3072]{1,0:T(8,128)(2,1)}, bf16[128,3072]{1,0:T(8,128)(2,1)}, u32[]{:S(2)}, u32[]{:S(2)}) %collective-permute-start.1) | collective-permute-done | bytes 786464 | tf_op jit(solution)/shard_map/acts_back/ppermute | solution.py:336
  26.6 1.8 %slice.6 = bf16[80,3072]{1,0:T(8,128)(2,1)} slice(bf16[128,3072]{1,0:T(8,128)(2,1)} %collective-permute-done.refs_1_), slice={[0:80], [0:3072]} | slice | bytes 983040 | tf_op jit(solution)/shard_map/slice | solution.py:350
  28.5 2.9 %collective-permute-start.2 = (bf16[80,3072]{1,0:T(8,128)(2,1)}, bf16[80,3072]{1,0:T(8,128)(2,1)}, u32[]{:S(2)}, u32[]{:S(2)}) collective-permute-start(bf16[80,3072]{1,0:T(8,128)(2,1)} %slice.6), channel_id=1, source_target_pairs={{0,1},{8,11},{1,2},{9,8},{2,3},{10,9},{3,0},{11,10},{4,5},{12,15},... | collective-permute-start | bytes 1474568 | tf_op jit(solution)/shard_map/acts_far0/ppermute | solution.py:336
  31.4 0.6 pad_add_fusion.1.index_ref
  32.1 6.8 %resid.3.waited_ref.refs_9_ = bf16[384,768]{1,0:T(8,128)(2,1)} custom-call(s32[3]{0:T(128)} %pad_add_fusion.1.index_ref, bf16[3072,768]{1,0:T(8,128)(2,1)} %bitcast.60, bf16[128,3072]{1,0:T(8,128)(2,1)} %refs_0_.3, bf16[128,3072]{1,0:T(8,128)(2,1)} %collective-permute-done.refs_1_, bf16[128,3072]{1,0:T(8,128)(2,1)} %collective-permute-done.1.refs_2_, ...), custom_call_target="tpu_custom_call" | custom-call | flops 113246208 | bytes 516096 | tf_op jit(solution)/shard_map/resid/pallas_call | solution.py:134
  38.9 1.1 copy-done.2
  40.0 11.3 %collective-permute-done.8.far = bf16[4,96,768]{2,1,0:T(8,128)(2,1)S(1)} collective-permute-done((bf16[4,96,768]{2,1,0:T(8,128)(2,1)}, bf16[4,96,768]{2,1,0:T(8,128)(2,1)S(1)}, u32[]{:S(2)}, u32[]{:S(2)}) %collective-permute-start.8) | collective-permute-done | bytes 589856 | tf_op jit(solution)/shard_map/sum_far/ppermute | solution.py:319
  51.3 1.1 total.1
  52.3 2.9 %collective-permute-start.9 = (bf16[128,3072]{1,0:T(8,128)(2,1)S(1)}, bf16[128,3072]{1,0:T(8,128)(2,1)S(1)}, u32[]{:S(2)}, u32[]{:S(2)}) collective-permute-start(bf16[128,3072]{1,0:T(8,128)(2,1)S(1)} %collective-permute-done.4.in_ref.refs_2_.refs_5_), channel_id=1, source_target_pairs={{0,1},{8,11},{1,2},{9,8},{2,3},{10,9},{3,0},{11,10},{4,5},{12,15},... | collective-permute-start | bytes 2359304 | tf_op jit(solution)/shard_map/acts_znear/ppermute | solution.py:336
  55.2 1.6 %collective-permute-start.13 = (bf16[96,768]{1,0:T(8,128)(2,1)S(1)}, bf16[96,768]{1,0:T(8,128)(2,1)S(1)}, u32[]{:S(2)}, u32[]{:S(2)}) collective-permute-start(bf16[96,768]{1,0:T(8,128)(2,1)S(1)} %get-tuple-element.48), channel_id=1, source_target_pairs={{0,192},{64,0},{128,64},{192,128},{1,193},{65,1},{129,65},{193,129... | collective-permute-start | bytes 442376 | tf_op jit(solution)/shard_map/sum_z3/ppermute | solution.py:319
  56.9 1.0 collective-permute-start.11
  57.9 1.0 slice.7
  58.8 0.8 collective-permute-done.13
  59.6 4.0 %collective-permute-start.3 = (bf16[48,3072]{1,0:T(8,128)(2,1)S(1)}, bf16[48,3072]{1,0:T(8,128)(2,1)S(1)}, u32[]{:S(2)}, u32[]{:S(2)}) collective-permute-start(bf16[48,3072]{1,0:T(8,128)(2,1)S(1)} %slice.7), channel_id=1, source_target_pairs={{0,1},{8,11},{1,2},{9,8},{2,3},{10,9},{3,0},{11,10},{4,5},{12,15},... | collective-permute-start | bytes 884744 | tf_op jit(solution)/shard_map/acts_far1/ppermute | solution.py:336
  63.6 0.4 collective-permute-done.12
  64.0 5.9 %collective-permute-done.11 = bf16[96,768]{1,0:T(8,128)(2,1)S(1)} collective-permute-done((bf16[96,768]{1,0:T(8,128)(2,1)S(1)}, bf16[96,768]{1,0:T(8,128)(2,1)S(1)}, u32[]{:S(2)}, u32[]{:S(2)}) %collective-permute-start.11) | collective-permute-done | bytes 147488 | tf_op jit(solution)/shard_map/sum_z2/ppermute | solution.py:319
  69.9 1.2 collective-permute-done.9.refs_3_.refs_6_
  71.1 3.5 %collective-permute-start.14 = (bf16[128,3072]{1,0:T(8,128)(2,1)S(1)}, bf16[128,3072]{1,0:T(8,128)(2,1)}, u32[]{:S(2)}, u32[]{:S(2)}) collective-permute-start(bf16[128,3072]{1,0:T(8,128)(2,1)S(1)} %collective-permute-done.9.refs_3_.refs_6_), channel_id=1, source_target_pairs={{0,1},{8,11},{1,2},{9,8},{2,3},{10,9},{3,0},{11,10},{4,5},{12,15},... | collective-permute-start | bytes 2359304 | tf_op jit(solution)/shard_map/acts_zfar/ppermute | solution.py:336
  74.7 0.9 convert_bitcast_fusion
  75.6 1.6 %collective-permute-start.21 = (bf16[1,96,768]{2,1,0:T(8,128)(2,1)S(1)}, bf16[1,96,768]{2,1,0:T(8,128)(2,1)S(1)}, u32[]{:S(2)}, u32[]{:S(2)}) collective-permute-start(bf16[1,96,768]{2,1,0:T(8,128)(2,1)S(1)} %get-tuple-element.69), channel_id=1, source_target_pairs={{0,192},{64,0},{128,64},{192,128},{1,193},{65,1},{129,65},{193,129... | collective-permute-start | bytes 442376 | tf_op jit(solution)/shard_map/new_z3/ppermute | solution.py:319
  77.2 0.3 collective-permute-start.20
  77.5 0.7 collective-permute-start.19
  78.2 0.7 pad_add_fusion.2.index_ref
  78.9 7.5 %resid.4.refs_10_ = bf16[512,768]{1,0:T(8,128)(2,1)} custom-call(s32[4]{0:T(128)} %pad_add_fusion.2.index_ref, bf16[3072,768]{1,0:T(8,128)(2,1)} %bitcast.61, bf16[80,3072]{1,0:T(8,128)(2,1)} %collective-permute-done.2.refs_0_.refs_3_, bf16[48,3072]{1,0:T(8,128)(2,1)} %copy-done.13, bf16[128,3072]{1,0:T(8,128)(2,1)} %copy-done.1, ...), custom_call_target="tpu_custom_call" | custom-call | flops 150994944 | bytes 589824 | tf_op jit(solution)/shard_map/resid/pallas_call | solution.py:134
  86.4 3.9 %collective-permute-done.20 = bf16[1,96,768]{2,1,0:T(8,128)(2,1)S(1)} collective-permute-done((bf16[1,96,768]{2,1,0:T(8,128)(2,1)S(1)}, bf16[1,96,768]{2,1,0:T(8,128)(2,1)S(1)}, u32[]{:S(2)}, u32[]{:S(2)}) %collective-permute-start.20) | collective-permute-done | bytes 147488 | tf_op jit(solution)/shard_map/new_z2/ppermute | solution.py:319
  90.5 2.7 %collective-permute-start.23 = (bf16[4,96,768]{2,1,0:T(8,128)(2,1)S(1)}, bf16[4,96,768]{2,1,0:T(8,128)(2,1)S(1)}, u32[]{:S(2)}, u32[]{:S(2)}) collective-permute-start(bf16[4,96,768]{2,1,0:T(8,128)(2,1)S(1)} %pad_maximum_fusion.refs_0_), channel_id=1, source_target_pairs={{0,16},{8,56},{16,32},{24,8},{32,48},{40,24},{48,0},{56,40},{1,17}... | collective-permute-start | bytes 1769480 | tf_op jit(solution)/shard_map/new_near/ppermute | solution.py:336
  93.2 4.5 %resid.5.refs_11_ = bf16[128,768]{1,0:T(8,128)(2,1)} custom-call(s32[1]{0:T(128)} %bitcast.53.index_ref, bf16[3072,768]{1,0:T(8,128)(2,1)} %bitcast.62, bf16[128,3072]{1,0:T(8,128)(2,1)} %collective-permute-done.14.refs_0_.refs_8_, bf16[1024,768]{1,0:T(8,128)(2,1)} %refs_1_.1), custom_call_target="tpu_custom_call" | custom-call | flops 37748736 | bytes 368640 | tf_op jit(solution)/shard_map/resid/pallas_call | solution.py:134
  97.7 10.2 %grad.1 = (bf16[3072,768]{1,0:T(8,128)(2,1)}, f32[1,3072]{1,0:T(1,128)}, f32[1,768]{1,0:T(1,128)}) custom-call(bf16[128,3072]{1,0:T(8,128)(2,1)} %refs_0_.3, bf16[128,3072]{1,0:T(8,128)(2,1)} %collective-permute-done.refs_1_, bf16[128,3072]{1,0:T(8,128)(2,1)} %collective-permute-done.1.refs_2_, bf16[80,3072]{1,0:T(8,128)(2,1)} %collective-permute-done.2.refs_0_.refs_3_, ...), custom_call_target="tpu_custom_call" | custom-call | flops 4831838208 | bytes 12582912 | tf_op jit(solution)/shard_map/grad/pallas_call | solution.py:191
  108.1 1.6 %collective-permute-start.17 = (f32[24,128]{1,0:T(8,128)}, f32[24,128]{1,0:T(8,128)S(1)}, u32[]{:S(2)}, u32[]{:S(2)}) collective-permute-start(f32[24,128]{1,0:T(8,128)} %bitcast.69), channel_id=1, source_target_pairs={{0,3},{1,0},{2,1},{3,2},{4,7},{5,4},{6,5},{7,6},{8,11},{9,8},{10,9... | collective-permute-start | bytes 36872 | tf_op jit(solution)/shard_map/row_y/ppermute | solution.py:319
  109.7 0.6 collective-permute-start.15
  110.3 0.7 collective-permute-done.17
  111.0 3.0 %collective-permute-done.16 = f32[24,128]{1,0:T(8,128)S(1)} collective-permute-done((f32[24,128]{1,0:T(8,128)}, f32[24,128]{1,0:T(8,128)S(1)}, u32[]{:S(2)}, u32[]{:S(2)}) %collective-permute-start.16) | collective-permute-done | bytes 12320 | tf_op jit(solution)/shard_map/row_y/ppermute | solution.py:319
  114.0 0.7 add_add_fusion.row_a
  114.7 1.9 %collective-permute-start.18 = (f32[24,128]{1,0:T(8,128)S(1)}, f32[24,128]{1,0:T(8,128)S(1)}, u32[]{:S(2)}, u32[]{:S(2)}) collective-permute-start(f32[24,128]{1,0:T(8,128)S(1)} %add_add_fusion.row_a), channel_id=1, source_target_pairs={{0,4},{4,0},{1,5},{5,1},{2,6},{6,2},{3,7},{7,3},{8,12},{12,8},{9,1... | collective-permute-start | bytes 36872 | tf_op jit(solution)/shard_map/row_z/ppermute | solution.py:319
  116.6 3.9 %collective-permute-start.22 = (bf16[4,96,768]{2,1,0:T(8,128)(2,1)S(1)}, bf16[4,96,768]{2,1,0:T(8,128)(2,1)S(1)}, u32[]{:S(2)}, u32[]{:S(2)}) collective-permute-start(bf16[4,96,768]{2,1,0:T(8,128)(2,1)S(1)} %pad_maximum_fusion.refs_0_), channel_id=1, source_target_pairs={{0,8},{8,0},{1,9},{9,1},{2,10},{10,2},{3,11},{11,3},{4,12},{12,4},... | collective-permute-start | bytes 1769480 | tf_op jit(solution)/shard_map/new_core/ppermute | solution.py:319
  120.6 0.5 collective-permute-start.26
  121.2 2.8 %collective-permute-start.28 = (bf16[4,96,768]{2,1,0:T(8,128)(2,1)S(1)}, bf16[4,96,768]{2,1,0:T(8,128)(2,1)}, u32[]{:S(2)}, u32[]{:S(2)}) collective-permute-start(bf16[4,96,768]{2,1,0:T(8,128)(2,1)S(1)} %collective-permute-done.27.refs_6_), channel_id=1, source_target_pairs={{0,8},{8,0},{1,9},{9,1},{2,10},{10,2},{3,11},{11,3},{4,12},{12,4},... | collective-permute-start | bytes 1769480 | tf_op jit(solution)/shard_map/new_core/ppermute | solution.py:319
  123.9 0.7 stack.194.index_ref
  124.7 1.0 collective-permute-done.28.refs_7_
  125.7 9.6 %merge.1 = (bf16[3072,768]{1,0:T(8,128)(2,1)}, f32[24,128]{1,0:T(8,128)}, f32[1,768]{1,0:T(1,128)}) custom-call(s32[32]{0:T(128)} %stack.194.index_ref, f32[24,128]{1,0:T(8,128)} %bitcast.68, f32[24,128]{1,0:T(8,128)} %copy-done.14, f32[24,128]{1,0:T(8,128)} %copy-done.15, f32[1,768]{1,0:T(1,128)} %col_state.1, f32[1,768]{1,0:T(1,128)} %get-tuple-element.56.col_sum, ...), custom_call_target="tpu_custom_call" | custom-call | flops 18874368 | bytes 18874368 | tf_op jit(solution)/shard_map/merge/pallas_call | solution.py:285
  (62 shorter events, 0.9 us)
Async XLA Ops:
  3.9 11.2 %collective-permute-start.5 = (bf16[4,4,96,768]{3,2,1,0:T(8,128)(2,1)}, bf16[4,4,96,768]{3,2,1,0:T(8,128)(2,1)S(1)}, u32[]{:S(2)}, u32[]{:S(2)}) collective-permute-start(bf16[4,4,96,768]{3,2,1,0:T(8,128)(2,1)} %dynamic-slice_bitcast_fusion), channel_id=1, source_target_pairs={{0,8},{8,0},{1,9},{9,1},{2,10},{10,2},{3,11},{11,3},{4,12},{12,4},... | collective-permute-start | bytes 7077896 | tf_op jit(solution)/shard_map/sum_core/ppermute | solution.py:319
  7.1 19.3 %collective-permute-start.1 = (bf16[128,3072]{1,0:T(8,128)(2,1)}, bf16[128,3072]{1,0:T(8,128)(2,1)}, u32[]{:S(2)}, u32[]{:S(2)}) collective-permute-start(bf16[128,3072]{1,0:T(8,128)(2,1)} %refs_0_.3), channel_id=1, source_target_pairs={{0,3},{8,9},{1,0},{9,10},{2,1},{10,11},{3,2},{11,8},{4,7},{12,13},... | collective-permute-start | bytes 2359304 | tf_op jit(solution)/shard_map/acts_back/ppermute | solution.py:336
  7.1 19.5 %collective-permute-start = (bf16[128,3072]{1,0:T(8,128)(2,1)}, bf16[128,3072]{1,0:T(8,128)(2,1)}, u32[]{:S(2)}, u32[]{:S(2)}) collective-permute-start(bf16[128,3072]{1,0:T(8,128)(2,1)} %refs_0_.3), channel_id=1, source_target_pairs={{0,1},{8,11},{1,2},{9,8},{2,3},{10,9},{3,0},{11,10},{4,5},{12,15},... | collective-permute-start | bytes 2359304 | tf_op jit(solution)/shard_map/acts_near/ppermute | solution.py:336
  9.8 29.1 %collective-permute-start.4 = (bf16[128,3072]{1,0:T(8,128)(2,1)}, bf16[128,3072]{1,0:T(8,128)(2,1)S(1)}, u32[]{:S(2)}, u32[]{:S(2)}) collective-permute-start(bf16[128,3072]{1,0:T(8,128)(2,1)} %refs_0_.3), channel_id=1, source_target_pairs={{0,4},{4,0},{1,5},{5,1},{2,6},{6,2},{3,7},{7,3},{8,12},{12,8},{9,1... | collective-permute-start | bytes 2359304 | tf_op jit(solution)/shard_map/acts_zown/ppermute | solution.py:319
  15.1 2.3 %copy-start = (bf16[1,3072,768]{2,1,0:T(8,128)(2,1)S(1)}, bf16[1,3072,768]{2,1,0:T(8,128)(2,1)}, u32[]{:S(2)}) copy-start(bf16[1,3072,768]{2,1,0:T(8,128)(2,1)} %param.9) | copy-start | bytes 14155780
  19.8 0.9 copy-start.3
  20.7 19.3 %collective-permute-start.6 = (bf16[4,96,768]{2,1,0:T(8,128)(2,1)}, bf16[4,96,768]{2,1,0:T(8,128)(2,1)S(1)}, u32[]{:S(2)}, u32[]{:S(2)}) collective-permute-start(bf16[4,96,768]{2,1,0:T(8,128)(2,1)} %get-tuple-element.40), channel_id=1, source_target_pairs={{0,16},{8,56},{16,32},{24,8},{32,48},{40,24},{48,0},{56,40},{1,17}... | collective-permute-start | bytes 1769480 | tf_op jit(solution)/shard_map/sum_near/ppermute | solution.py:336
  23.2 16.8 %collective-permute-start.7 = (bf16[4,96,768]{2,1,0:T(8,128)(2,1)}, bf16[4,96,768]{2,1,0:T(8,128)(2,1)S(1)}, u32[]{:S(2)}, u32[]{:S(2)}) collective-permute-start(bf16[4,96,768]{2,1,0:T(8,128)(2,1)} %get-tuple-element.41), channel_id=1, source_target_pairs={{0,48},{8,24},{16,0},{24,40},{32,16},{40,56},{48,32},{56,8},{1,49}... | collective-permute-start | bytes 1769480 | tf_op jit(solution)/shard_map/sum_back/ppermute | solution.py:336
  26.4 24.9 %collective-permute-start.8 = (bf16[4,96,768]{2,1,0:T(8,128)(2,1)}, bf16[4,96,768]{2,1,0:T(8,128)(2,1)S(1)}, u32[]{:S(2)}, u32[]{:S(2)}) collective-permute-start(bf16[4,96,768]{2,1,0:T(8,128)(2,1)} %get-tuple-element.42), channel_id=1, source_target_pairs={{0,32},{16,48},{32,0},{48,16},{1,33},{17,49},{33,1},{49,17},{2,34}... | collective-permute-start | bytes 1769480 | tf_op jit(solution)/shard_map/sum_far/ppermute | solution.py:319
  28.5 23.9 %collective-permute-start.2 = (bf16[80,3072]{1,0:T(8,128)(2,1)}, bf16[80,3072]{1,0:T(8,128)(2,1)}, u32[]{:S(2)}, u32[]{:S(2)}) collective-permute-start(bf16[80,3072]{1,0:T(8,128)(2,1)} %slice.6), channel_id=1, source_target_pairs={{0,1},{8,11},{1,2},{9,8},{2,3},{10,9},{3,0},{11,10},{4,5},{12,15},... | collective-permute-start | bytes 1474568 | tf_op jit(solution)/shard_map/acts_far0/ppermute | solution.py:336
  32.1 19.2 %copy-start.4 = (bf16[4,96,768]{2,1,0:T(8,128)(2,1)S(1)}, bf16[4,96,768]{2,1,0:T(8,128)(2,1)}, u32[]{:S(2)}) copy-start(bf16[4,96,768]{2,1,0:T(8,128)(2,1)} %copy-done.3) | copy-start | bytes 1769476
  38.9 1.1 copy-start.2
  39.9 38.9 %copy-start.1 = (bf16[128,3072]{1,0:T(8,128)(2,1)}, bf16[128,3072]{1,0:T(8,128)(2,1)S(1)}, u32[]{:S(2)}) copy-start(bf16[128,3072]{1,0:T(8,128)(2,1)S(1)} %collective-permute-done.4.in_ref.refs_2_.refs_5_) | copy-start | bytes 2359300
  39.9 34.7 %copy-start.11 = (f32[96,768]{1,0:T(8,128)S(1)}, f32[96,768]{1,0:T(8,128)}, u32[]{:S(2)}) copy-start(f32[96,768]{1,0:T(8,128)} %param.12) | copy-start | bytes 884740
  39.9 34.7 %copy-start.12 = (f32[96,768]{1,0:T(8,128)S(1)}, f32[96,768]{1,0:T(8,128)}, u32[]{:S(2)}) copy-start(f32[96,768]{1,0:T(8,128)} %param.13) | copy-start | bytes 884740
  52.3 18.7 %collective-permute-start.9 = (bf16[128,3072]{1,0:T(8,128)(2,1)S(1)}, bf16[128,3072]{1,0:T(8,128)(2,1)S(1)}, u32[]{:S(2)}, u32[]{:S(2)}) collective-permute-start(bf16[128,3072]{1,0:T(8,128)(2,1)S(1)} %collective-permute-done.4.in_ref.refs_2_.refs_5_), channel_id=1, source_target_pairs={{0,1},{8,11},{1,2},{9,8},{2,3},{10,9},{3,0},{11,10},{4,5},{12,15},... | collective-permute-start | bytes 2359304 | tf_op jit(solution)/shard_map/acts_znear/ppermute | solution.py:336
  55.2 23.7 %collective-permute-start.10 = (bf16[128,3072]{1,0:T(8,128)(2,1)S(1)}, bf16[128,3072]{1,0:T(8,128)(2,1)}, u32[]{:S(2)}, u32[]{:S(2)}) collective-permute-start(bf16[128,3072]{1,0:T(8,128)(2,1)S(1)} %collective-permute-done.4.in_ref.refs_2_.refs_5_), channel_id=1, source_target_pairs={{0,3},{8,9},{1,0},{9,10},{2,1},{10,11},{3,2},{11,8},{4,7},{12,13},... | collective-permute-start | bytes 2359304 | tf_op jit(solution)/shard_map/acts_zback/ppermute | solution.py:336
  55.2 4.4 %collective-permute-start.13 = (bf16[96,768]{1,0:T(8,128)(2,1)S(1)}, bf16[96,768]{1,0:T(8,128)(2,1)S(1)}, u32[]{:S(2)}, u32[]{:S(2)}) collective-permute-start(bf16[96,768]{1,0:T(8,128)(2,1)S(1)} %get-tuple-element.48), channel_id=1, source_target_pairs={{0,192},{64,0},{128,64},{192,128},{1,193},{65,1},{129,65},{193,129... | collective-permute-start | bytes 442376 | tf_op jit(solution)/shard_map/sum_z3/ppermute | solution.py:319
  56.9 7.1 %collective-permute-start.12 = (bf16[96,768]{1,0:T(8,128)(2,1)S(1)}, bf16[96,768]{1,0:T(8,128)(2,1)S(1)}, u32[]{:S(2)}, u32[]{:S(2)}) collective-permute-start(bf16[96,768]{1,0:T(8,128)(2,1)S(1)} %get-tuple-element.46), channel_id=1, source_target_pairs={{0,64},{64,128},{128,192},{192,0},{1,65},{65,129},{129,193},{193,1... | collective-permute-start | bytes 442376 | tf_op jit(solution)/shard_map/sum_z1/ppermute | solution.py:319
  56.9 13.0 %collective-permute-start.11 = (bf16[96,768]{1,0:T(8,128)(2,1)S(1)}, bf16[96,768]{1,0:T(8,128)(2,1)S(1)}, u32[]{:S(2)}, u32[]{:S(2)}) collective-permute-start(bf16[96,768]{1,0:T(8,128)(2,1)S(1)} %get-tuple-element.44), channel_id=1, source_target_pairs={{0,128},{64,192},{128,0},{192,64},{1,129},{65,193},{129,1},{193,65... | collective-permute-start | bytes 442376 | tf_op jit(solution)/shard_map/sum_z2/ppermute | solution.py:319
  59.6 17.9 %collective-permute-start.3 = (bf16[48,3072]{1,0:T(8,128)(2,1)S(1)}, bf16[48,3072]{1,0:T(8,128)(2,1)S(1)}, u32[]{:S(2)}, u32[]{:S(2)}) collective-permute-start(bf16[48,3072]{1,0:T(8,128)(2,1)S(1)} %slice.7), channel_id=1, source_target_pairs={{0,1},{8,11},{1,2},{9,8},{2,3},{10,9},{3,0},{11,10},{4,5},{12,15},... | collective-permute-start | bytes 884744 | tf_op jit(solution)/shard_map/acts_far1/ppermute | solution.py:336
  71.1 7.8 %copy-start.6 = (bf16[128,3072]{1,0:T(8,128)(2,1)}, bf16[128,3072]{1,0:T(8,128)(2,1)S(1)}, u32[]{:S(2)}) copy-start(bf16[128,3072]{1,0:T(8,128)(2,1)S(1)} %collective-permute-done.9.refs_3_.refs_6_) | copy-start | bytes 2359300
  71.1 22.1 %collective-permute-start.14 = (bf16[128,3072]{1,0:T(8,128)(2,1)S(1)}, bf16[128,3072]{1,0:T(8,128)(2,1)}, u32[]{:S(2)}, u32[]{:S(2)}) collective-permute-start(bf16[128,3072]{1,0:T(8,128)(2,1)S(1)} %collective-permute-done.9.refs_3_.refs_6_), channel_id=1, source_target_pairs={{0,1},{8,11},{1,2},{9,8},{2,3},{10,9},{3,0},{11,10},{4,5},{12,15},... | collective-permute-start | bytes 2359304 | tf_op jit(solution)/shard_map/acts_zfar/ppermute | solution.py:336
  75.6 10.8 %collective-permute-start.21 = (bf16[1,96,768]{2,1,0:T(8,128)(2,1)S(1)}, bf16[1,96,768]{2,1,0:T(8,128)(2,1)S(1)}, u32[]{:S(2)}, u32[]{:S(2)}) collective-permute-start(bf16[1,96,768]{2,1,0:T(8,128)(2,1)S(1)} %get-tuple-element.69), channel_id=1, source_target_pairs={{0,192},{64,0},{128,64},{192,128},{1,193},{65,1},{129,65},{193,129... | collective-permute-start | bytes 442376 | tf_op jit(solution)/shard_map/new_z3/ppermute | solution.py:319
  77.2 13.1 %collective-permute-start.20 = (bf16[1,96,768]{2,1,0:T(8,128)(2,1)S(1)}, bf16[1,96,768]{2,1,0:T(8,128)(2,1)S(1)}, u32[]{:S(2)}, u32[]{:S(2)}) collective-permute-start(bf16[1,96,768]{2,1,0:T(8,128)(2,1)S(1)} %get-tuple-element.69), channel_id=1, source_target_pairs={{0,128},{64,192},{128,0},{192,64},{1,129},{65,193},{129,1},{193,65... | collective-permute-start | bytes 442376 | tf_op jit(solution)/shard_map/new_z2/ppermute | solution.py:319
  77.5 1.4 %copy-start.13 = (bf16[48,3072]{1,0:T(8,128)(2,1)}, bf16[48,3072]{1,0:T(8,128)(2,1)S(1)}, u32[]{:S(2)}) copy-start(bf16[48,3072]{1,0:T(8,128)(2,1)S(1)} %collective-permute-done.3.refs_1_.refs_4_) | copy-start | bytes 884740
  77.5 12.8 %collective-permute-start.19 = (bf16[1,96,768]{2,1,0:T(8,128)(2,1)S(1)}, bf16[1,96,768]{2,1,0:T(8,128)(2,1)S(1)}, u32[]{:S(2)}, u32[]{:S(2)}) collective-permute-start(bf16[1,96,768]{2,1,0:T(8,128)(2,1)S(1)} %get-tuple-element.69), channel_id=1, source_target_pairs={{0,64},{64,128},{128,192},{192,0},{1,65},{65,129},{129,193},{193,1... | collective-permute-start | bytes 442376 | tf_op jit(solution)/shard_map/new_z1/ppermute | solution.py:319
  90.4 26.2 %copy-start.5 = (bf16[4,96,768]{2,1,0:T(8,128)(2,1)}, bf16[4,96,768]{2,1,0:T(8,128)(2,1)S(1)}, u32[]{:S(2)}) copy-start(bf16[4,96,768]{2,1,0:T(8,128)(2,1)S(1)} %pad_maximum_fusion.refs_0_) | copy-start | bytes 1769476
  90.4 17.5 %collective-permute-start.25 = (bf16[4,96,768]{2,1,0:T(8,128)(2,1)S(1)}, bf16[4,96,768]{2,1,0:T(8,128)(2,1)S(1)}, u32[]{:S(2)}, u32[]{:S(2)}) collective-permute-start(bf16[4,96,768]{2,1,0:T(8,128)(2,1)S(1)} %pad_maximum_fusion.refs_0_), channel_id=1, source_target_pairs={{0,48},{8,24},{16,0},{24,40},{32,16},{40,56},{48,32},{56,8},{1,49}... | collective-permute-start | bytes 1769480 | tf_op jit(solution)/shard_map/new_back/ppermute | solution.py:336
  90.5 17.5 %collective-permute-start.23 = (bf16[4,96,768]{2,1,0:T(8,128)(2,1)S(1)}, bf16[4,96,768]{2,1,0:T(8,128)(2,1)S(1)}, u32[]{:S(2)}, u32[]{:S(2)}) collective-permute-start(bf16[4,96,768]{2,1,0:T(8,128)(2,1)S(1)} %pad_maximum_fusion.refs_0_), channel_id=1, source_target_pairs={{0,16},{8,56},{16,32},{24,8},{32,48},{40,24},{48,0},{56,40},{1,17}... | collective-permute-start | bytes 1769480 | tf_op jit(solution)/shard_map/new_near/ppermute | solution.py:336
  107.9 17.8 %copy-start.7 = (bf16[4,96,768]{2,1,0:T(8,128)(2,1)}, bf16[4,96,768]{2,1,0:T(8,128)(2,1)S(1)}, u32[]{:S(2)}) copy-start(bf16[4,96,768]{2,1,0:T(8,128)(2,1)S(1)} %collective-permute-done.25.refs_4_) | copy-start | bytes 1769476
  108.0 17.7 %copy-start.8 = (bf16[4,96,768]{2,1,0:T(8,128)(2,1)}, bf16[4,96,768]{2,1,0:T(8,128)(2,1)S(1)}, u32[]{:S(2)}) copy-start(bf16[4,96,768]{2,1,0:T(8,128)(2,1)S(1)} %collective-permute-done.23.refs_2_) | copy-start | bytes 1769476
  108.0 13.2 %collective-permute-start.27 = (bf16[4,96,768]{2,1,0:T(8,128)(2,1)S(1)}, bf16[4,96,768]{2,1,0:T(8,128)(2,1)S(1)}, u32[]{:S(2)}, u32[]{:S(2)}) collective-permute-start(bf16[4,96,768]{2,1,0:T(8,128)(2,1)S(1)} %collective-permute-done.23.refs_2_), channel_id=1, source_target_pairs={{0,16},{8,56},{16,32},{24,8},{32,48},{40,24},{48,0},{56,40},{1,17}... | collective-permute-start | bytes 1769480 | tf_op jit(solution)/shard_map/new_far/ppermute | solution.py:336
  108.1 2.9 %collective-permute-start.17 = (f32[24,128]{1,0:T(8,128)}, f32[24,128]{1,0:T(8,128)S(1)}, u32[]{:S(2)}, u32[]{:S(2)}) collective-permute-start(f32[24,128]{1,0:T(8,128)} %bitcast.69), channel_id=1, source_target_pairs={{0,3},{1,0},{2,1},{3,2},{4,7},{5,4},{6,5},{7,6},{8,11},{9,8},{10,9... | collective-permute-start | bytes 36872 | tf_op jit(solution)/shard_map/row_y/ppermute | solution.py:319
  109.7 4.3 %collective-permute-start.16 = (f32[24,128]{1,0:T(8,128)}, f32[24,128]{1,0:T(8,128)S(1)}, u32[]{:S(2)}, u32[]{:S(2)}) collective-permute-start(f32[24,128]{1,0:T(8,128)} %bitcast.70), channel_id=1, source_target_pairs={{0,2},{1,3},{2,0},{3,1},{4,6},{5,7},{6,4},{7,5},{8,10},{9,11},{10,... | collective-permute-start | bytes 36872 | tf_op jit(solution)/shard_map/row_y/ppermute | solution.py:319
  109.7 4.3 %collective-permute-start.15 = (f32[24,128]{1,0:T(8,128)}, f32[24,128]{1,0:T(8,128)S(1)}, u32[]{:S(2)}, u32[]{:S(2)}) collective-permute-start(f32[24,128]{1,0:T(8,128)} %bitcast.71), channel_id=1, source_target_pairs={{0,1},{1,2},{2,3},{3,0},{4,5},{5,6},{6,7},{7,4},{8,9},{9,10},{10,1... | collective-permute-start | bytes 36872 | tf_op jit(solution)/shard_map/row_y/ppermute | solution.py:319
  114.7 11.0 %copy-start.14 = (f32[24,128]{1,0:T(8,128)}, f32[24,128]{1,0:T(8,128)S(1)}, u32[]{:S(2)}) copy-start(f32[24,128]{1,0:T(8,128)S(1)} %add_add_fusion.row_a) | copy-start | bytes 36868
  114.7 6.5 %collective-permute-start.18 = (f32[24,128]{1,0:T(8,128)S(1)}, f32[24,128]{1,0:T(8,128)S(1)}, u32[]{:S(2)}, u32[]{:S(2)}) collective-permute-start(f32[24,128]{1,0:T(8,128)S(1)} %add_add_fusion.row_a), channel_id=1, source_target_pairs={{0,4},{4,0},{1,5},{5,1},{2,6},{6,2},{3,7},{7,3},{8,12},{12,8},{9,1... | collective-permute-start | bytes 36872 | tf_op jit(solution)/shard_map/row_z/ppermute | solution.py:319
  116.6 8.0 %collective-permute-start.22 = (bf16[4,96,768]{2,1,0:T(8,128)(2,1)S(1)}, bf16[4,96,768]{2,1,0:T(8,128)(2,1)S(1)}, u32[]{:S(2)}, u32[]{:S(2)}) collective-permute-start(bf16[4,96,768]{2,1,0:T(8,128)(2,1)S(1)} %pad_maximum_fusion.refs_0_), channel_id=1, source_target_pairs={{0,8},{8,0},{1,9},{9,1},{2,10},{10,2},{3,11},{11,3},{4,12},{12,4},... | collective-permute-start | bytes 1769480 | tf_op jit(solution)/shard_map/new_core/ppermute | solution.py:319
  120.6 4.1 %collective-permute-start.24 = (bf16[4,96,768]{2,1,0:T(8,128)(2,1)S(1)}, bf16[4,96,768]{2,1,0:T(8,128)(2,1)}, u32[]{:S(2)}, u32[]{:S(2)}) collective-permute-start(bf16[4,96,768]{2,1,0:T(8,128)(2,1)S(1)} %collective-permute-done.23.refs_2_), channel_id=1, source_target_pairs={{0,8},{8,0},{1,9},{9,1},{2,10},{10,2},{3,11},{11,3},{4,12},{12,4},... | collective-permute-start | bytes 1769480 | tf_op jit(solution)/shard_map/new_core/ppermute | solution.py:319
  120.6 4.1 %collective-permute-start.26 = (bf16[4,96,768]{2,1,0:T(8,128)(2,1)S(1)}, bf16[4,96,768]{2,1,0:T(8,128)(2,1)}, u32[]{:S(2)}, u32[]{:S(2)}) collective-permute-start(bf16[4,96,768]{2,1,0:T(8,128)(2,1)S(1)} %collective-permute-done.25.refs_4_), channel_id=1, source_target_pairs={{0,8},{8,0},{1,9},{9,1},{2,10},{10,2},{3,11},{11,3},{4,12},{12,4},... | collective-permute-start | bytes 1769480 | tf_op jit(solution)/shard_map/new_core/ppermute | solution.py:319
  121.2 4.5 %copy-start.15 = (f32[24,128]{1,0:T(8,128)}, f32[24,128]{1,0:T(8,128)S(1)}, u32[]{:S(2)}) copy-start(f32[24,128]{1,0:T(8,128)S(1)} %collective-permute-done.18.row_b) | copy-start | bytes 36868
  121.2 4.5 %copy-start.9 = (bf16[4,96,768]{2,1,0:T(8,128)(2,1)}, bf16[4,96,768]{2,1,0:T(8,128)(2,1)S(1)}, u32[]{:S(2)}) copy-start(bf16[4,96,768]{2,1,0:T(8,128)(2,1)S(1)} %collective-permute-done.27.refs_6_) | copy-start | bytes 1769476
  121.2 4.5 %collective-permute-start.28 = (bf16[4,96,768]{2,1,0:T(8,128)(2,1)S(1)}, bf16[4,96,768]{2,1,0:T(8,128)(2,1)}, u32[]{:S(2)}, u32[]{:S(2)}) collective-permute-start(bf16[4,96,768]{2,1,0:T(8,128)(2,1)S(1)} %collective-permute-done.27.refs_6_), channel_id=1, source_target_pairs={{0,8},{8,0},{1,9},{9,1},{2,10},{10,2},{3,11},{11,3},{4,12},{12,4},... | collective-permute-start | bytes 1769480 | tf_op jit(solution)/shard_map/new_core/ppermute | solution.py:319
  124.7 1.1 copy-start.10

commit v3 on v2

--- a/solution.py
+++ b/solution.py
@@ -390,7 +390,7 @@
         share = share + got.astype(jnp.float32)
     parts[1][0].extend((zown, znear, zback))
     parts[2][0].append(zfar)
-    share = after(share, znear)
+    share = after(share, far0)
 
     outer_grad = anchor - share / (NZ * NX * NC)
     momentum_next = outer_momentum * momentum + outer_grad

time: 136 us -> 136 us (level)
  no operation moved by 1% of the time
where the time goes in v3:
time: 136 us
  starting transfers between devices  46.4 us (34%)
  Pallas kernels  42.2 us (31%)
  waiting for transfers between devices  31.7 us (23%)
  local copies, waits for them, and re-layouts  11.2 us (8%)
  other arithmetic  3.07 us (2%)
    ppermute x17, waiting for transfers between devices, send(): return lax.ppermute(block, axis, ring(mesh_size[axis], k))  27 us
    ppermute x17, starting transfers between devices, send(): return lax.ppermute(block, axis, ring(mesh_size[axis], k))  25.1 us
    ppermute x12, starting transfers between devices, turn(): return lax.ppermute(block, axes, pairs)  21.3 us
    pallas_call x3, Pallas kernels, resid_call(): pl.pallas_call(functools.partial(resid_kernel, scale, heights), grid_spec...  18.8 us
    pallas_call x1, Pallas kernels, grad_call(): pl.pallas_call(functools.partial(grad_kernel, scale, len(blocks), len(res...  10.2 us
    pallas_call x1, Pallas kernels, merge_call(): pl.pallas_call(functools.partial(merge_kernel, pieces), in_specs=[pl.Bloc...  9.62 us
    ppermute x12, waiting for transfers between devices, turn(): return lax.ppermute(block, axes, pairs)  4.64 us
    unnamed x32, local copies, waits for them, and re-layouts  4.33 us
  transfers between devices with their start and end apart: 29, of which 12 were waited for; matrix products, arithmetic and copies ran while one was open for 5% of the time, Pallas kernels for 24%

profile of v3, /device:TPU:1, one launch (start us, length us, event | category | flops | bytes accessed | tf_op | source)
XLA Modules:
  0.0 135.5 jit_solution(3586871645436741825)
XLA Ops:
  0.6 3.2 %dynamic-slice_bitcast_fusion = bf16[4,4,96,768]{3,2,1,0:T(8,128)(2,1)} fusion(bf16[4,4,2,96,768]{4,3,2,1,0:T(8,128)(2,1)} %bitcast.59, s32[]{:T(128)S(6)} %select_n.177), kind=kLoop, calls=%fused_computation | loop fusion | bytes 4718596 | tf_op jit(solution)/shard_map/jit(dynamic_index_in_dim)/squeeze | solution.py:339
  3.9 3.2 %collective-permute-start.5 = (bf16[4,4,96,768]{3,2,1,0:T(8,128)(2,1)}, bf16[4,4,96,768]{3,2,1,0:T(8,128)(2,1)S(1)}, u32[]{:S(2)}, u32[]{:S(2)}) collective-permute-start(bf16[4,4,96,768]{3,2,1,0:T(8,128)(2,1)} %dynamic-slice_bitcast_fusion), channel_id=1, source_target_pairs={{0,8},{8,0},{1,9},{9,1},{2,10},{10,2},{3,11},{11,3},{4,12},{12,4},... | collective-permute-start | bytes 7077896 | tf_op jit(solution)/shard_map/sum_core/ppermute | solution.py:319
  7.1 2.7 %collective-permute-start = (bf16[128,3072]{1,0:T(8,128)(2,1)}, bf16[128,3072]{1,0:T(8,128)(2,1)}, u32[]{:S(2)}, u32[]{:S(2)}) collective-permute-start(bf16[128,3072]{1,0:T(8,128)(2,1)} %refs_0_.3), channel_id=1, source_target_pairs={{0,1},{8,11},{1,2},{9,8},{2,3},{10,9},{3,0},{11,10},{4,5},{12,15},... | collective-permute-start | bytes 2359304 | tf_op jit(solution)/shard_map/acts_near/ppermute | solution.py:336
  9.8 5.2 %collective-permute-start.4 = (bf16[128,3072]{1,0:T(8,128)(2,1)}, bf16[128,3072]{1,0:T(8,128)(2,1)S(1)}, u32[]{:S(2)}, u32[]{:S(2)}) collective-permute-start(bf16[128,3072]{1,0:T(8,128)(2,1)} %refs_0_.3), channel_id=1, source_target_pairs={{0,4},{4,0},{1,5},{5,1},{2,6},{6,2},{3,7},{7,3},{8,12},{12,8},{9,1... | collective-permute-start | bytes 2359304 | tf_op jit(solution)/shard_map/acts_zown/ppermute | solution.py:319
  15.1 2.3 %copy-done = bf16[1,3072,768]{2,1,0:T(8,128)(2,1)S(1)} copy-done((bf16[1,3072,768]{2,1,0:T(8,128)(2,1)S(1)}, bf16[1,3072,768]{2,1,0:T(8,128)(2,1)}, u32[]{:S(2)}) %copy-start) | copy-done | bytes 4718616
  17.4 2.4 %pieces.1 = (bf16[4,96,768]{2,1,0:T(8,128)(2,1)S(1)}, bf16[4,96,768]{2,1,0:T(8,128)(2,1)}, bf16[4,96,768]{2,1,0:T(8,128)(2,1)}, bf16[4,96,768]{2,1,0:T(8,128)(2,1)}) custom-call(s32[5]{0:T(128)S(1)} %stack.205.index_ref, bf16[4,4,2,96,768]{4,3,2,1,0:T(8,128)(2,1)S(1)} %bitcast.64, bf16[4,4,2,96,768]{4,3,2,1,0:T(8,128)(2,1)S(1)} %bitcast.65, ...), custom_call_target="tpu_custom_call" | custom-call | bytes 400000000 | tf_op jit(solution)/shard_map/pieces/pallas_call | solution.py:49
  19.8 0.9 copy-done.3
  20.7 2.5 %collective-permute-start.6 = (bf16[4,96,768]{2,1,0:T(8,128)(2,1)}, bf16[4,96,768]{2,1,0:T(8,128)(2,1)S(1)}, u32[]{:S(2)}, u32[]{:S(2)}) collective-permute-start(bf16[4,96,768]{2,1,0:T(8,128)(2,1)} %get-tuple-element.40), channel_id=1, source_target_pairs={{0,16},{8,56},{16,32},{24,8},{32,48},{40,24},{48,0},{56,40},{1,17}... | collective-permute-start | bytes 1769480 | tf_op jit(solution)/shard_map/sum_near/ppermute | solution.py:336
  23.2 3.2 %collective-permute-done.1.refs_2_ = bf16[128,3072]{1,0:T(8,128)(2,1)} collective-permute-done((bf16[128,3072]{1,0:T(8,128)(2,1)}, bf16[128,3072]{1,0:T(8,128)(2,1)}, u32[]{:S(2)}, u32[]{:S(2)}) %collective-permute-start.1) | collective-permute-done | bytes 786464 | tf_op jit(solution)/shard_map/acts_back/ppermute | solution.py:336
  26.6 1.8 %slice.6 = bf16[80,3072]{1,0:T(8,128)(2,1)} slice(bf16[128,3072]{1,0:T(8,128)(2,1)} %collective-permute-done.refs_1_), slice={[0:80], [0:3072]} | slice | bytes 983040 | tf_op jit(solution)/shard_map/slice | solution.py:350
  28.5 2.9 %collective-permute-start.2 = (bf16[80,3072]{1,0:T(8,128)(2,1)}, bf16[80,3072]{1,0:T(8,128)(2,1)}, u32[]{:S(2)}, u32[]{:S(2)}) collective-permute-start(bf16[80,3072]{1,0:T(8,128)(2,1)} %slice.6), channel_id=1, source_target_pairs={{0,1},{8,11},{1,2},{9,8},{2,3},{10,9},{3,0},{11,10},{4,5},{12,15},... | collective-permute-start | bytes 1474568 | tf_op jit(solution)/shard_map/acts_far0/ppermute | solution.py:336
  31.4 0.6 pad_add_fusion.1.index_ref
  32.1 6.8 %resid.3.waited_ref.refs_9_ = bf16[384,768]{1,0:T(8,128)(2,1)} custom-call(s32[3]{0:T(128)} %pad_add_fusion.1.index_ref, bf16[3072,768]{1,0:T(8,128)(2,1)} %bitcast.60, bf16[128,3072]{1,0:T(8,128)(2,1)} %refs_0_.3, bf16[128,3072]{1,0:T(8,128)(2,1)} %collective-permute-done.refs_1_, bf16[128,3072]{1,0:T(8,128)(2,1)} %collective-permute-done.1.refs_2_, ...), custom_call_target="tpu_custom_call" | custom-call | flops 113246208 | bytes 516096 | tf_op jit(solution)/shard_map/resid/pallas_call | solution.py:134
  38.9 1.1 copy-done.2
  40.0 11.3 %collective-permute-done.8.far = bf16[4,96,768]{2,1,0:T(8,128)(2,1)S(1)} collective-permute-done((bf16[4,96,768]{2,1,0:T(8,128)(2,1)}, bf16[4,96,768]{2,1,0:T(8,128)(2,1)S(1)}, u32[]{:S(2)}, u32[]{:S(2)}) %collective-permute-start.8) | collective-permute-done | bytes 589856 | tf_op jit(solution)/shard_map/sum_far/ppermute | solution.py:319
  51.3 1.1 total.1
  52.3 2.9 %collective-permute-start.9 = (bf16[128,3072]{1,0:T(8,128)(2,1)S(1)}, bf16[128,3072]{1,0:T(8,128)(2,1)S(1)}, u32[]{:S(2)}, u32[]{:S(2)}) collective-permute-start(bf16[128,3072]{1,0:T(8,128)(2,1)S(1)} %collective-permute-done.4.in_ref.refs_2_.refs_5_), channel_id=1, source_target_pairs={{0,1},{8,11},{1,2},{9,8},{2,3},{10,9},{3,0},{11,10},{4,5},{12,15},... | collective-permute-start | bytes 2359304 | tf_op jit(solution)/shard_map/acts_znear/ppermute | solution.py:336
  55.2 1.6 %collective-permute-start.13 = (bf16[96,768]{1,0:T(8,128)(2,1)S(1)}, bf16[96,768]{1,0:T(8,128)(2,1)S(1)}, u32[]{:S(2)}, u32[]{:S(2)}) collective-permute-start(bf16[96,768]{1,0:T(8,128)(2,1)S(1)} %get-tuple-element.48), channel_id=1, source_target_pairs={{0,192},{64,0},{128,64},{192,128},{1,193},{65,1},{129,65},{193,129... | collective-permute-start | bytes 442376 | tf_op jit(solution)/shard_map/sum_z3/ppermute | solution.py:319
  56.9 1.0 collective-permute-start.11
  57.9 1.0 slice.7
  58.8 0.8 collective-permute-done.13
  59.6 4.0 %collective-permute-start.3 = (bf16[48,3072]{1,0:T(8,128)(2,1)S(1)}, bf16[48,3072]{1,0:T(8,128)(2,1)S(1)}, u32[]{:S(2)}, u32[]{:S(2)}) collective-permute-start(bf16[48,3072]{1,0:T(8,128)(2,1)S(1)} %slice.7), channel_id=1, source_target_pairs={{0,1},{8,11},{1,2},{9,8},{2,3},{10,9},{3,0},{11,10},{4,5},{12,15},... | collective-permute-start | bytes 884744 | tf_op jit(solution)/shard_map/acts_far1/ppermute | solution.py:336
  63.6 0.4 collective-permute-done.12
  64.0 5.9 %collective-permute-done.11 = bf16[96,768]{1,0:T(8,128)(2,1)S(1)} collective-permute-done((bf16[96,768]{1,0:T(8,128)(2,1)S(1)}, bf16[96,768]{1,0:T(8,128)(2,1)S(1)}, u32[]{:S(2)}, u32[]{:S(2)}) %collective-permute-start.11) | collective-permute-done | bytes 147488 | tf_op jit(solution)/shard_map/sum_z2/ppermute | solution.py:319
  69.9 1.2 collective-permute-done.9.refs_3_.refs_6_
  71.1 3.5 %collective-permute-start.14 = (bf16[128,3072]{1,0:T(8,128)(2,1)S(1)}, bf16[128,3072]{1,0:T(8,128)(2,1)}, u32[]{:S(2)}, u32[]{:S(2)}) collective-permute-start(bf16[128,3072]{1,0:T(8,128)(2,1)S(1)} %collective-permute-done.9.refs_3_.refs_6_), channel_id=1, source_target_pairs={{0,1},{8,11},{1,2},{9,8},{2,3},{10,9},{3,0},{11,10},{4,5},{12,15},... | collective-permute-start | bytes 2359304 | tf_op jit(solution)/shard_map/acts_zfar/ppermute | solution.py:336
  74.7 0.9 convert_bitcast_fusion
  75.6 1.6 %collective-permute-start.21 = (bf16[1,96,768]{2,1,0:T(8,128)(2,1)S(1)}, bf16[1,96,768]{2,1,0:T(8,128)(2,1)S(1)}, u32[]{:S(2)}, u32[]{:S(2)}) collective-permute-start(bf16[1,96,768]{2,1,0:T(8,128)(2,1)S(1)} %get-tuple-element.69), channel_id=1, source_target_pairs={{0,192},{64,0},{128,64},{192,128},{1,193},{65,1},{129,65},{193,129... | collective-permute-start | bytes 442376 | tf_op jit(solution)/shard_map/new_z3/ppermute | solution.py:319
  77.2 0.3 collective-permute-start.20
  77.5 0.7 collective-permute-start.19
  78.2 0.7 pad_add_fusion.2.index_ref
  78.9 7.5 %resid.4.refs_10_ = bf16[512,768]{1,0:T(8,128)(2,1)} custom-call(s32[4]{0:T(128)} %pad_add_fusion.2.index_ref, bf16[3072,768]{1,0:T(8,128)(2,1)} %bitcast.61, bf16[80,3072]{1,0:T(8,128)(2,1)} %collective-permute-done.2.refs_0_.refs_3_, bf16[48,3072]{1,0:T(8,128)(2,1)} %copy-done.13, bf16[128,3072]{1,0:T(8,128)(2,1)} %copy-done.1, ...), custom_call_target="tpu_custom_call" | custom-call | flops 150994944 | bytes 589824 | tf_op jit(solution)/shard_map/resid/pallas_call | solution.py:134
  86.4 3.9 %collective-permute-done.20 = bf16[1,96,768]{2,1,0:T(8,128)(2,1)S(1)} collective-permute-done((bf16[1,96,768]{2,1,0:T(8,128)(2,1)S(1)}, bf16[1,96,768]{2,1,0:T(8,128)(2,1)S(1)}, u32[]{:S(2)}, u32[]{:S(2)}) %collective-permute-start.20) | collective-permute-done | bytes 147488 | tf_op jit(solution)/shard_map/new_z2/ppermute | solution.py:319
  90.5 2.7 %collective-permute-start.23 = (bf16[4,96,768]{2,1,0:T(8,128)(2,1)S(1)}, bf16[4,96,768]{2,1,0:T(8,128)(2,1)S(1)}, u32[]{:S(2)}, u32[]{:S(2)}) collective-permute-start(bf16[4,96,768]{2,1,0:T(8,128)(2,1)S(1)} %pad_maximum_fusion.refs_0_), channel_id=1, source_target_pairs={{0,16},{8,56},{16,32},{24,8},{32,48},{40,24},{48,0},{56,40},{1,17}... | collective-permute-start | bytes 1769480 | tf_op jit(solution)/shard_map/new_near/ppermute | solution.py:336
  93.2 4.5 %resid.5.refs_11_ = bf16[128,768]{1,0:T(8,128)(2,1)} custom-call(s32[1]{0:T(128)} %bitcast.53.index_ref, bf16[3072,768]{1,0:T(8,128)(2,1)} %bitcast.62, bf16[128,3072]{1,0:T(8,128)(2,1)} %collective-permute-done.14.refs_0_.refs_8_, bf16[1024,768]{1,0:T(8,128)(2,1)} %refs_1_.1), custom_call_target="tpu_custom_call" | custom-call | flops 37748736 | bytes 368640 | tf_op jit(solution)/shard_map/resid/pallas_call | solution.py:134
  97.7 10.2 %grad.1 = (bf16[3072,768]{1,0:T(8,128)(2,1)}, f32[1,3072]{1,0:T(1,128)}, f32[1,768]{1,0:T(1,128)}) custom-call(bf16[128,3072]{1,0:T(8,128)(2,1)} %refs_0_.3, bf16[128,3072]{1,0:T(8,128)(2,1)} %collective-permute-done.refs_1_, bf16[128,3072]{1,0:T(8,128)(2,1)} %collective-permute-done.1.refs_2_, bf16[80,3072]{1,0:T(8,128)(2,1)} %collective-permute-done.2.refs_0_.refs_3_, ...), custom_call_target="tpu_custom_call" | custom-call | flops 4831838208 | bytes 12582912 | tf_op jit(solution)/shard_map/grad/pallas_call | solution.py:191
  108.1 1.6 %collective-permute-start.17 = (f32[24,128]{1,0:T(8,128)}, f32[24,128]{1,0:T(8,128)S(1)}, u32[]{:S(2)}, u32[]{:S(2)}) collective-permute-start(f32[24,128]{1,0:T(8,128)} %bitcast.69), channel_id=1, source_target_pairs={{0,3},{1,0},{2,1},{3,2},{4,7},{5,4},{6,5},{7,6},{8,11},{9,8},{10,9... | collective-permute-start | bytes 36872 | tf_op jit(solution)/shard_map/row_y/ppermute | solution.py:319
  109.7 0.6 collective-permute-start.15
  110.3 0.7 collective-permute-done.17
  111.0 3.0 %collective-permute-done.16 = f32[24,128]{1,0:T(8,128)S(1)} collective-permute-done((f32[24,128]{1,0:T(8,128)}, f32[24,128]{1,0:T(8,128)S(1)}, u32[]{:S(2)}, u32[]{:S(2)}) %collective-permute-start.16) | collective-permute-done | bytes 12320 | tf_op jit(solution)/shard_map/row_y/ppermute | solution.py:319
  114.0 0.7 add_add_fusion.row_a
  114.7 1.9 %collective-permute-start.18 = (f32[24,128]{1,0:T(8,128)S(1)}, f32[24,128]{1,0:T(8,128)S(1)}, u32[]{:S(2)}, u32[]{:S(2)}) collective-permute-start(f32[24,128]{1,0:T(8,128)S(1)} %add_add_fusion.row_a), channel_id=1, source_target_pairs={{0,4},{4,0},{1,5},{5,1},{2,6},{6,2},{3,7},{7,3},{8,12},{12,8},{9,1... | collective-permute-start | bytes 36872 | tf_op jit(solution)/shard_map/row_z/ppermute | solution.py:319
  116.6 3.9 %collective-permute-start.22 = (bf16[4,96,768]{2,1,0:T(8,128)(2,1)S(1)}, bf16[4,96,768]{2,1,0:T(8,128)(2,1)S(1)}, u32[]{:S(2)}, u32[]{:S(2)}) collective-permute-start(bf16[4,96,768]{2,1,0:T(8,128)(2,1)S(1)} %pad_maximum_fusion.refs_0_), channel_id=1, source_target_pairs={{0,8},{8,0},{1,9},{9,1},{2,10},{10,2},{3,11},{11,3},{4,12},{12,4},... | collective-permute-start | bytes 1769480 | tf_op jit(solution)/shard_map/new_core/ppermute | solution.py:319
  120.6 0.5 collective-permute-start.26
  121.2 2.8 %collective-permute-start.28 = (bf16[4,96,768]{2,1,0:T(8,128)(2,1)S(1)}, bf16[4,96,768]{2,1,0:T(8,128)(2,1)}, u32[]{:S(2)}, u32[]{:S(2)}) collective-permute-start(bf16[4,96,768]{2,1,0:T(8,128)(2,1)S(1)} %collective-permute-done.27.refs_6_), channel_id=1, source_target_pairs={{0,8},{8,0},{1,9},{9,1},{2,10},{10,2},{3,11},{11,3},{4,12},{12,4},... | collective-permute-start | bytes 1769480 | tf_op jit(solution)/shard_map/new_core/ppermute | solution.py:319
  123.9 0.7 stack.194.index_ref
  124.7 1.0 collective-permute-done.28.refs_7_
  125.7 9.6 %merge.1 = (bf16[3072,768]{1,0:T(8,128)(2,1)}, f32[24,128]{1,0:T(8,128)}, f32[1,768]{1,0:T(1,128)}) custom-call(s32[32]{0:T(128)} %stack.194.index_ref, f32[24,128]{1,0:T(8,128)} %bitcast.68, f32[24,128]{1,0:T(8,128)} %copy-done.14, f32[24,128]{1,0:T(8,128)} %copy-done.15, f32[1,768]{1,0:T(1,128)} %col_state.1, f32[1,768]{1,0:T(1,128)} %get-tuple-element.56.col_sum, ...), custom_call_target="tpu_custom_call" | custom-call | flops 18874368 | bytes 18874368 | tf_op jit(solution)/shard_map/merge/pallas_call | solution.py:285
  (62 shorter events, 0.9 us)
Async XLA Ops:
  3.9 11.2 %collective-permute-start.5 = (bf16[4,4,96,768]{3,2,1,0:T(8,128)(2,1)}, bf16[4,4,96,768]{3,2,1,0:T(8,128)(2,1)S(1)}, u32[]{:S(2)}, u32[]{:S(2)}) collective-permute-start(bf16[4,4,96,768]{3,2,1,0:T(8,128)(2,1)} %dynamic-slice_bitcast_fusion), channel_id=1, source_target_pairs={{0,8},{8,0},{1,9},{9,1},{2,10},{10,2},{3,11},{11,3},{4,12},{12,4},... | collective-permute-start | bytes 7077896 | tf_op jit(solution)/shard_map/sum_core/ppermute | solution.py:319
  7.1 19.3 %collective-permute-start.1 = (bf16[128,3072]{1,0:T(8,128)(2,1)}, bf16[128,3072]{1,0:T(8,128)(2,1)}, u32[]{:S(2)}, u32[]{:S(2)}) collective-permute-start(bf16[128,3072]{1,0:T(8,128)(2,1)} %refs_0_.3), channel_id=1, source_target_pairs={{0,3},{8,9},{1,0},{9,10},{2,1},{10,11},{3,2},{11,8},{4,7},{12,13},... | collective-permute-start | bytes 2359304 | tf_op jit(solution)/shard_map/acts_back/ppermute | solution.py:336
  7.1 19.5 %collective-permute-start = (bf16[128,3072]{1,0:T(8,128)(2,1)}, bf16[128,3072]{1,0:T(8,128)(2,1)}, u32[]{:S(2)}, u32[]{:S(2)}) collective-permute-start(bf16[128,3072]{1,0:T(8,128)(2,1)} %refs_0_.3), channel_id=1, source_target_pairs={{0,1},{8,11},{1,2},{9,8},{2,3},{10,9},{3,0},{11,10},{4,5},{12,15},... | collective-permute-start | bytes 2359304 | tf_op jit(solution)/shard_map/acts_near/ppermute | solution.py:336
  9.8 29.1 %collective-permute-start.4 = (bf16[128,3072]{1,0:T(8,128)(2,1)}, bf16[128,3072]{1,0:T(8,128)(2,1)S(1)}, u32[]{:S(2)}, u32[]{:S(2)}) collective-permute-start(bf16[128,3072]{1,0:T(8,128)(2,1)} %refs_0_.3), channel_id=1, source_target_pairs={{0,4},{4,0},{1,5},{5,1},{2,6},{6,2},{3,7},{7,3},{8,12},{12,8},{9,1... | collective-permute-start | bytes 2359304 | tf_op jit(solution)/shard_map/acts_zown/ppermute | solution.py:319
  15.1 2.3 %copy-start = (bf16[1,3072,768]{2,1,0:T(8,128)(2,1)S(1)}, bf16[1,3072,768]{2,1,0:T(8,128)(2,1)}, u32[]{:S(2)}) copy-start(bf16[1,3072,768]{2,1,0:T(8,128)(2,1)} %param.9) | copy-start | bytes 14155780
  19.8 0.9 copy-start.3
  20.7 19.3 %collective-permute-start.6 = (bf16[4,96,768]{2,1,0:T(8,128)(2,1)}, bf16[4,96,768]{2,1,0:T(8,128)(2,1)S(1)}, u32[]{:S(2)}, u32[]{:S(2)}) collective-permute-start(bf16[4,96,768]{2,1,0:T(8,128)(2,1)} %get-tuple-element.40), channel_id=1, source_target_pairs={{0,16},{8,56},{16,32},{24,8},{32,48},{40,24},{48,0},{56,40},{1,17}... | collective-permute-start | bytes 1769480 | tf_op jit(solution)/shard_map/sum_near/ppermute | solution.py:336
  23.2 16.8 %collective-permute-start.7 = (bf16[4,96,768]{2,1,0:T(8,128)(2,1)}, bf16[4,96,768]{2,1,0:T(8,128)(2,1)S(1)}, u32[]{:S(2)}, u32[]{:S(2)}) collective-permute-start(bf16[4,96,768]{2,1,0:T(8,128)(2,1)} %get-tuple-element.41), channel_id=1, source_target_pairs={{0,48},{8,24},{16,0},{24,40},{32,16},{40,56},{48,32},{56,8},{1,49}... | collective-permute-start | bytes 1769480 | tf_op jit(solution)/shard_map/sum_back/ppermute | solution.py:336
  26.4 24.9 %collective-permute-start.8 = (bf16[4,96,768]{2,1,0:T(8,128)(2,1)}, bf16[4,96,768]{2,1,0:T(8,128)(2,1)S(1)}, u32[]{:S(2)}, u32[]{:S(2)}) collective-permute-start(bf16[4,96,768]{2,1,0:T(8,128)(2,1)} %get-tuple-element.42), channel_id=1, source_target_pairs={{0,32},{16,48},{32,0},{48,16},{1,33},{17,49},{33,1},{49,17},{2,34}... | collective-permute-start | bytes 1769480 | tf_op jit(solution)/shard_map/sum_far/ppermute | solution.py:319
  28.5 23.9 %collective-permute-start.2 = (bf16[80,3072]{1,0:T(8,128)(2,1)}, bf16[80,3072]{1,0:T(8,128)(2,1)}, u32[]{:S(2)}, u32[]{:S(2)}) collective-permute-start(bf16[80,3072]{1,0:T(8,128)(2,1)} %slice.6), channel_id=1, source_target_pairs={{0,1},{8,11},{1,2},{9,8},{2,3},{10,9},{3,0},{11,10},{4,5},{12,15},... | collective-permute-start | bytes 1474568 | tf_op jit(solution)/shard_map/acts_far0/ppermute | solution.py:336
  32.1 19.2 %copy-start.4 = (bf16[4,96,768]{2,1,0:T(8,128)(2,1)S(1)}, bf16[4,96,768]{2,1,0:T(8,128)(2,1)}, u32[]{:S(2)}) copy-start(bf16[4,96,768]{2,1,0:T(8,128)(2,1)} %copy-done.3) | copy-start | bytes 1769476
  38.9 1.1 copy-start.2
  39.9 38.9 %copy-start.1 = (bf16[128,3072]{1,0:T(8,128)(2,1)}, bf16[128,3072]{1,0:T(8,128)(2,1)S(1)}, u32[]{:S(2)}) copy-start(bf16[128,3072]{1,0:T(8,128)(2,1)S(1)} %collective-permute-done.4.in_ref.refs_2_.refs_5_) | copy-start | bytes 2359300
  39.9 34.7 %copy-start.11 = (f32[96,768]{1,0:T(8,128)S(1)}, f32[96,768]{1,0:T(8,128)}, u32[]{:S(2)}) copy-start(f32[96,768]{1,0:T(8,128)} %param.12) | copy-start | bytes 884740
  39.9 34.7 %copy-start.12 = (f32[96,768]{1,0:T(8,128)S(1)}, f32[96,768]{1,0:T(8,128)}, u32[]{:S(2)}) copy-start(f32[96,768]{1,0:T(8,128)} %param.13) | copy-start | bytes 884740
  52.3 18.7 %collective-permute-start.9 = (bf16[128,3072]{1,0:T(8,128)(2,1)S(1)}, bf16[128,3072]{1,0:T(8,128)(2,1)S(1)}, u32[]{:S(2)}, u32[]{:S(2)}) collective-permute-start(bf16[128,3072]{1,0:T(8,128)(2,1)S(1)} %collective-permute-done.4.in_ref.refs_2_.refs_5_), channel_id=1, source_target_pairs={{0,1},{8,11},{1,2},{9,8},{2,3},{10,9},{3,0},{11,10},{4,5},{12,15},... | collective-permute-start | bytes 2359304 | tf_op jit(solution)/shard_map/acts_znear/ppermute | solution.py:336
  55.2 23.7 %collective-permute-start.10 = (bf16[128,3072]{1,0:T(8,128)(2,1)S(1)}, bf16[128,3072]{1,0:T(8,128)(2,1)}, u32[]{:S(2)}, u32[]{:S(2)}) collective-permute-start(bf16[128,3072]{1,0:T(8,128)(2,1)S(1)} %collective-permute-done.4.in_ref.refs_2_.refs_5_), channel_id=1, source_target_pairs={{0,3},{8,9},{1,0},{9,10},{2,1},{10,11},{3,2},{11,8},{4,7},{12,13},... | collective-permute-start | bytes 2359304 | tf_op jit(solution)/shard_map/acts_zback/ppermute | solution.py:336
  55.2 4.4 %collective-permute-start.13 = (bf16[96,768]{1,0:T(8,128)(2,1)S(1)}, bf16[96,768]{1,0:T(8,128)(2,1)S(1)}, u32[]{:S(2)}, u32[]{:S(2)}) collective-permute-start(bf16[96,768]{1,0:T(8,128)(2,1)S(1)} %get-tuple-element.48), channel_id=1, source_target_pairs={{0,192},{64,0},{128,64},{192,128},{1,193},{65,1},{129,65},{193,129... | collective-permute-start | bytes 442376 | tf_op jit(solution)/shard_map/sum_z3/ppermute | solution.py:319
  56.9 7.1 %collective-permute-start.12 = (bf16[96,768]{1,0:T(8,128)(2,1)S(1)}, bf16[96,768]{1,0:T(8,128)(2,1)S(1)}, u32[]{:S(2)}, u32[]{:S(2)}) collective-permute-start(bf16[96,768]{1,0:T(8,128)(2,1)S(1)} %get-tuple-element.46), channel_id=1, source_target_pairs={{0,64},{64,128},{128,192},{192,0},{1,65},{65,129},{129,193},{193,1... | collective-permute-start | bytes 442376 | tf_op jit(solution)/shard_map/sum_z1/ppermute | solution.py:319
  56.9 13.0 %collective-permute-start.11 = (bf16[96,768]{1,0:T(8,128)(2,1)S(1)}, bf16[96,768]{1,0:T(8,128)(2,1)S(1)}, u32[]{:S(2)}, u32[]{:S(2)}) collective-permute-start(bf16[96,768]{1,0:T(8,128)(2,1)S(1)} %get-tuple-element.44), channel_id=1, source_target_pairs={{0,128},{64,192},{128,0},{192,64},{1,129},{65,193},{129,1},{193,65... | collective-permute-start | bytes 442376 | tf_op jit(solution)/shard_map/sum_z2/ppermute | solution.py:319
  59.6 17.9 %collective-permute-start.3 = (bf16[48,3072]{1,0:T(8,128)(2,1)S(1)}, bf16[48,3072]{1,0:T(8,128)(2,1)S(1)}, u32[]{:S(2)}, u32[]{:S(2)}) collective-permute-start(bf16[48,3072]{1,0:T(8,128)(2,1)S(1)} %slice.7), channel_id=1, source_target_pairs={{0,1},{8,11},{1,2},{9,8},{2,3},{10,9},{3,0},{11,10},{4,5},{12,15},... | collective-permute-start | bytes 884744 | tf_op jit(solution)/shard_map/acts_far1/ppermute | solution.py:336
  71.1 7.8 %copy-start.6 = (bf16[128,3072]{1,0:T(8,128)(2,1)}, bf16[128,3072]{1,0:T(8,128)(2,1)S(1)}, u32[]{:S(2)}) copy-start(bf16[128,3072]{1,0:T(8,128)(2,1)S(1)} %collective-permute-done.9.refs_3_.refs_6_) | copy-start | bytes 2359300
  71.1 22.1 %collective-permute-start.14 = (bf16[128,3072]{1,0:T(8,128)(2,1)S(1)}, bf16[128,3072]{1,0:T(8,128)(2,1)}, u32[]{:S(2)}, u32[]{:S(2)}) collective-permute-start(bf16[128,3072]{1,0:T(8,128)(2,1)S(1)} %collective-permute-done.9.refs_3_.refs_6_), channel_id=1, source_target_pairs={{0,1},{8,11},{1,2},{9,8},{2,3},{10,9},{3,0},{11,10},{4,5},{12,15},... | collective-permute-start | bytes 2359304 | tf_op jit(solution)/shard_map/acts_zfar/ppermute | solution.py:336
  75.6 10.8 %collective-permute-start.21 = (bf16[1,96,768]{2,1,0:T(8,128)(2,1)S(1)}, bf16[1,96,768]{2,1,0:T(8,128)(2,1)S(1)}, u32[]{:S(2)}, u32[]{:S(2)}) collective-permute-start(bf16[1,96,768]{2,1,0:T(8,128)(2,1)S(1)} %get-tuple-element.69), channel_id=1, source_target_pairs={{0,192},{64,0},{128,64},{192,128},{1,193},{65,1},{129,65},{193,129... | collective-permute-start | bytes 442376 | tf_op jit(solution)/shard_map/new_z3/ppermute | solution.py:319
  77.2 13.1 %collective-permute-start.20 = (bf16[1,96,768]{2,1,0:T(8,128)(2,1)S(1)}, bf16[1,96,768]{2,1,0:T(8,128)(2,1)S(1)}, u32[]{:S(2)}, u32[]{:S(2)}) collective-permute-start(bf16[1,96,768]{2,1,0:T(8,128)(2,1)S(1)} %get-tuple-element.69), channel_id=1, source_target_pairs={{0,128},{64,192},{128,0},{192,64},{1,129},{65,193},{129,1},{193,65... | collective-permute-start | bytes 442376 | tf_op jit(solution)/shard_map/new_z2/ppermute | solution.py:319
  77.5 1.4 %copy-start.13 = (bf16[48,3072]{1,0:T(8,128)(2,1)}, bf16[48,3072]{1,0:T(8,128)(2,1)S(1)}, u32[]{:S(2)}) copy-start(bf16[48,3072]{1,0:T(8,128)(2,1)S(1)} %collective-permute-done.3.refs_1_.refs_4_) | copy-start | bytes 884740
  77.5 12.8 %collective-permute-start.19 = (bf16[1,96,768]{2,1,0:T(8,128)(2,1)S(1)}, bf16[1,96,768]{2,1,0:T(8,128)(2,1)S(1)}, u32[]{:S(2)}, u32[]{:S(2)}) collective-permute-start(bf16[1,96,768]{2,1,0:T(8,128)(2,1)S(1)} %get-tuple-element.69), channel_id=1, source_target_pairs={{0,64},{64,128},{128,192},{192,0},{1,65},{65,129},{129,193},{193,1... | collective-permute-start | bytes 442376 | tf_op jit(solution)/shard_map/new_z1/ppermute | solution.py:319
  90.4 26.2 %copy-start.5 = (bf16[4,96,768]{2,1,0:T(8,128)(2,1)}, bf16[4,96,768]{2,1,0:T(8,128)(2,1)S(1)}, u32[]{:S(2)}) copy-start(bf16[4,96,768]{2,1,0:T(8,128)(2,1)S(1)} %pad_maximum_fusion.refs_0_) | copy-start | bytes 1769476
  90.4 17.5 %collective-permute-start.25 = (bf16[4,96,768]{2,1,0:T(8,128)(2,1)S(1)}, bf16[4,96,768]{2,1,0:T(8,128)(2,1)S(1)}, u32[]{:S(2)}, u32[]{:S(2)}) collective-permute-start(bf16[4,96,768]{2,1,0:T(8,128)(2,1)S(1)} %pad_maximum_fusion.refs_0_), channel_id=1, source_target_pairs={{0,48},{8,24},{16,0},{24,40},{32,16},{40,56},{48,32},{56,8},{1,49}... | collective-permute-start | bytes 1769480 | tf_op jit(solution)/shard_map/new_back/ppermute | solution.py:336
  90.5 17.5 %collective-permute-start.23 = (bf16[4,96,768]{2,1,0:T(8,128)(2,1)S(1)}, bf16[4,96,768]{2,1,0:T(8,128)(2,1)S(1)}, u32[]{:S(2)}, u32[]{:S(2)}) collective-permute-start(bf16[4,96,768]{2,1,0:T(8,128)(2,1)S(1)} %pad_maximum_fusion.refs_0_), channel_id=1, source_target_pairs={{0,16},{8,56},{16,32},{24,8},{32,48},{40,24},{48,0},{56,40},{1,17}... | collective-permute-start | bytes 1769480 | tf_op jit(solution)/shard_map/new_near/ppermute | solution.py:336
  107.9 17.8 %copy-start.7 = (bf16[4,96,768]{2,1,0:T(8,128)(2,1)}, bf16[4,96,768]{2,1,0:T(8,128)(2,1)S(1)}, u32[]{:S(2)}) copy-start(bf16[4,96,768]{2,1,0:T(8,128)(2,1)S(1)} %collective-permute-done.25.refs_4_) | copy-start | bytes 1769476
  108.0 17.7 %copy-start.8 = (bf16[4,96,768]{2,1,0:T(8,128)(2,1)}, bf16[4,96,768]{2,1,0:T(8,128)(2,1)S(1)}, u32[]{:S(2)}) copy-start(bf16[4,96,768]{2,1,0:T(8,128)(2,1)S(1)} %collective-permute-done.23.refs_2_) | copy-start | bytes 1769476
  108.0 13.2 %collective-permute-start.27 = (bf16[4,96,768]{2,1,0:T(8,128)(2,1)S(1)}, bf16[4,96,768]{2,1,0:T(8,128)(2,1)S(1)}, u32[]{:S(2)}, u32[]{:S(2)}) collective-permute-start(bf16[4,96,768]{2,1,0:T(8,128)(2,1)S(1)} %collective-permute-done.23.refs_2_), channel_id=1, source_target_pairs={{0,16},{8,56},{16,32},{24,8},{32,48},{40,24},{48,0},{56,40},{1,17}... | collective-permute-start | bytes 1769480 | tf_op jit(solution)/shard_map/new_far/ppermute | solution.py:336
  108.1 2.9 %collective-permute-start.17 = (f32[24,128]{1,0:T(8,128)}, f32[24,128]{1,0:T(8,128)S(1)}, u32[]{:S(2)}, u32[]{:S(2)}) collective-permute-start(f32[24,128]{1,0:T(8,128)} %bitcast.69), channel_id=1, source_target_pairs={{0,3},{1,0},{2,1},{3,2},{4,7},{5,4},{6,5},{7,6},{8,11},{9,8},{10,9... | collective-permute-start | bytes 36872 | tf_op jit(solution)/shard_map/row_y/ppermute | solution.py:319
  109.7 4.3 %collective-permute-start.16 = (f32[24,128]{1,0:T(8,128)}, f32[24,128]{1,0:T(8,128)S(1)}, u32[]{:S(2)}, u32[]{:S(2)}) collective-permute-start(f32[24,128]{1,0:T(8,128)} %bitcast.70), channel_id=1, source_target_pairs={{0,2},{1,3},{2,0},{3,1},{4,6},{5,7},{6,4},{7,5},{8,10},{9,11},{10,... | collective-permute-start | bytes 36872 | tf_op jit(solution)/shard_map/row_y/ppermute | solution.py:319
  109.7 4.3 %collective-permute-start.15 = (f32[24,128]{1,0:T(8,128)}, f32[24,128]{1,0:T(8,128)S(1)}, u32[]{:S(2)}, u32[]{:S(2)}) collective-permute-start(f32[24,128]{1,0:T(8,128)} %bitcast.71), channel_id=1, source_target_pairs={{0,1},{1,2},{2,3},{3,0},{4,5},{5,6},{6,7},{7,4},{8,9},{9,10},{10,1... | collective-permute-start | bytes 36872 | tf_op jit(solution)/shard_map/row_y/ppermute | solution.py:319
  114.7 11.0 %copy-start.14 = (f32[24,128]{1,0:T(8,128)}, f32[24,128]{1,0:T(8,128)S(1)}, u32[]{:S(2)}) copy-start(f32[24,128]{1,0:T(8,128)S(1)} %add_add_fusion.row_a) | copy-start | bytes 36868
  114.7 6.5 %collective-permute-start.18 = (f32[24,128]{1,0:T(8,128)S(1)}, f32[24,128]{1,0:T(8,128)S(1)}, u32[]{:S(2)}, u32[]{:S(2)}) collective-permute-start(f32[24,128]{1,0:T(8,128)S(1)} %add_add_fusion.row_a), channel_id=1, source_target_pairs={{0,4},{4,0},{1,5},{5,1},{2,6},{6,2},{3,7},{7,3},{8,12},{12,8},{9,1... | collective-permute-start | bytes 36872 | tf_op jit(solution)/shard_map/row_z/ppermute | solution.py:319
  116.6 8.0 %collective-permute-start.22 = (bf16[4,96,768]{2,1,0:T(8,128)(2,1)S(1)}, bf16[4,96,768]{2,1,0:T(8,128)(2,1)S(1)}, u32[]{:S(2)}, u32[]{:S(2)}) collective-permute-start(bf16[4,96,768]{2,1,0:T(8,128)(2,1)S(1)} %pad_maximum_fusion.refs_0_), channel_id=1, source_target_pairs={{0,8},{8,0},{1,9},{9,1},{2,10},{10,2},{3,11},{11,3},{4,12},{12,4},... | collective-permute-start | bytes 1769480 | tf_op jit(solution)/shard_map/new_core/ppermute | solution.py:319
  120.6 4.1 %collective-permute-start.24 = (bf16[4,96,768]{2,1,0:T(8,128)(2,1)S(1)}, bf16[4,96,768]{2,1,0:T(8,128)(2,1)}, u32[]{:S(2)}, u32[]{:S(2)}) collective-permute-start(bf16[4,96,768]{2,1,0:T(8,128)(2,1)S(1)} %collective-permute-done.23.refs_2_), channel_id=1, source_target_pairs={{0,8},{8,0},{1,9},{9,1},{2,10},{10,2},{3,11},{11,3},{4,12},{12,4},... | collective-permute-start | bytes 1769480 | tf_op jit(solution)/shard_map/new_core/ppermute | solution.py:319
  120.6 4.1 %collective-permute-start.26 = (bf16[4,96,768]{2,1,0:T(8,128)(2,1)S(1)}, bf16[4,96,768]{2,1,0:T(8,128)(2,1)}, u32[]{:S(2)}, u32[]{:S(2)}) collective-permute-start(bf16[4,96,768]{2,1,0:T(8,128)(2,1)S(1)} %collective-permute-done.25.refs_4_), channel_id=1, source_target_pairs={{0,8},{8,0},{1,9},{9,1},{2,10},{10,2},{3,11},{11,3},{4,12},{12,4},... | collective-permute-start | bytes 1769480 | tf_op jit(solution)/shard_map/new_core/ppermute | solution.py:319
  121.2 4.5 %copy-start.15 = (f32[24,128]{1,0:T(8,128)}, f32[24,128]{1,0:T(8,128)S(1)}, u32[]{:S(2)}) copy-start(f32[24,128]{1,0:T(8,128)S(1)} %collective-permute-done.18.row_b) | copy-start | bytes 36868
  121.2 4.5 %copy-start.9 = (bf16[4,96,768]{2,1,0:T(8,128)(2,1)}, bf16[4,96,768]{2,1,0:T(8,128)(2,1)S(1)}, u32[]{:S(2)}) copy-start(bf16[4,96,768]{2,1,0:T(8,128)(2,1)S(1)} %collective-permute-done.27.refs_6_) | copy-start | bytes 1769476
  121.2 4.5 %collective-permute-start.28 = (bf16[4,96,768]{2,1,0:T(8,128)(2,1)S(1)}, bf16[4,96,768]{2,1,0:T(8,128)(2,1)}, u32[]{:S(2)}, u32[]{:S(2)}) collective-permute-start(bf16[4,96,768]{2,1,0:T(8,128)(2,1)S(1)} %collective-permute-done.27.refs_6_), channel_id=1, source_target_pairs={{0,8},{8,0},{1,9},{9,1},{2,10},{10,2},{3,11},{11,3},{4,12},{12,4},... | collective-permute-start | bytes 1769480 | tf_op jit(solution)/shard_map/new_core/ppermute | solution.py:319
  124.7 1.1 copy-start.10
